TPU v7x, 256 devices: a whole 4x4x8 slice. The times are simulated.
256 devices in a mesh: dp: 8 (over z_hi, y), mp: 32 (over x, z_lo, core).
Axes of the slice: x: 4, y: 4, z: 8 (z_hi: 2, z_lo: 4; z = z_hi * 4 + z_lo), core: 2. Of those that a mesh axis runs over, the one named last changes fastest.
Arguments:
- tokens: bfloat16 [8192, 2560], P('dp'), may hold values from -6 to 6
- cotangent: bfloat16 [8192, 10240], P('dp', 'mp'), may hold values from -0.0625 to 0.0625
- saved_panels: bfloat16 [2048, 8192], P(None, 'mp'), may hold values from -0.125 to 0.125
- owners: int32 [32, 2], replicated, may hold values from 0 to 7, as said below
- row_growth: bfloat16 [2560, 2048], P(None, 'dp'), may hold values from -0.125 to 0.125
- col_growth: bfloat16 [10240, 8192], P('mp', 'dp'), may hold values from -0.0625 to 0.0625
Outputs:
- grown_out: bfloat16 [8192, 10240], P('dp', 'mp')
- grad_grown: float32 [2560, 10240], P('dp', 'mp')
- grad_row_growth: float32 [2560, 2048], P('mp', 'dp')
- grad_col_growth: float32 [10240, 8192], P('mp', 'dp')
Inputs may be any that keep to these rules, and one draw needn't show every extreme that they name: `owners`: column 0 is a rank below 8, column 1 a section below 4; every pair of rank and section names exactly one panel.
All inputs are finite; a program needn't handle non-finite values.
Results may differ from a plain program's by a relative error of at most 0.006.
Values may be sent and summed in bfloat16 or wider, within the bound.
No kernel may reach another device: no remote copies, remote signals or barrier semaphores. Data moves between devices by JAX's collectives and lax.ppermute only.
A program may use at most 128 MiB of HBM per device.

v0:
```python
import jax
import jax.numpy as jnp
from jax import lax
from jax.experimental import pallas as pl
from jax.experimental.pallas import tpu as pltpu
from jax.sharding import PartitionSpec as P

SECTIONS = 4
ZH, NY = 2, 4
NX, NZ, NC = 4, 4, 2
MP = NX * NZ * NC
PLANE_GROUPS = [[(x * NZ + z) * NC + c for x in range(NX) for z in range(NZ)] for c in range(NC)]
SWAP_ZH = [(i, (i + NY) % (ZH * NY)) for i in range(ZH * NY)]
SWAP_CORE = [(m, m ^ 1) for m in range(MP)]
BF, F32 = jnp.bfloat16, jnp.float32
NN, NT, TN = ((1,), (0,)), ((1,), (1,)), ((0,), (0,))


def shift_y(k):
    return [(h * NY + y, h * NY + (y + k) % NY) for h in range(ZH) for y in range(NY)]


def shift_x(k):
    return [
        ((x * NZ + z) * NC + c, ((x + k) % NX * NZ + z) * NC + c)
        for x in range(NX) for z in range(NZ) for c in range(NC)
    ]


def flip_z(k):
    return [
        ((x * NZ + z) * NC + c, (x * NZ + (z ^ k)) * NC + c)
        for x in range(NX) for z in range(NZ) for c in range(NC)
    ]


def dot(a, b, dims):
    return lax.dot_general(a, b, (dims, ((), ())), preferred_element_type=F32)


def pick(blocks, index, axis=0):
    return lax.dynamic_index_in_dim(blocks, index, axis, keepdims=False)


def choose(index, cases):
    out = cases[-1]
    for at in range(len(cases) - 1):
        out = jnp.where(index == at, cases[at], out)
    return out


def call(body, place, arrays, outs, flops, scratch=(), grid=None, in_specs=None, out_specs=None):
    size = lambda s: s.size * s.dtype.itemsize
    whole = pl.BlockSpec(memory_space=pltpu.VMEM)
    return pl.pallas_call(
        body,
        out_shape=outs,
        grid=grid or (),
        in_specs=[pl.BlockSpec(memory_space=pltpu.SMEM)] + (in_specs or [whole] * len(arrays)),
        out_specs=out_specs or jax.tree.map(lambda _: whole, outs),
        scratch_shapes=list(scratch),
        compiler_params=pltpu.CompilerParams(vmem_limit_bytes=40 * 2**20),
        cost_estimate=pl.CostEstimate(
            flops=flops,
            bytes_accessed=sum(map(size, arrays)) + sum(map(size, jax.tree.leaves(outs))),
            transcendentals=0,
        ),
    )(place, *arrays)


def struct(shape, kind):
    return jax.ShapeDtypeStruct(shape, kind)


def put(value, k, at, outs):
    for case, out in enumerate(outs):
        @pl.when(k == case)
        def _():
            out[at] = value.astype(out.dtype)


def grad_body(place, tokens, cot, *outs):
    step = pl.program_id(0)
    both = dot(cot[...], tokens[...], NN)
    n = both.shape[1] // 2
    for half in range(2):
        block = 2 * step + half
        put(
            both[:, half * n:(half + 1) * n],
            lax.rem(lax.rem(block, NY) - place[0] + NY, NY),
            block // NY,
            outs,
        )


def grad_terms(place, tokens, cot):
    n = tokens.shape[1] // (ZH * NY)
    hidden = cot.shape[0]
    shape = (ZH, hidden, n)
    outs = [struct(shape, F32)] + [struct(shape, BF)] * (NY - 1)
    full = pl.BlockSpec(shape, lambda s: (0, 0, 0))
    return call(
        grad_body, place, (tokens, cot), outs, 2 * tokens.size * hidden,
        grid=(ZH * NY // 2,),
        in_specs=[
            pl.BlockSpec((tokens.shape[0], 2 * n), lambda s: (0, s)),
            pl.BlockSpec(cot.shape, lambda s: (0, 0)),
        ],
        out_specs=[full] * NY,
    )


def back_body(place, grown, *refs):
    grads, out = refs[:NY], refs[NY]
    n = grads[0].shape[2]
    total = jnp.zeros(out.shape, F32)
    for k in range(NY):
        for h in range(ZH):
            first = (h * NY + lax.rem(place[0] - k + NY, NY)) * n
            total += dot(grads[k][h], grown[pl.ds(pl.multiple_of(first, n), n), :], NN)
    out[...] = total.astype(out.dtype)


def back_block(place, row_growth, grads):
    hidden, old = grads[0].shape[1], row_growth.shape[1]
    return call(
        back_body, place, (row_growth, *grads), struct((hidden, old), BF),
        2 * row_growth.size * hidden,
    )


def inner_body(place, col, *refs):
    source, outs = refs[:2 * NX], refs[2 * NX:]
    for k in range(NX):
        for c in range(NC):
            block = dot(col[...], source[2 * k + c][...], NT)
            where = lax.rem(place[2] - k - place[0] + 2 * NX, NX)
            put(block, where, place[3] ^ c, outs)


def inner_terms(place, col, source):
    hidden, rows = col.shape[0], source[0].shape[0]
    shape = (ZH, hidden, rows)
    outs = [struct(shape, F32)] + [struct(shape, BF)] * (NY - 1)
    return call(inner_body, place, (col, *source), outs, 2 * col.size * rows * len(source))


def col_body(place, *refs):
    source, back, out, held = refs[:2 * NX], refs[2 * NX:2 * NX + NY], refs[-2], refs[-1]
    for k in range(NY):
        held[k] = back[k][...]
    total = jnp.zeros(out.shape, F32)
    for k in range(NX):
        for c in range(NC):
            at = lax.rem(place[0] - place[2] + k + NY, NY)
            total += dot(held[at, place[3] ^ c], source[2 * k + c][...], NN)
    out[...] = total


def col_grad(place, source, back):
    hidden, rows = back[0].shape[1:]
    return call(
        col_body, place, (*source, *back), struct((hidden, source[0].shape[1]), F32),
        2 * hidden * sum(s.size for s in source),
        scratch=[pltpu.VMEM((NY, *back[0].shape), BF)],
    )


def row_body(place, inner, *refs):
    grads, keep, give = refs[:NY], refs[NY], refs[NY + 1]
    rows = keep.shape[1]
    for k in range(NY):
        for h in range(ZH):
            block = dot(grads[k][h], inner[...], TN)
            at = (h * NY + lax.rem(place[0] - k + NY, NY)) * 2
            for q in range(2):
                one = block[2 * q * rows:(2 * q + 1) * rows]
                two = block[(2 * q + 1) * rows:(2 * q + 2) * rows]
                first = place[3] == 0
                keep[at + q] = jnp.where(first, one, two)
                give[at + q] = jnp.where(first, two, one).astype(BF)


def row_terms(place, inner, grads):
    old, n = inner.shape[1], grads[0].shape[2]
    shape = (NX * NZ, n * ZH * NY // MP, old)
    return call(
        row_body, place, (inner, *grads), [struct(shape, F32), struct(shape, BF)],
        2 * inner.size * n * ZH * NY,
    )


def out_body(place, mixed, *refs):
    inner, out = refs[:NY], refs[NY]
    total = jnp.zeros(out.shape, F32)
    for k in range(NY):
        for h in range(ZH):
            rows = mixed[:, h, k]
            total += dot(inner[k][h], rows.reshape(-1, rows.shape[-1]), NN)
    out[...] = total.astype(out.dtype)


def grown_output(place, mixed, inner):
    hidden = inner[0].shape[1]
    return call(
        out_body, place, (mixed, *inner), struct((hidden, mixed.shape[-1]), BF),
        2 * mixed.size * hidden,
    )


def exchange_y(block_for):
    got = {k: lax.ppermute(block_for(k), "dp", shift_y(k)) for k in (2, 1, 3)}
    return [None, got[1], got[2], got[3]]


def sum_dp(blocks):
    got = exchange_y(lambda k: blocks[k])
    part = blocks[0] + got[1].astype(F32) + got[2].astype(F32) + got[3].astype(F32)
    return part + lax.ppermute(part.astype(BF), "dp", SWAP_ZH).astype(F32)


def gather_y(block):
    return [block] + exchange_y(lambda k: block)[1:]


def source_blocks(saved, slot_of, z_hi, y):
    width = saved.shape[1]
    sub = saved.shape[0] // (MP * NY)
    rows = saved.reshape(NC, NX, NZ, NY, sub, width)
    mine = pick(rows, y, 3).transpose(1, 2, 0, 3, 4).reshape(MP, sub, width)
    slots = lax.all_to_all(mine, "mp", 0, 0)
    panels = jnp.take(slots, slot_of, axis=0).reshape(ZH, NY, -1, sub, width)
    panels = pick(panels, z_hi)
    got = exchange_y(lambda k: pick(panels, (y + k) % NY))
    got[0] = pick(panels, y)
    chunk = jnp.stack([choose((y - j) % NY, got) for j in range(NY)])
    chunk = chunk.transpose(0, 2, 1, 3).reshape(NY * sub, -1)
    z = lax.axis_index("mp") // NC % NZ
    got = [chunk] + [lax.ppermute(chunk, "mp", flip_z(k)) for k in (1, 2, 3)]
    strip = jnp.concatenate([choose(z ^ j, got) for j in range(NZ)])
    got = {k: lax.ppermute(strip, "mp", shift_x(k)) for k in (2, 1, 3)}
    got[0] = strip
    blocks = []
    for k in range(NX):
        blocks += [got[k], lax.ppermute(got[k], "mp", SWAP_CORE)]
    return blocks


def mixed_strips(tokens, row_growth, z_hi, mp_index):
    old = row_growth.shape[1]
    strip = old // (NX * NZ)
    mine = pick(row_growth.T.reshape(NX * NZ, strip, -1), mp_index // NC)
    other = lax.ppermute(mine, "dp", SWAP_ZH)
    mine = jnp.where(z_hi == mp_index % NC, mine, other)
    strips = jnp.concatenate(gather_y(mine))
    mixed = dot(strips, tokens, NT).astype(BF)
    mixed = lax.all_gather(mixed, "mp", axis=0, tiled=True)
    return mixed.reshape(NX * NZ, NC, NY, strip, -1)


def shards(tokens, cotangent, saved_panels, owners, row_growth, col_growth):
    dp_index, mp_index = lax.axis_index("dp"), lax.axis_index("mp")
    z_hi, y = dp_index // NY, dp_index % NY
    x, core = mp_index // (NZ * NC), mp_index % NC
    place = jnp.stack([y, z_hi, x, core]).astype(jnp.int32)
    slot_of = owners[:, 1] * (MP // SECTIONS) + owners[:, 0]

    source = source_blocks(saved_panels, slot_of, z_hi, y)
    mixed = mixed_strips(tokens, row_growth, z_hi, mp_index)

    grads = sum_dp(grad_terms(place, tokens, cotangent.T))
    grad = pick(grads, z_hi).T
    grads = gather_y(grads.astype(BF))
    back = back_block(place, row_growth, grads)
    other = lax.ppermute(back, "dp", SWAP_ZH)
    pair = jnp.where(z_hi == 0, jnp.stack([back, other]), jnp.stack([other, back]))
    grad_col = col_grad(place, source, gather_y(pair))

    inners = sum_dp(inner_terms(place, col_growth, source)).astype(BF)
    keep, give = row_terms(place, pick(inners, z_hi), grads)
    keep = keep + lax.ppermute(give, "mp", SWAP_CORE).astype(F32)
    keep = lax.all_to_all(keep.astype(BF), "mp", 0, 0, axis_index_groups=PLANE_GROUPS)
    grad_row = keep.astype(F32).sum(axis=0)
    grown_out = grown_output(place, mixed, gather_y(inners)).T
    return (grown_out, grad, grad_row, grad_col)


def solution(mesh):
    in_specs = (P("dp", None), P("dp", "mp"), P(None, "mp"), P(), P(None, "dp"), P("mp", "dp"))
    out_specs = (P("dp", "mp"), P("dp", "mp"), P("mp", "dp"), P("mp", "dp"))
    return jax.shard_map(shards, mesh=mesh, in_specs=in_specs, out_specs=out_specs, check_vma=False)
```

profile of v0, /device:TPU:30, one launch (start us, length us, event | category | flops | bytes accessed | tf_op | source)
XLA Modules:
  0.0 282.3 jit_solution(9431521433032318225)
XLA Ops:
  9.0 7.3 %collective-permute-start = (bf16[16,2560]{1,0:T(8,128)(2,1)S(1)}, bf16[16,2560]{1,0:T(8,128)(2,1)S(1)}, u32[]{:S(2)}, u32[]{:S(2)}) collective-permute-start(bf16[16,2560]{1,0:T(8,128)(2,1)S(1)} %dynamic-slice_bitcast_fusion.2), channel_id=1, source_target_pairs={{0,128},{32,160},{64,192},{96,224},{128,0},{160,32},{192,64},{224,... | collective-permute-start | bytes 245768 | tf_op jit(solution)/shard_map/ppermute | solution.py:253
  16.2 3.0 %collective-permute-done = bf16[16,2560]{1,0:T(8,128)(2,1)S(1)} collective-permute-done((bf16[16,2560]{1,0:T(8,128)(2,1)S(1)}, bf16[16,2560]{1,0:T(8,128)(2,1)S(1)}, u32[]{:S(2)}, u32[]{:S(2)}) %collective-permute-start) | collective-permute-done | bytes 81952 | tf_op jit(solution)/shard_map/ppermute | solution.py:253
  27.8 4.8 %convolution_convert_fusion = bf16[64,1024]{1,0:T(8,128)(2,1)} fusion(bf16[1024,2560]{1,0:T(8,128)(2,1)} %tokens.1, bf16[16,2560]{1,0:T(8,128)(2,1)S(1)} %collective-permute-done.3, bf16[16,2560]{1,0:T(8,128)(2,1)S(1)} %collective-permute-done.2, bf16[16,2560]{1,0:T(8,128)(2,1)S(1)} %collective-permute-done.1, bf16[16,2560]{1,0:T(8,128)(2,1)S(1)} %broadcast_select_fusion.1), kind=kOutput, calls=%fused_computation.3 | convolution fusion | flops 336920576 | bytes 5701632 | tf_op jit(solution)/shard_map/dot_general | solution.py:38
  33.5 7.4 %all-to-all-start = ((bf16[32,16,256]{2,1,0:T(8,128)(2,1)}), bf16[32,16,256]{2,1,0:T(8,128)(2,1)S(1)}, u32[]{:S(2)}, u32[]{:S(2)}) async-start(bf16[32,16,256]{2,1,0:T(8,128)(2,1)} %bitcast.11), calls=%async_computation | async-start | bytes 524288 | tf_op jit(solution)/shard_map/all_to_all | solution.py:231
  41.1 8.7 %all-to-all-done = bf16[32,16,256]{2,1,0:T(8,128)(2,1)S(1)} async-done(((bf16[32,16,256]{2,1,0:T(8,128)(2,1)}), bf16[32,16,256]{2,1,0:T(8,128)(2,1)S(1)}, u32[]{:S(2)}, u32[]{:S(2)}) %all-to-all-start) | async-done | bytes 262176 | tf_op jit(solution)/shard_map/all_to_all | solution.py:231
  53.3 2.7 collective-permute-done.4
  62.8 4.4 %collective-permute-done.7 = bf16[64,1024]{1,0:T(8,128)(2,1)S(1)} collective-permute-done((bf16[64,1024]{1,0:T(8,128)(2,1)S(1)}, bf16[64,1024]{1,0:T(8,128)(2,1)S(1)}, u32[]{:S(2)}, u32[]{:S(2)}) %collective-permute-start.7) | collective-permute-done | bytes 131104 | tf_op jit(solution)/shard_map/ppermute | solution.py:239
  69.5 4.9 %collective-permute-done.9 = bf16[64,1024]{1,0:T(8,128)(2,1)S(1)} collective-permute-done((bf16[64,1024]{1,0:T(8,128)(2,1)S(1)}, bf16[64,1024]{1,0:T(8,128)(2,1)S(1)}, u32[]{:S(2)}, u32[]{:S(2)}) %collective-permute-start.9) | collective-permute-done | bytes 131104 | tf_op jit(solution)/shard_map/ppermute | solution.py:239
  76.9 17.0 %collective-permute-done.11.refs_2_ = bf16[256,1024]{1,0:T(8,128)(2,1)S(1)} collective-permute-done((bf16[256,1024]{1,0:T(8,128)(2,1)S(1)}, bf16[256,1024]{1,0:T(8,128)(2,1)S(1)}, u32[]{:S(2)}, u32[]{:S(2)}) %collective-permute-start.11) | collective-permute-done | bytes 524320 | tf_op jit(solution)/shard_map/ppermute | solution.py:241
  95.8 9.4 %collective-permute-done.15.refs_6_ = bf16[256,1024]{1,0:T(8,128)(2,1)S(1)} collective-permute-done((bf16[256,1024]{1,0:T(8,128)(2,1)S(1)}, bf16[256,1024]{1,0:T(8,128)(2,1)S(1)}, u32[]{:S(2)}, u32[]{:S(2)}) %collective-permute-start.15) | collective-permute-done | bytes 524320 | tf_op jit(solution)/shard_map/ppermute | solution.py:241
  109.0 4.6 %shard_map.95 = (f32[2,320,320]{2,1,0:T(8,128)S(1)}, bf16[2,320,320]{2,1,0:T(8,128)(2,1)S(1)}, bf16[2,320,320]{2,1,0:T(8,128)(2,1)S(1)}, bf16[2,320,320]{2,1,0:T(8,128)(2,1)S(1)}) custom-call(s32[4]{0:T(128)S(1)} %pad_add_fusion.place, bf16[1024,2560]{1,0:T(8,128)(2,1)S(1)} %copy-done.1, bf16[320,1024]{1,0:T(8,128)(2,1)S(1)} %bitcast.82), custom_call_target="tpu_custom_call" | custom-call | flops 1677721600 | bytes 7946240 | tf_op jit(solution)/shard_map/pallas_call | solution.py:55
  116.8 5.8 %shard_map.93 = (f32[2,320,256]{2,1,0:T(8,128)S(1)}, bf16[2,320,256]{2,1,0:T(8,128)(2,1)S(1)}, bf16[2,320,256]{2,1,0:T(8,128)(2,1)S(1)}, bf16[2,320,256]{2,1,0:T(8,128)(2,1)S(1)}) custom-call(s32[4]{0:T(128)S(1)} %pad_add_fusion.place, bf16[320,1024]{1,0:T(8,128)(2,1)S(1)} %copy-done.25, bf16[256,1024]{1,0:T(8,128)(2,1)S(1)} %pad_maximum_fusion.refs_0_, ...), custom_call_target="tpu_custom_call" | custom-call | flops 1342177280 | bytes 6488064 | tf_op jit(solution)/shard_map/pallas_call | solution.py:55
  130.1 10.6 %collective-permute-done.26 = bf16[2,320,320]{2,1,0:T(8,128)(2,1)S(1)} collective-permute-done((bf16[2,320,320]{2,1,0:T(8,128)(2,1)S(1)}, bf16[2,320,320]{2,1,0:T(8,128)(2,1)S(1)}, u32[]{:S(2)}, u32[]{:S(2)}) %collective-permute-start.26) | collective-permute-done | bytes 409632 | tf_op jit(solution)/shard_map/ppermute | solution.py:212
  140.9 5.5 %collective-permute-start.27 = (bf16[2,320,320]{2,1,0:T(8,128)(2,1)S(1)}, bf16[2,320,320]{2,1,0:T(8,128)(2,1)S(1)}, u32[]{:S(2)}, u32[]{:S(2)}) collective-permute-start(bf16[2,320,320]{2,1,0:T(8,128)(2,1)S(1)} %fusion.7), channel_id=1, source_target_pairs={{0,128},{32,160},{64,192},{96,224},{128,0},{160,32},{192,64},{224,... | collective-permute-start | bytes 1228808 | tf_op jit(solution)/shard_map/ppermute | solution.py:219
  147.7 6.1 %collective-permute-done.19 = bf16[2,320,256]{2,1,0:T(8,128)(2,1)S(1)} collective-permute-done((bf16[2,320,256]{2,1,0:T(8,128)(2,1)S(1)}, bf16[2,320,256]{2,1,0:T(8,128)(2,1)S(1)}, u32[]{:S(2)}, u32[]{:S(2)}) %collective-permute-start.19) | collective-permute-done | bytes 327712 | tf_op jit(solution)/shard_map/ppermute | solution.py:212
  153.9 5.5 %collective-permute-start.20 = (bf16[2,320,256]{2,1,0:T(8,128)(2,1)S(1)}, bf16[2,320,256]{2,1,0:T(8,128)(2,1)S(1)}, u32[]{:S(2)}, u32[]{:S(2)}) collective-permute-start(bf16[2,320,256]{2,1,0:T(8,128)(2,1)S(1)} %fusion.8), channel_id=1, source_target_pairs={{0,128},{32,160},{64,192},{96,224},{128,0},{160,32},{192,64},{224,... | collective-permute-start | bytes 983048 | tf_op jit(solution)/shard_map/ppermute | solution.py:219
  162.7 10.9 %collective-permute-done.20 = bf16[2,320,256]{2,1,0:T(8,128)(2,1)S(1)} collective-permute-done((bf16[2,320,256]{2,1,0:T(8,128)(2,1)S(1)}, bf16[2,320,256]{2,1,0:T(8,128)(2,1)S(1)}, u32[]{:S(2)}, u32[]{:S(2)}) %collective-permute-start.20) | collective-permute-done | bytes 327712 | tf_op jit(solution)/shard_map/ppermute | solution.py:219
  177.0 8.4 %collective-permute-done.30.refs_3_ = bf16[2,320,320]{2,1,0:T(8,128)(2,1)S(1)} collective-permute-done((bf16[2,320,320]{2,1,0:T(8,128)(2,1)S(1)}, bf16[2,320,320]{2,1,0:T(8,128)(2,1)S(1)}, u32[]{:S(2)}, u32[]{:S(2)}) %collective-permute-start.30) | collective-permute-done | bytes 409632 | tf_op jit(solution)/shard_map/ppermute | solution.py:212
  190.1 25.2 %all-to-all-start.1 = ((bf16[16,80,256]{2,1,0:T(8,128)(2,1)}), bf16[16,80,256]{2,1,0:T(8,128)(2,1)}, u32[]{:S(2)}, u32[]{:S(2)}) async-start(bf16[16,80,256]{2,1,0:T(8,128)(2,1)} %add_convert_fusion), calls=%async_computation.1 | async-start | bytes 1310720 | tf_op jit(solution)/shard_map/all_to_all | solution.py:282
  219.8 5.4 %collective-permute-start.32 = (bf16[320,256]{1,0:T(8,128)(2,1)S(1)}, bf16[320,256]{1,0:T(8,128)(2,1)S(1)}, u32[]{:S(2)}, u32[]{:S(2)}) collective-permute-start(bf16[320,256]{1,0:T(8,128)(2,1)S(1)} %shard_map.97), channel_id=1, source_target_pairs={{0,128},{32,160},{64,192},{96,224},{128,0},{160,32},{192,64},{224,... | collective-permute-start | bytes 491528 | tf_op jit(solution)/shard_map/ppermute | solution.py:275
  225.2 13.6 %collective-permute-done.32 = bf16[320,256]{1,0:T(8,128)(2,1)S(1)} collective-permute-done((bf16[320,256]{1,0:T(8,128)(2,1)S(1)}, bf16[320,256]{1,0:T(8,128)(2,1)S(1)}, u32[]{:S(2)}, u32[]{:S(2)}) %collective-permute-start.32) | collective-permute-done | bytes 163872 | tf_op jit(solution)/shard_map/ppermute | solution.py:275
  245.7 7.0 %collective-permute-done.33.refs_9_ = bf16[2,320,256]{2,1,0:T(8,128)(2,1)S(1)} collective-permute-done((bf16[2,320,256]{2,1,0:T(8,128)(2,1)S(1)}, bf16[2,320,256]{2,1,0:T(8,128)(2,1)S(1)}, u32[]{:S(2)}, u32[]{:S(2)}) %collective-permute-start.33) | collective-permute-done | bytes 327712 | tf_op jit(solution)/shard_map/ppermute | solution.py:212
  263.9 4.0 %shard_map.98 = f32[320,1024]{1,0:T(8,128)} custom-call(s32[4]{0:T(128)S(1)} %pad_add_fusion.place, bf16[256,1024]{1,0:T(8,128)(2,1)S(1)} %pad_maximum_fusion.refs_0_, bf16[256,1024]{1,0:T(8,128)(2,1)} %collective-permute-done.10.refs_1_, bf16[256,1024]{1,0:T(8,128)(2,1)S(1)} %copy-done.13, bf16[256,1024]{1,0:T(8,128)(2,1)} %collective-permute-done.12.refs_3_, ...), custom_call_target="tpu_custom_call" | custom-call | flops 1342177280 | bytes 6815744 | tf_op jit(solution)/shard_map/pallas_call | solution.py:55
  272.0 3.5 %shard_map.94 = bf16[320,1024]{1,0:T(8,128)(2,1)} custom-call(s32[4]{0:T(128)S(1)} %pad_add_fusion.place, bf16[16,2,4,16,1024]{4,3,2,1,0:T(8,128)(2,1)S(1)} %bitcast.80, bf16[2,320,256]{2,1,0:T(8,128)(2,1)S(1)} %copy-done.5, bf16[2,320,256]{2,1,0:T(8,128)(2,1)} %collective-permute-done.21.refs_1_, bf16[2,320,256]{2,1,0:T(8,128)(2,1)} %collective-permute-done.22.refs_2_, ...), custom_call_target="tpu_custom_call" | custom-call | flops 1342177280 | bytes 6160384 | tf_op jit(solution)/shard_map/pallas_call | solution.py:55
  (144 shorter events, 82.1 us)
Async XLA Ops:
  7.2 262.6 %all-gather.2.cloned.1.call-start = ((), (), s32[]{:S(2)}) async-start(), calls=%async_computation.2 | async-start | bytes 4325376 | tf_op jit(solution)/shard_map/all_gather | solution.py:257
  33.5 16.3 %all-to-all-start = ((bf16[32,16,256]{2,1,0:T(8,128)(2,1)}), bf16[32,16,256]{2,1,0:T(8,128)(2,1)S(1)}, u32[]{:S(2)}, u32[]{:S(2)}) async-start(bf16[32,16,256]{2,1,0:T(8,128)(2,1)} %bitcast.11), calls=%async_computation | async-start | bytes 524288 | tf_op jit(solution)/shard_map/all_to_all | solution.py:231
  74.5 19.4 %collective-permute-start.11 = (bf16[256,1024]{1,0:T(8,128)(2,1)S(1)}, bf16[256,1024]{1,0:T(8,128)(2,1)S(1)}, u32[]{:S(2)}, u32[]{:S(2)}) collective-permute-start(bf16[256,1024]{1,0:T(8,128)(2,1)S(1)} %pad_maximum_fusion.refs_0_), channel_id=1, source_target_pairs={{0,8},{1,9},{2,10},{3,11},{4,12},{5,13},{6,14},{7,15},{8,16},{9,17... | collective-permute-start | bytes 1572872 | tf_op jit(solution)/shard_map/ppermute | solution.py:241
  75.9 19.9 %collective-permute-start.13 = (bf16[256,1024]{1,0:T(8,128)(2,1)S(1)}, bf16[256,1024]{1,0:T(8,128)(2,1)S(1)}, u32[]{:S(2)}, u32[]{:S(2)}) collective-permute-start(bf16[256,1024]{1,0:T(8,128)(2,1)S(1)} %pad_maximum_fusion.refs_0_), channel_id=1, source_target_pairs={{0,16},{1,17},{2,18},{3,19},{4,20},{5,21},{6,22},{7,23},{8,24},{9,... | collective-permute-start | bytes 1572872 | tf_op jit(solution)/shard_map/ppermute | solution.py:241
  75.9 29.3 %collective-permute-start.15 = (bf16[256,1024]{1,0:T(8,128)(2,1)S(1)}, bf16[256,1024]{1,0:T(8,128)(2,1)S(1)}, u32[]{:S(2)}, u32[]{:S(2)}) collective-permute-start(bf16[256,1024]{1,0:T(8,128)(2,1)S(1)} %pad_maximum_fusion.refs_0_), channel_id=1, source_target_pairs={{0,24},{1,25},{2,26},{3,27},{4,28},{5,29},{6,30},{7,31},{8,0},{9,1... | collective-permute-start | bytes 1572872 | tf_op jit(solution)/shard_map/ppermute | solution.py:241
  76.9 37.6 %collective-permute-start.10 = (bf16[256,1024]{1,0:T(8,128)(2,1)S(1)}, bf16[256,1024]{1,0:T(8,128)(2,1)}, u32[]{:S(2)}, u32[]{:S(2)}) collective-permute-start(bf16[256,1024]{1,0:T(8,128)(2,1)S(1)} %pad_maximum_fusion.refs_0_), channel_id=1, source_target_pairs={{0,1},{1,0},{2,3},{3,2},{4,5},{5,4},{6,7},{7,6},{8,9},{9,8},{10,11... | collective-permute-start | bytes 1572872 | tf_op jit(solution)/shard_map/ppermute | solution.py:245
  93.9 21.7 %collective-permute-start.12 = (bf16[256,1024]{1,0:T(8,128)(2,1)S(1)}, bf16[256,1024]{1,0:T(8,128)(2,1)}, u32[]{:S(2)}, u32[]{:S(2)}) collective-permute-start(bf16[256,1024]{1,0:T(8,128)(2,1)S(1)} %collective-permute-done.11.refs_2_), channel_id=1, source_target_pairs={{0,1},{1,0},{2,3},{3,2},{4,5},{5,4},{6,7},{7,6},{8,9},{9,8},{10,11... | collective-permute-start | bytes 1572872 | tf_op jit(solution)/shard_map/ppermute | solution.py:245
  95.8 20.9 %collective-permute-start.14 = (bf16[256,1024]{1,0:T(8,128)(2,1)S(1)}, bf16[256,1024]{1,0:T(8,128)(2,1)S(1)}, u32[]{:S(2)}, u32[]{:S(2)}) collective-permute-start(bf16[256,1024]{1,0:T(8,128)(2,1)S(1)} %collective-permute-done.13.refs_4_), channel_id=1, source_target_pairs={{0,1},{1,0},{2,3},{3,2},{4,5},{5,4},{6,7},{7,6},{8,9},{9,8},{10,11... | collective-permute-start | bytes 1572872 | tf_op jit(solution)/shard_map/ppermute | solution.py:245
  114.5 15.6 %collective-permute-start.25 = (bf16[2,320,320]{2,1,0:T(8,128)(2,1)S(1)}, bf16[2,320,320]{2,1,0:T(8,128)(2,1)S(1)}, u32[]{:S(2)}, u32[]{:S(2)}) collective-permute-start(bf16[2,320,320]{2,1,0:T(8,128)(2,1)S(1)} %get-tuple-element.20), channel_id=1, source_target_pairs={{0,64},{32,96},{64,0},{96,32},{128,192},{160,224},{192,128},{224,1... | collective-permute-start | bytes 1228808 | tf_op jit(solution)/shard_map/ppermute | solution.py:212
  115.6 25.1 %collective-permute-start.26 = (bf16[2,320,320]{2,1,0:T(8,128)(2,1)S(1)}, bf16[2,320,320]{2,1,0:T(8,128)(2,1)S(1)}, u32[]{:S(2)}, u32[]{:S(2)}) collective-permute-start(bf16[2,320,320]{2,1,0:T(8,128)(2,1)S(1)} %get-tuple-element.21), channel_id=1, source_target_pairs={{0,96},{32,0},{64,32},{96,64},{128,224},{160,128},{192,160},{224,1... | collective-permute-start | bytes 1228808 | tf_op jit(solution)/shard_map/ppermute | solution.py:212
  122.6 23.9 %collective-permute-start.17 = (bf16[2,320,256]{2,1,0:T(8,128)(2,1)S(1)}, bf16[2,320,256]{2,1,0:T(8,128)(2,1)S(1)}, u32[]{:S(2)}, u32[]{:S(2)}) collective-permute-start(bf16[2,320,256]{2,1,0:T(8,128)(2,1)S(1)} %get-tuple-element.15), channel_id=1, source_target_pairs={{0,32},{32,64},{64,96},{96,0},{128,160},{160,192},{192,224},{224,1... | collective-permute-start | bytes 983048 | tf_op jit(solution)/shard_map/ppermute | solution.py:212
  124.8 22.9 %collective-permute-start.18 = (bf16[2,320,256]{2,1,0:T(8,128)(2,1)S(1)}, bf16[2,320,256]{2,1,0:T(8,128)(2,1)S(1)}, u32[]{:S(2)}, u32[]{:S(2)}) collective-permute-start(bf16[2,320,256]{2,1,0:T(8,128)(2,1)S(1)} %get-tuple-element.16), channel_id=1, source_target_pairs={{0,64},{32,96},{64,0},{96,32},{128,192},{160,224},{192,128},{224,1... | collective-permute-start | bytes 983048 | tf_op jit(solution)/shard_map/ppermute | solution.py:212
  127.7 26.0 %collective-permute-start.19 = (bf16[2,320,256]{2,1,0:T(8,128)(2,1)S(1)}, bf16[2,320,256]{2,1,0:T(8,128)(2,1)S(1)}, u32[]{:S(2)}, u32[]{:S(2)}) collective-permute-start(bf16[2,320,256]{2,1,0:T(8,128)(2,1)S(1)} %get-tuple-element.17), channel_id=1, source_target_pairs={{0,96},{32,0},{64,32},{96,64},{128,224},{160,128},{192,160},{224,1... | collective-permute-start | bytes 983048 | tf_op jit(solution)/shard_map/ppermute | solution.py:212
  140.9 18.5 %collective-permute-start.27 = (bf16[2,320,320]{2,1,0:T(8,128)(2,1)S(1)}, bf16[2,320,320]{2,1,0:T(8,128)(2,1)S(1)}, u32[]{:S(2)}, u32[]{:S(2)}) collective-permute-start(bf16[2,320,320]{2,1,0:T(8,128)(2,1)S(1)} %fusion.7), channel_id=1, source_target_pairs={{0,128},{32,160},{64,192},{96,224},{128,0},{160,32},{192,64},{224,... | collective-permute-start | bytes 1228808 | tf_op jit(solution)/shard_map/ppermute | solution.py:219
  153.9 19.6 %collective-permute-start.20 = (bf16[2,320,256]{2,1,0:T(8,128)(2,1)S(1)}, bf16[2,320,256]{2,1,0:T(8,128)(2,1)S(1)}, u32[]{:S(2)}, u32[]{:S(2)}) collective-permute-start(bf16[2,320,256]{2,1,0:T(8,128)(2,1)S(1)} %fusion.8), channel_id=1, source_target_pairs={{0,128},{32,160},{64,192},{96,224},{128,0},{160,32},{192,64},{224,... | collective-permute-start | bytes 983048 | tf_op jit(solution)/shard_map/ppermute | solution.py:219
  161.3 15.7 %collective-permute-start.29 = (bf16[2,320,320]{2,1,0:T(8,128)(2,1)S(1)}, bf16[2,320,320]{2,1,0:T(8,128)(2,1)S(1)}, u32[]{:S(2)}, u32[]{:S(2)}) collective-permute-start(bf16[2,320,320]{2,1,0:T(8,128)(2,1)S(1)} %get-tuple-element.32.refs_0_), channel_id=1, source_target_pairs={{0,64},{32,96},{64,0},{96,32},{128,192},{160,224},{192,128},{224,1... | collective-permute-start | bytes 1228808 | tf_op jit(solution)/shard_map/ppermute | solution.py:212
  161.6 23.8 %collective-permute-start.30 = (bf16[2,320,320]{2,1,0:T(8,128)(2,1)S(1)}, bf16[2,320,320]{2,1,0:T(8,128)(2,1)S(1)}, u32[]{:S(2)}, u32[]{:S(2)}) collective-permute-start(bf16[2,320,320]{2,1,0:T(8,128)(2,1)S(1)} %get-tuple-element.32.refs_0_), channel_id=1, source_target_pairs={{0,96},{32,0},{64,32},{96,64},{128,224},{160,128},{192,160},{224,1... | collective-permute-start | bytes 1228808 | tf_op jit(solution)/shard_map/ppermute | solution.py:212
  190.1 77.8 %all-to-all-start.1 = ((bf16[16,80,256]{2,1,0:T(8,128)(2,1)}), bf16[16,80,256]{2,1,0:T(8,128)(2,1)}, u32[]{:S(2)}, u32[]{:S(2)}) async-start(bf16[16,80,256]{2,1,0:T(8,128)(2,1)} %add_convert_fusion), calls=%async_computation.1 | async-start | bytes 1310720 | tf_op jit(solution)/shard_map/all_to_all | solution.py:282
  219.8 19.1 %collective-permute-start.32 = (bf16[320,256]{1,0:T(8,128)(2,1)S(1)}, bf16[320,256]{1,0:T(8,128)(2,1)S(1)}, u32[]{:S(2)}, u32[]{:S(2)}) collective-permute-start(bf16[320,256]{1,0:T(8,128)(2,1)S(1)} %shard_map.97), channel_id=1, source_target_pairs={{0,128},{32,160},{64,192},{96,224},{128,0},{160,32},{192,64},{224,... | collective-permute-start | bytes 491528 | tf_op jit(solution)/shard_map/ppermute | solution.py:275
  240.1 18.2 %collective-permute-start.34 = (bf16[2,320,256]{2,1,0:T(8,128)(2,1)S(1)}, bf16[2,320,256]{2,1,0:T(8,128)(2,1)}, u32[]{:S(2)}, u32[]{:S(2)}) collective-permute-start(bf16[2,320,256]{2,1,0:T(8,128)(2,1)S(1)} %maximum_select_fusion.refs_8_), channel_id=1, source_target_pairs={{0,64},{32,96},{64,0},{96,32},{128,192},{160,224},{192,128},{224,1... | collective-permute-start | bytes 983048 | tf_op jit(solution)/shard_map/ppermute | solution.py:212
  240.8 19.0 %collective-permute-start.35 = (bf16[2,320,256]{2,1,0:T(8,128)(2,1)S(1)}, bf16[2,320,256]{2,1,0:T(8,128)(2,1)}, u32[]{:S(2)}, u32[]{:S(2)}) collective-permute-start(bf16[2,320,256]{2,1,0:T(8,128)(2,1)S(1)} %maximum_select_fusion.refs_8_), channel_id=1, source_target_pairs={{0,96},{32,0},{64,32},{96,64},{128,224},{160,128},{192,160},{224,1... | collective-permute-start | bytes 983048 | tf_op jit(solution)/shard_map/ppermute | solution.py:212
  241.6 28.2 %collective-permute-start.21 = (bf16[2,320,256]{2,1,0:T(8,128)(2,1)}, bf16[2,320,256]{2,1,0:T(8,128)(2,1)}, u32[]{:S(2)}, u32[]{:S(2)}) collective-permute-start(bf16[2,320,256]{2,1,0:T(8,128)(2,1)} %copy-done.4), channel_id=1, source_target_pairs={{0,32},{32,64},{64,96},{96,0},{128,160},{160,192},{192,224},{224,1... | collective-permute-start | bytes 983048 | tf_op jit(solution)/shard_map/ppermute | solution.py:212
  244.0 25.7 %collective-permute-start.22 = (bf16[2,320,256]{2,1,0:T(8,128)(2,1)}, bf16[2,320,256]{2,1,0:T(8,128)(2,1)}, u32[]{:S(2)}, u32[]{:S(2)}) collective-permute-start(bf16[2,320,256]{2,1,0:T(8,128)(2,1)} %copy-done.4), channel_id=1, source_target_pairs={{0,64},{32,96},{64,0},{96,32},{128,192},{160,224},{192,128},{224,1... | collective-permute-start | bytes 983048 | tf_op jit(solution)/shard_map/ppermute | solution.py:212
  252.7 17.1 %collective-permute-start.23 = (bf16[2,320,256]{2,1,0:T(8,128)(2,1)}, bf16[2,320,256]{2,1,0:T(8,128)(2,1)}, u32[]{:S(2)}, u32[]{:S(2)}) collective-permute-start(bf16[2,320,256]{2,1,0:T(8,128)(2,1)} %copy-done.4), channel_id=1, source_target_pairs={{0,96},{32,0},{64,32},{96,64},{128,224},{160,128},{192,160},{224,1... | collective-permute-start | bytes 983048 | tf_op jit(solution)/shard_map/ppermute | solution.py:212
  (42 other events, 368.0 us)
Sparse Core Ops, SparseCore 0:
  32.8 82.6 all-gather.1
where the time goes:
time: 285 us; the launch traced here: 282 us
  waiting for transfers between devices  131 us (46%)
  starting transfers between devices  86.2 us (30%)
  Pallas kernels  20.7 us (7%)
  local copies, waits for them, and re-layouts  20.2 us (7%)
  between operations  14.5 us (5%)
  other arithmetic  5.01 us (2%)
  matrix products  4.85 us (2%)
    ppermute x21, waiting for transfers between devices, exchange_y(): got = {k: lax.ppermute(block_for(k), 'dp', shift_y(k)) for k in (2, 1, 3)}  52.5 us
    ppermute x3, waiting for transfers between devices, source_blocks(): got = {k: lax.ppermute(strip, 'mp', shift_x(k)) for k in (2, 1, 3)}  28.4 us
    all_to_all x1, starting transfers between devices, shards(): lax.all_to_all(keep.astype(BF), 'mp', 0, 0, axis_index_groups=PLANE_GROUPS)  25.2 us
    ppermute x21, starting transfers between devices, exchange_y(): got = {k: lax.ppermute(block_for(k), 'dp', shift_y(k)) for k in (2, 1, 3)}  22.9 us
    pallas_call x6, Pallas kernels, call(): pl.pallas_call(body, out_shape=outs, grid=grid or (), in_specs=[pl.BlockS...  20.7 us
    unnamed x58, local copies, waits for them, and re-layouts  17.6 us
    ppermute x1, waiting for transfers between devices, shards(): other = lax.ppermute(back, 'dp', SWAP_ZH)  13.6 us
    ppermute x3, waiting for transfers between devices, source_blocks(): got = [chunk] + [lax.ppermute(chunk, 'mp', flip_z(k)) for k in (1, 2, 3)]  11.6 us
  transfers between devices with their start and end apart: 39, of which 26 were waited for; matrix products, arithmetic and copies ran while one was open for 4% of the time, Pallas kernels for 6%

commit v1 on v0

--- a/solution.py
+++ b/solution.py
@@ -208,14 +208,21 @@
     )
 
 
+def after(value, *done):
+    return lax.optimization_barrier((value, done))[0]
+
+
 def exchange_y(block_for):
     got = {k: lax.ppermute(block_for(k), "dp", shift_y(k)) for k in (2, 1, 3)}
     return [None, got[1], got[2], got[3]]
 
 
-def sum_dp(blocks):
+def sum_y(blocks):
     got = exchange_y(lambda k: blocks[k])
-    part = blocks[0] + got[1].astype(F32) + got[2].astype(F32) + got[3].astype(F32)
+    return blocks[0] + got[1].astype(F32) + got[2].astype(F32) + got[3].astype(F32)
+
+
+def sum_z(part):
     return part + lax.ppermute(part.astype(BF), "dp", SWAP_ZH).astype(F32)
 
 
@@ -223,12 +230,16 @@
     return [block] + exchange_y(lambda k: block)[1:]
 
 
-def source_blocks(saved, slot_of, z_hi, y):
+def panel_slots(saved, y):
     width = saved.shape[1]
     sub = saved.shape[0] // (MP * NY)
     rows = saved.reshape(NC, NX, NZ, NY, sub, width)
     mine = pick(rows, y, 3).transpose(1, 2, 0, 3, 4).reshape(MP, sub, width)
-    slots = lax.all_to_all(mine, "mp", 0, 0)
+    return lax.all_to_all(mine, "mp", 0, 0)
+
+
+def panel_strip(slots, slot_of, z_hi, y):
+    sub, width = slots.shape[1:]
     panels = jnp.take(slots, slot_of, axis=0).reshape(ZH, NY, -1, sub, width)
     panels = pick(panels, z_hi)
     got = exchange_y(lambda k: pick(panels, (y + k) % NY))
@@ -237,7 +248,10 @@
     chunk = chunk.transpose(0, 2, 1, 3).reshape(NY * sub, -1)
     z = lax.axis_index("mp") // NC % NZ
     got = [chunk] + [lax.ppermute(chunk, "mp", flip_z(k)) for k in (1, 2, 3)]
-    strip = jnp.concatenate([choose(z ^ j, got) for j in range(NZ)])
+    return jnp.concatenate([choose(z ^ j, got) for j in range(NZ)])
+
+
+def source_blocks(strip):
     got = {k: lax.ppermute(strip, "mp", shift_x(k)) for k in (2, 1, 3)}
     got[0] = strip
     blocks = []
@@ -253,9 +267,7 @@
     other = lax.ppermute(mine, "dp", SWAP_ZH)
     mine = jnp.where(z_hi == mp_index % NC, mine, other)
     strips = jnp.concatenate(gather_y(mine))
-    mixed = dot(strips, tokens, NT).astype(BF)
-    mixed = lax.all_gather(mixed, "mp", axis=0, tiled=True)
-    return mixed.reshape(NX * NZ, NC, NY, strip, -1)
+    return dot(strips, tokens, NT).astype(BF)
 
 
 def shards(tokens, cotangent, saved_panels, owners, row_growth, col_growth):
@@ -265,23 +277,33 @@
     place = jnp.stack([y, z_hi, x, core]).astype(jnp.int32)
     slot_of = owners[:, 1] * (MP // SECTIONS) + owners[:, 0]
 
-    source = source_blocks(saved_panels, slot_of, z_hi, y)
+    slots = panel_slots(saved_panels, y)
+    terms = grad_terms(place, tokens, cotangent.T)
     mixed = mixed_strips(tokens, row_growth, z_hi, mp_index)
-
-    grads = sum_dp(grad_terms(place, tokens, cotangent.T))
+    mixed_all = lax.all_gather(mixed, "mp", axis=0, tiled=True)
+    mixed_all = mixed_all.reshape(NX * NZ, NC, NY, -1, mixed.shape[1])
+
+    strip = panel_strip(after(slots, terms), slot_of, z_hi, y)
+    part = sum_y(terms)
+    source = source_blocks(after(strip, part, mixed))
+
+    grads = sum_z(part)
     grad = pick(grads, z_hi).T
     grads = gather_y(grads.astype(BF))
     back = back_block(place, row_growth, grads)
+
     other = lax.ppermute(back, "dp", SWAP_ZH)
     pair = jnp.where(z_hi == 0, jnp.stack([back, other]), jnp.stack([other, back]))
-    grad_col = col_grad(place, source, gather_y(pair))
-
-    inners = sum_dp(inner_terms(place, col_growth, source)).astype(BF)
+    backs = gather_y(pair)
+    grad_col = col_grad(place, source, backs)
+
+    inners = inner_terms(place, col_growth, after(source, grads))
+    inners = sum_z(after(sum_y(inners), pair)).astype(BF)
     keep, give = row_terms(place, pick(inners, z_hi), grads)
     keep = keep + lax.ppermute(give, "mp", SWAP_CORE).astype(F32)
     keep = lax.all_to_all(keep.astype(BF), "mp", 0, 0, axis_index_groups=PLANE_GROUPS)
     grad_row = keep.astype(F32).sum(axis=0)
-    grown_out = grown_output(place, mixed, gather_y(inners)).T
+    grown_out = grown_output(place, mixed_all, gather_y(after(inners, backs))).T
     return (grown_out, grad, grad_row, grad_col)
 
 

time: 285 us -> 280 us (0.982)
  waiting for transfers between devices: 131 us -> 106 us
  starting transfers between devices: 86.2 us -> 96.4 us
  other arithmetic: 5.01 us -> 11.1 us
  local copies, waits for them, and re-layouts: 20.2 us -> 23.7 us
    ppermute x3, starting transfers between devices: 2.32 us -> 17.1 us  [source_blocks(): got = {k: lax.ppermute(strip, 'mp', shift_x(k)) for k in (2, 1, 3)}]
    ppermute x3, waiting for transfers between devices: 28.4 us -> 14 us  [source_blocks(): got = {k: lax.ppermute(strip, 'mp', shift_x(k)) for k in (2, 1, 3)}]
    ppermute x21, waiting for transfers between devices: 52.5 us -> 65.7 us  [exchange_y(): got = {k: lax.ppermute(block_for(k), 'dp', shift_y(k)) for k in (2, 1, 3)}]
    all_to_all x1, starting transfers between devices: 25.2 us -> 14.7 us  [shards(): lax.all_to_all(keep.astype(BF), 'mp', 0, 0, axis_index_groups=PLANE_GROUPS)]
    ppermute x1, waiting for transfers between devices: 13.6 us -> 3.56 us  [shards(): other = lax.ppermute(back, 'dp', SWAP_ZH)]
    all_to_all x1, waiting for transfers between devices: 8.66 us -> 0.01 us  [panel_slots(): return lax.all_to_all(mine, 'mp', 0, 0)]
    ppermute x1, starting transfers between devices: 5.44 us -> 10.7 us  [shards(): other = lax.ppermute(back, 'dp', SWAP_ZH)]
    ppermute x5, waiting for transfers between devices: 22.5 us -> 17.9 us  [the longest x2 13.9 us: sum_z(): return part + lax.ppermute(part.astype(BF), 'dp', SWAP_ZH).astype(F32)]
  transfers between devices with their start and end apart: 39 -> 39, of which waited for: 26 -> 18; matrix products, arithmetic and copies ran while one was open for 4% -> 6% of each run, Pallas kernels for 6% -> 6%
where the time goes in v1:
time: 280 us; the launch traced here: 277 us
  waiting for transfers between devices  106 us (38%)
  starting transfers between devices  96.4 us (34%)
  local copies, waits for them, and re-layouts  23.7 us (8%)
  Pallas kernels  19.9 us (7%)
  between operations  14.6 us (5%)
  other arithmetic  11.1 us (4%)
  matrix products  4.84 us (2%)
    ppermute x21, waiting for transfers between devices, exchange_y(): got = {k: lax.ppermute(block_for(k), 'dp', shift_y(k)) for k in (2, 1, 3)}  65.7 us
    unnamed x70, local copies, waits for them, and re-layouts  21 us
    pallas_call x6, Pallas kernels, call(): pl.pallas_call(body, out_shape=outs, grid=grid or (), in_specs=[pl.BlockS...  19.9 us
    ppermute x21, starting transfers between devices, exchange_y(): got = {k: lax.ppermute(block_for(k), 'dp', shift_y(k)) for k in (2, 1, 3)}  19 us
    ppermute x3, starting transfers between devices, source_blocks(): got = {k: lax.ppermute(strip, 'mp', shift_x(k)) for k in (2, 1, 3)}  17.1 us
    ppermute x2, starting transfers between devices, sum_z(): return part + lax.ppermute(part.astype(BF), 'dp', SWAP_ZH).astype(F32)  15.6 us
    all_to_all x1, starting transfers between devices, shards(): lax.all_to_all(keep.astype(BF), 'mp', 0, 0, axis_index_groups=PLANE_GROUPS)  14.7 us
    ppermute x3, waiting for transfers between devices, source_blocks(): got = {k: lax.ppermute(strip, 'mp', shift_x(k)) for k in (2, 1, 3)}  14 us
  transfers between devices with their start and end apart: 39, of which 18 were waited for; matrix products, arithmetic and copies ran while one was open for 6% of the time, Pallas kernels for 6%

profile of v1, /device:TPU:30, one launch (start us, length us, event | category | flops | bytes accessed | tf_op | source)
XLA Modules:
  0.0 276.9 jit_solution(227061499308872347)
XLA Ops:
  9.0 7.3 %collective-permute-start = (bf16[16,2560]{1,0:T(8,128)(2,1)S(1)}, bf16[16,2560]{1,0:T(8,128)(2,1)S(1)}, u32[]{:S(2)}, u32[]{:S(2)}) collective-permute-start(bf16[16,2560]{1,0:T(8,128)(2,1)S(1)} %dynamic-slice_bitcast_fusion.2), channel_id=1, source_target_pairs={{0,128},{32,160},{64,192},{96,224},{128,0},{160,32},{192,64},{224,... | collective-permute-start | bytes 245768 | tf_op jit(solution)/shard_map/ppermute | solution.py:267
  16.2 3.0 %collective-permute-done = bf16[16,2560]{1,0:T(8,128)(2,1)S(1)} collective-permute-done((bf16[16,2560]{1,0:T(8,128)(2,1)S(1)}, bf16[16,2560]{1,0:T(8,128)(2,1)S(1)}, u32[]{:S(2)}, u32[]{:S(2)}) %collective-permute-start) | collective-permute-done | bytes 81952 | tf_op jit(solution)/shard_map/ppermute | solution.py:267
  27.8 4.8 %convolution_convert_fusion = bf16[64,1024]{1,0:T(8,128)(2,1)} fusion(bf16[1024,2560]{1,0:T(8,128)(2,1)} %tokens.1, bf16[16,2560]{1,0:T(8,128)(2,1)S(1)} %collective-permute-done.3, bf16[16,2560]{1,0:T(8,128)(2,1)S(1)} %collective-permute-done.2, bf16[16,2560]{1,0:T(8,128)(2,1)S(1)} %collective-permute-done.1, bf16[16,2560]{1,0:T(8,128)(2,1)S(1)} %broadcast_select_fusion.1), kind=kOutput, calls=%fused_computation.3 | convolution fusion | flops 336920576 | bytes 5701632 | tf_op jit(solution)/shard_map/dot_general | solution.py:38
  33.5 7.4 %all-to-all-start = ((bf16[32,16,256]{2,1,0:T(8,128)(2,1)}), bf16[32,16,256]{2,1,0:T(8,128)(2,1)S(1)}, u32[]{:S(2)}, u32[]{:S(2)}) async-start(bf16[32,16,256]{2,1,0:T(8,128)(2,1)} %bitcast.11), calls=%async_computation | async-start | bytes 524288 | tf_op jit(solution)/shard_map/all_to_all | solution.py:238
  43.7 4.6 %shard_map.93 = (f32[2,320,320]{2,1,0:T(8,128)S(1)}, bf16[2,320,320]{2,1,0:T(8,128)(2,1)S(1)}, bf16[2,320,320]{2,1,0:T(8,128)(2,1)S(1)}, bf16[2,320,320]{2,1,0:T(8,128)(2,1)S(1)}) custom-call(s32[4]{0:T(128)S(1)} %pad_add_fusion.place, bf16[1024,2560]{1,0:T(8,128)(2,1)S(1)} %copy-done.1, bf16[320,1024]{1,0:T(8,128)(2,1)S(1)} %bitcast.82), custom_call_target="tpu_custom_call" | custom-call | flops 1677721600 | bytes 7946240 | tf_op jit(solution)/shard_map/pallas_call | solution.py:55
  57.6 19.1 %collective-permute-done.5 = bf16[4,16,256]{2,1,0:T(8,128)(2,1)S(1)} collective-permute-done((bf16[4,16,256]{2,1,0:T(8,128)(2,1)S(1)}, bf16[4,16,256]{2,1,0:T(8,128)(2,1)S(1)}, u32[]{:S(2)}, u32[]{:S(2)}) %collective-permute-start.5) | collective-permute-done | bytes 32800 | tf_op jit(solution)/shard_map/ppermute | solution.py:216
  86.3 5.6 %collective-permute-start.20 = (bf16[2,320,320]{2,1,0:T(8,128)(2,1)}, bf16[2,320,320]{2,1,0:T(8,128)(2,1)}, u32[]{:S(2)}, u32[]{:S(2)}) collective-permute-start(bf16[2,320,320]{2,1,0:T(8,128)(2,1)} %get-tuple-element.58), channel_id=1, source_target_pairs={{0,128},{32,160},{64,192},{96,224},{128,0},{160,32},{192,64},{224,... | collective-permute-start | bytes 1228808 | tf_op jit(solution)/shard_map/ppermute | solution.py:226
  92.0 4.0 %collective-permute-done.9 = bf16[64,1024]{1,0:T(8,128)(2,1)} collective-permute-done((bf16[64,1024]{1,0:T(8,128)(2,1)S(1)}, bf16[64,1024]{1,0:T(8,128)(2,1)}, u32[]{:S(2)}, u32[]{:S(2)}) %collective-permute-start.9) | collective-permute-done | bytes 131104 | tf_op jit(solution)/shard_map/ppermute | solution.py:250
  98.4 14.5 %collective-permute-start.16 = (bf16[256,1024]{1,0:T(8,128)(2,1)S(1)}, bf16[256,1024]{1,0:T(8,128)(2,1)S(1)}, u32[]{:S(2)}, u32[]{:S(2)}) collective-permute-start(bf16[256,1024]{1,0:T(8,128)(2,1)S(1)} %pad_maximum_fusion.refs_0_), channel_id=1, source_target_pairs={{0,16},{1,17},{2,18},{3,19},{4,20},{5,21},{6,22},{7,23},{8,24},{9,... | collective-permute-start | bytes 1572872 | tf_op jit(solution)/shard_map/ppermute | solution.py:255
  114.2 5.9 %collective-permute-done.20 = bf16[2,320,320]{2,1,0:T(8,128)(2,1)} collective-permute-done((bf16[2,320,320]{2,1,0:T(8,128)(2,1)}, bf16[2,320,320]{2,1,0:T(8,128)(2,1)}, u32[]{:S(2)}, u32[]{:S(2)}) %collective-permute-start.20) | collective-permute-done | bytes 409632 | tf_op jit(solution)/shard_map/ppermute | solution.py:226
  122.4 3.2 %collective-permute-done.16.refs_4_ = bf16[256,1024]{1,0:T(8,128)(2,1)S(1)} collective-permute-done((bf16[256,1024]{1,0:T(8,128)(2,1)S(1)}, bf16[256,1024]{1,0:T(8,128)(2,1)S(1)}, u32[]{:S(2)}, u32[]{:S(2)}) %collective-permute-start.16) | collective-permute-done | bytes 524320 | tf_op jit(solution)/shard_map/ppermute | solution.py:255
  125.7 10.8 %collective-permute-done.18.refs_6_ = bf16[256,1024]{1,0:T(8,128)(2,1)S(1)} collective-permute-done((bf16[256,1024]{1,0:T(8,128)(2,1)S(1)}, bf16[256,1024]{1,0:T(8,128)(2,1)S(1)}, u32[]{:S(2)}, u32[]{:S(2)}) %collective-permute-start.18) | collective-permute-done | bytes 524320 | tf_op jit(solution)/shard_map/ppermute | solution.py:255
  137.5 14.6 %collective-permute-done.22.refs_2_ = bf16[2,320,320]{2,1,0:T(8,128)(2,1)S(1)} collective-permute-done((bf16[2,320,320]{2,1,0:T(8,128)(2,1)S(1)}, bf16[2,320,320]{2,1,0:T(8,128)(2,1)S(1)}, u32[]{:S(2)}, u32[]{:S(2)}) %collective-permute-start.22) | collective-permute-done | bytes 409632 | tf_op jit(solution)/shard_map/ppermute | solution.py:216
  152.1 10.0 %collective-permute-done.23.refs_3_ = bf16[2,320,320]{2,1,0:T(8,128)(2,1)S(1)} collective-permute-done((bf16[2,320,320]{2,1,0:T(8,128)(2,1)S(1)}, bf16[2,320,320]{2,1,0:T(8,128)(2,1)S(1)}, u32[]{:S(2)}, u32[]{:S(2)}) %collective-permute-start.23) | collective-permute-done | bytes 409632 | tf_op jit(solution)/shard_map/ppermute | solution.py:216
  162.2 5.8 %shard_map.94 = (f32[2,320,256]{2,1,0:T(8,128)S(1)}, bf16[2,320,256]{2,1,0:T(8,128)(2,1)}, bf16[2,320,256]{2,1,0:T(8,128)(2,1)}, bf16[2,320,256]{2,1,0:T(8,128)(2,1)}) custom-call(s32[4]{0:T(128)S(1)} %pad_add_fusion.place, bf16[320,1024]{1,0:T(8,128)(2,1)S(1)} %copy-done.29, bf16[256,1024]{1,0:T(8,128)(2,1)S(1)} %pad_maximum_fusion.refs_0_, ...), custom_call_target="tpu_custom_call" | custom-call | flops 1342177280 | bytes 6488064 | tf_op jit(solution)/shard_map/pallas_call | solution.py:55
  171.9 10.7 %collective-permute-start.27 = (bf16[320,256]{1,0:T(8,128)(2,1)S(1)}, bf16[320,256]{1,0:T(8,128)(2,1)S(1)}, u32[]{:S(2)}, u32[]{:S(2)}) collective-permute-start(bf16[320,256]{1,0:T(8,128)(2,1)S(1)} %shard_map.95), channel_id=1, source_target_pairs={{0,128},{32,160},{64,192},{96,224},{128,0},{160,32},{192,64},{224,... | collective-permute-start | bytes 491528 | tf_op jit(solution)/shard_map/ppermute | solution.py:295
  182.6 3.6 %collective-permute-done.27 = bf16[320,256]{1,0:T(8,128)(2,1)S(1)} collective-permute-done((bf16[320,256]{1,0:T(8,128)(2,1)S(1)}, bf16[320,256]{1,0:T(8,128)(2,1)S(1)}, u32[]{:S(2)}, u32[]{:S(2)}) %collective-permute-start.27) | collective-permute-done | bytes 163872 | tf_op jit(solution)/shard_map/ppermute | solution.py:295
  188.5 9.9 %collective-permute-start.28 = (bf16[2,320,256]{2,1,0:T(8,128)(2,1)S(1)}, bf16[2,320,256]{2,1,0:T(8,128)(2,1)S(1)}, u32[]{:S(2)}, u32[]{:S(2)}) collective-permute-start(bf16[2,320,256]{2,1,0:T(8,128)(2,1)S(1)} %convert_element_type.58), channel_id=1, source_target_pairs={{0,128},{32,160},{64,192},{96,224},{128,0},{160,32},{192,64},{224,... | collective-permute-start | bytes 983048 | tf_op jit(solution)/shard_map/ppermute | solution.py:226
  198.5 8.0 %collective-permute-done.28 = bf16[2,320,256]{2,1,0:T(8,128)(2,1)S(1)} collective-permute-done((bf16[2,320,256]{2,1,0:T(8,128)(2,1)S(1)}, bf16[2,320,256]{2,1,0:T(8,128)(2,1)S(1)}, u32[]{:S(2)}, u32[]{:S(2)}) %collective-permute-start.28) | collective-permute-done | bytes 327712 | tf_op jit(solution)/shard_map/ppermute | solution.py:226
  211.2 14.7 %all-to-all-start.1 = ((bf16[16,80,256]{2,1,0:T(8,128)(2,1)}), bf16[16,80,256]{2,1,0:T(8,128)(2,1)}, u32[]{:S(2)}, u32[]{:S(2)}) async-start(bf16[16,80,256]{2,1,0:T(8,128)(2,1)} %add_convert_fusion), calls=%async_computation.1 | async-start | bytes 1310720 | tf_op jit(solution)/shard_map/all_to_all | solution.py:304
  228.7 8.0 %collective-permute-done.29.refs_9_ = bf16[2,320,256]{2,1,0:T(8,128)(2,1)S(1)} collective-permute-done((bf16[2,320,256]{2,1,0:T(8,128)(2,1)S(1)}, bf16[2,320,256]{2,1,0:T(8,128)(2,1)S(1)}, u32[]{:S(2)}, u32[]{:S(2)}) %collective-permute-start.29) | collective-permute-done | bytes 327712 | tf_op jit(solution)/shard_map/ppermute | solution.py:216
  239.2 4.6 %collective-permute-done.31.refs_11_ = bf16[2,320,256]{2,1,0:T(8,128)(2,1)S(1)} collective-permute-done((bf16[2,320,256]{2,1,0:T(8,128)(2,1)S(1)}, bf16[2,320,256]{2,1,0:T(8,128)(2,1)S(1)}, u32[]{:S(2)}, u32[]{:S(2)}) %collective-permute-start.31) | collective-permute-done | bytes 327712 | tf_op jit(solution)/shard_map/ppermute | solution.py:216
  259.3 3.2 %shard_map.98 = f32[320,1024]{1,0:T(8,128)} custom-call(s32[4]{0:T(128)S(1)} %pad_add_fusion.place, bf16[256,1024]{1,0:T(8,128)(2,1)S(1)} %pad_maximum_fusion.refs_0_, bf16[256,1024]{1,0:T(8,128)(2,1)S(1)} %copy-done.15, bf16[256,1024]{1,0:T(8,128)(2,1)S(1)} %copy-done.9, bf16[256,1024]{1,0:T(8,128)(2,1)S(1)} %copy-done.17, ...), custom_call_target="tpu_custom_call" | custom-call | flops 1342177280 | bytes 6815744 | tf_op jit(solution)/shard_map/pallas_call | solution.py:55
  266.5 3.5 %shard_map.96 = bf16[320,1024]{1,0:T(8,128)(2,1)} custom-call(s32[4]{0:T(128)S(1)} %pad_add_fusion.place, bf16[16,2,4,16,1024]{4,3,2,1,0:T(8,128)(2,1)S(1)} %bitcast.80, bf16[2,320,256]{2,1,0:T(8,128)(2,1)S(1)} %add_convert_fusion.1.refs_0_, bf16[2,320,256]{2,1,0:T(8,128)(2,1)} %collective-permute-done.32.refs_1_, ...), custom_call_target="tpu_custom_call" | custom-call | flops 1342177280 | bytes 6160384 | tf_op jit(solution)/shard_map/pallas_call | solution.py:55
  (157 shorter events, 75.4 us)
Async XLA Ops:
  7.2 257.1 %all-gather.2.cloned.1.call-start = ((), (), s32[]{:S(2)}) async-start(), calls=%async_computation.2 | async-start | bytes 4325376 | tf_op jit(solution)/shard_map/all_gather | solution.py:283
  51.3 31.4 %collective-permute-start.10 = (bf16[2,320,320]{2,1,0:T(8,128)(2,1)}, bf16[2,320,320]{2,1,0:T(8,128)(2,1)}, u32[]{:S(2)}, u32[]{:S(2)}) collective-permute-start(bf16[2,320,320]{2,1,0:T(8,128)(2,1)} %copy-done.31), channel_id=1, source_target_pairs={{0,32},{32,64},{64,96},{96,0},{128,160},{160,192},{192,224},{224,1... | collective-permute-start | bytes 1228808 | tf_op jit(solution)/shard_map/ppermute | solution.py:216
  53.0 31.0 %collective-permute-start.11 = (bf16[2,320,320]{2,1,0:T(8,128)(2,1)}, bf16[2,320,320]{2,1,0:T(8,128)(2,1)}, u32[]{:S(2)}, u32[]{:S(2)}) collective-permute-start(bf16[2,320,320]{2,1,0:T(8,128)(2,1)} %copy-done.30), channel_id=1, source_target_pairs={{0,64},{32,96},{64,0},{96,32},{128,192},{160,224},{192,128},{224,1... | collective-permute-start | bytes 1228808 | tf_op jit(solution)/shard_map/ppermute | solution.py:216
  54.2 29.8 %collective-permute-start.12 = (bf16[2,320,320]{2,1,0:T(8,128)(2,1)S(1)}, bf16[2,320,320]{2,1,0:T(8,128)(2,1)}, u32[]{:S(2)}, u32[]{:S(2)}) collective-permute-start(bf16[2,320,320]{2,1,0:T(8,128)(2,1)S(1)} %get-tuple-element.29), channel_id=1, source_target_pairs={{0,96},{32,0},{64,32},{96,64},{128,224},{160,128},{192,160},{224,1... | collective-permute-start | bytes 1228808 | tf_op jit(solution)/shard_map/ppermute | solution.py:216
  55.6 21.1 %collective-permute-start.5 = (bf16[4,16,256]{2,1,0:T(8,128)(2,1)S(1)}, bf16[4,16,256]{2,1,0:T(8,128)(2,1)S(1)}, u32[]{:S(2)}, u32[]{:S(2)}) collective-permute-start(bf16[4,16,256]{2,1,0:T(8,128)(2,1)S(1)} %get-tuple-element.71), channel_id=1, source_target_pairs={{0,32},{32,64},{64,96},{96,0},{128,160},{160,192},{192,224},{224,1... | collective-permute-start | bytes 98312 | tf_op jit(solution)/shard_map/ppermute | solution.py:216
  57.4 21.9 %collective-permute-start.6 = (bf16[4,16,256]{2,1,0:T(8,128)(2,1)S(1)}, bf16[4,16,256]{2,1,0:T(8,128)(2,1)S(1)}, u32[]{:S(2)}, u32[]{:S(2)}) collective-permute-start(bf16[4,16,256]{2,1,0:T(8,128)(2,1)S(1)} %get-tuple-element.70), channel_id=1, source_target_pairs={{0,96},{32,0},{64,32},{96,64},{128,224},{160,128},{192,160},{224,1... | collective-permute-start | bytes 98312 | tf_op jit(solution)/shard_map/ppermute | solution.py:216
  86.3 33.8 %collective-permute-start.20 = (bf16[2,320,320]{2,1,0:T(8,128)(2,1)}, bf16[2,320,320]{2,1,0:T(8,128)(2,1)}, u32[]{:S(2)}, u32[]{:S(2)}) collective-permute-start(bf16[2,320,320]{2,1,0:T(8,128)(2,1)} %get-tuple-element.58), channel_id=1, source_target_pairs={{0,128},{32,160},{64,192},{96,224},{128,0},{160,32},{192,64},{224,... | collective-permute-start | bytes 1228808 | tf_op jit(solution)/shard_map/ppermute | solution.py:226
  97.1 25.3 %collective-permute-start.14 = (bf16[256,1024]{1,0:T(8,128)(2,1)S(1)}, bf16[256,1024]{1,0:T(8,128)(2,1)S(1)}, u32[]{:S(2)}, u32[]{:S(2)}) collective-permute-start(bf16[256,1024]{1,0:T(8,128)(2,1)S(1)} %pad_maximum_fusion.refs_0_), channel_id=1, source_target_pairs={{0,8},{1,9},{2,10},{3,11},{4,12},{5,13},{6,14},{7,15},{8,16},{9,17... | collective-permute-start | bytes 1572872 | tf_op jit(solution)/shard_map/ppermute | solution.py:255
  98.4 27.2 %collective-permute-start.16 = (bf16[256,1024]{1,0:T(8,128)(2,1)S(1)}, bf16[256,1024]{1,0:T(8,128)(2,1)S(1)}, u32[]{:S(2)}, u32[]{:S(2)}) collective-permute-start(bf16[256,1024]{1,0:T(8,128)(2,1)S(1)} %pad_maximum_fusion.refs_0_), channel_id=1, source_target_pairs={{0,16},{1,17},{2,18},{3,19},{4,20},{5,21},{6,22},{7,23},{8,24},{9,... | collective-permute-start | bytes 1572872 | tf_op jit(solution)/shard_map/ppermute | solution.py:255
  112.9 23.6 %collective-permute-start.18 = (bf16[256,1024]{1,0:T(8,128)(2,1)S(1)}, bf16[256,1024]{1,0:T(8,128)(2,1)S(1)}, u32[]{:S(2)}, u32[]{:S(2)}) collective-permute-start(bf16[256,1024]{1,0:T(8,128)(2,1)S(1)} %pad_maximum_fusion.refs_0_), channel_id=1, source_target_pairs={{0,24},{1,25},{2,26},{3,27},{4,28},{5,29},{6,30},{7,31},{8,0},{9,1... | collective-permute-start | bytes 1572872 | tf_op jit(solution)/shard_map/ppermute | solution.py:255
  114.2 22.3 %collective-permute-start.13 = (bf16[256,1024]{1,0:T(8,128)(2,1)S(1)}, bf16[256,1024]{1,0:T(8,128)(2,1)S(1)}, u32[]{:S(2)}, u32[]{:S(2)}) collective-permute-start(bf16[256,1024]{1,0:T(8,128)(2,1)S(1)} %pad_maximum_fusion.refs_0_), channel_id=1, source_target_pairs={{0,1},{1,0},{2,3},{3,2},{4,5},{5,4},{6,7},{7,6},{8,9},{9,8},{10,11... | collective-permute-start | bytes 1572872 | tf_op jit(solution)/shard_map/ppermute | solution.py:259
  122.4 39.8 %collective-permute-start.15 = (bf16[256,1024]{1,0:T(8,128)(2,1)S(1)}, bf16[256,1024]{1,0:T(8,128)(2,1)S(1)}, u32[]{:S(2)}, u32[]{:S(2)}) collective-permute-start(bf16[256,1024]{1,0:T(8,128)(2,1)S(1)} %collective-permute-done.14.refs_2_), channel_id=1, source_target_pairs={{0,1},{1,0},{2,3},{3,2},{4,5},{5,4},{6,7},{7,6},{8,9},{9,8},{10,11... | collective-permute-start | bytes 1572872 | tf_op jit(solution)/shard_map/ppermute | solution.py:259
  125.6 36.5 %collective-permute-start.17 = (bf16[256,1024]{1,0:T(8,128)(2,1)S(1)}, bf16[256,1024]{1,0:T(8,128)(2,1)S(1)}, u32[]{:S(2)}, u32[]{:S(2)}) collective-permute-start(bf16[256,1024]{1,0:T(8,128)(2,1)S(1)} %collective-permute-done.16.refs_4_), channel_id=1, source_target_pairs={{0,1},{1,0},{2,3},{3,2},{4,5},{5,4},{6,7},{7,6},{8,9},{9,8},{10,11... | collective-permute-start | bytes 1572872 | tf_op jit(solution)/shard_map/ppermute | solution.py:259
  136.5 25.7 %collective-permute-start.19 = (bf16[256,1024]{1,0:T(8,128)(2,1)S(1)}, bf16[256,1024]{1,0:T(8,128)(2,1)S(1)}, u32[]{:S(2)}, u32[]{:S(2)}) collective-permute-start(bf16[256,1024]{1,0:T(8,128)(2,1)S(1)} %collective-permute-done.18.refs_6_), channel_id=1, source_target_pairs={{0,1},{1,0},{2,3},{3,2},{4,5},{5,4},{6,7},{7,6},{8,9},{9,8},{10,11... | collective-permute-start | bytes 1572872 | tf_op jit(solution)/shard_map/ppermute | solution.py:259
  137.5 24.7 %collective-permute-start.23 = (bf16[2,320,320]{2,1,0:T(8,128)(2,1)S(1)}, bf16[2,320,320]{2,1,0:T(8,128)(2,1)S(1)}, u32[]{:S(2)}, u32[]{:S(2)}) collective-permute-start(bf16[2,320,320]{2,1,0:T(8,128)(2,1)S(1)} %get-tuple-element.56.refs_0_), channel_id=1, source_target_pairs={{0,96},{32,0},{64,32},{96,64},{128,224},{160,128},{192,160},{224,1... | collective-permute-start | bytes 1228808 | tf_op jit(solution)/shard_map/ppermute | solution.py:216
  168.1 18.9 %collective-permute-start.24 = (bf16[2,320,256]{2,1,0:T(8,128)(2,1)}, bf16[2,320,256]{2,1,0:T(8,128)(2,1)}, u32[]{:S(2)}, u32[]{:S(2)}) collective-permute-start(bf16[2,320,256]{2,1,0:T(8,128)(2,1)} %get-tuple-element.41), channel_id=1, source_target_pairs={{0,32},{32,64},{64,96},{96,0},{128,160},{160,192},{192,224},{224,1... | collective-permute-start | bytes 983048 | tf_op jit(solution)/shard_map/ppermute | solution.py:216
  168.8 18.2 %collective-permute-start.25 = (bf16[2,320,256]{2,1,0:T(8,128)(2,1)}, bf16[2,320,256]{2,1,0:T(8,128)(2,1)}, u32[]{:S(2)}, u32[]{:S(2)}) collective-permute-start(bf16[2,320,256]{2,1,0:T(8,128)(2,1)} %get-tuple-element.42), channel_id=1, source_target_pairs={{0,64},{32,96},{64,0},{96,32},{128,192},{160,224},{192,128},{224,1... | collective-permute-start | bytes 983048 | tf_op jit(solution)/shard_map/ppermute | solution.py:216
  169.7 17.3 %collective-permute-start.26 = (bf16[2,320,256]{2,1,0:T(8,128)(2,1)}, bf16[2,320,256]{2,1,0:T(8,128)(2,1)}, u32[]{:S(2)}, u32[]{:S(2)}) collective-permute-start(bf16[2,320,256]{2,1,0:T(8,128)(2,1)} %get-tuple-element.43), channel_id=1, source_target_pairs={{0,96},{32,0},{64,32},{96,64},{128,224},{160,128},{192,160},{224,1... | collective-permute-start | bytes 983048 | tf_op jit(solution)/shard_map/ppermute | solution.py:216
  188.5 17.9 %collective-permute-start.28 = (bf16[2,320,256]{2,1,0:T(8,128)(2,1)S(1)}, bf16[2,320,256]{2,1,0:T(8,128)(2,1)S(1)}, u32[]{:S(2)}, u32[]{:S(2)}) collective-permute-start(bf16[2,320,256]{2,1,0:T(8,128)(2,1)S(1)} %convert_element_type.58), channel_id=1, source_target_pairs={{0,128},{32,160},{64,192},{96,224},{128,0},{160,32},{192,64},{224,... | collective-permute-start | bytes 983048 | tf_op jit(solution)/shard_map/ppermute | solution.py:226
  211.2 51.2 %all-to-all-start.1 = ((bf16[16,80,256]{2,1,0:T(8,128)(2,1)}), bf16[16,80,256]{2,1,0:T(8,128)(2,1)}, u32[]{:S(2)}, u32[]{:S(2)}) async-start(bf16[16,80,256]{2,1,0:T(8,128)(2,1)} %add_convert_fusion), calls=%async_computation.1 | async-start | bytes 1310720 | tf_op jit(solution)/shard_map/all_to_all | solution.py:304
  227.4 16.5 %collective-permute-start.31 = (bf16[2,320,256]{2,1,0:T(8,128)(2,1)S(1)}, bf16[2,320,256]{2,1,0:T(8,128)(2,1)S(1)}, u32[]{:S(2)}, u32[]{:S(2)}) collective-permute-start(bf16[2,320,256]{2,1,0:T(8,128)(2,1)S(1)} %copy-done.6), channel_id=1, source_target_pairs={{0,96},{32,0},{64,32},{96,64},{128,224},{160,128},{192,160},{224,1... | collective-permute-start | bytes 983048 | tf_op jit(solution)/shard_map/ppermute | solution.py:216
  244.6 19.7 %collective-permute-start.32 = (bf16[2,320,256]{2,1,0:T(8,128)(2,1)S(1)}, bf16[2,320,256]{2,1,0:T(8,128)(2,1)}, u32[]{:S(2)}, u32[]{:S(2)}) collective-permute-start(bf16[2,320,256]{2,1,0:T(8,128)(2,1)S(1)} %add_convert_fusion.1.refs_0_), channel_id=1, source_target_pairs={{0,32},{32,64},{64,96},{96,0},{128,160},{160,192},{192,224},{224,1... | collective-permute-start | bytes 983048 | tf_op jit(solution)/shard_map/ppermute | solution.py:216
  246.4 17.9 %collective-permute-start.33 = (bf16[2,320,256]{2,1,0:T(8,128)(2,1)S(1)}, bf16[2,320,256]{2,1,0:T(8,128)(2,1)}, u32[]{:S(2)}, u32[]{:S(2)}) collective-permute-start(bf16[2,320,256]{2,1,0:T(8,128)(2,1)S(1)} %add_convert_fusion.1.refs_0_), channel_id=1, source_target_pairs={{0,64},{32,96},{64,0},{96,32},{128,192},{160,224},{192,128},{224,1... | collective-permute-start | bytes 983048 | tf_op jit(solution)/shard_map/ppermute | solution.py:216
  246.5 17.8 %collective-permute-start.34 = (bf16[2,320,256]{2,1,0:T(8,128)(2,1)S(1)}, bf16[2,320,256]{2,1,0:T(8,128)(2,1)}, u32[]{:S(2)}, u32[]{:S(2)}) collective-permute-start(bf16[2,320,256]{2,1,0:T(8,128)(2,1)S(1)} %add_convert_fusion.1.refs_0_), channel_id=1, source_target_pairs={{0,96},{32,0},{64,32},{96,64},{128,224},{160,128},{192,160},{224,1... | collective-permute-start | bytes 983048 | tf_op jit(solution)/shard_map/ppermute | solution.py:216
  (48 other events, 593.5 us)
Sparse Core Ops, SparseCore 0:
  32.8 75.4 all-gather.1

commit v2 on v1

--- a/solution.py
+++ b/solution.py
@@ -18,20 +18,6 @@
 
 def shift_y(k):
     return [(h * NY + y, h * NY + (y + k) % NY) for h in range(ZH) for y in range(NY)]
-
-
-def shift_x(k):
-    return [
-        ((x * NZ + z) * NC + c, ((x + k) % NX * NZ + z) * NC + c)
-        for x in range(NX) for z in range(NZ) for c in range(NC)
-    ]
-
-
-def flip_z(k):
-    return [
-        ((x * NZ + z) * NC + c, (x * NZ + (z ^ k)) * NC + c)
-        for x in range(NX) for z in range(NZ) for c in range(NC)
-    ]
 
 
 def dot(a, b, dims):
@@ -129,40 +115,58 @@
     )
 
 
-def inner_body(place, col, *refs):
-    source, outs = refs[:2 * NX], refs[2 * NX:]
-    for k in range(NX):
-        for c in range(NC):
-            block = dot(col[...], source[2 * k + c][...], NT)
-            where = lax.rem(place[2] - k - place[0] + 2 * NX, NX)
-            put(block, where, place[3] ^ c, outs)
+def inner_body(place, col, mine, other, *outs):
+    block = pl.program_id(0)
+    k = lax.rem(block - place[0] + NY, NY)
+    put(dot(col[...], mine[...], NT), k, place[3], outs)
+    put(dot(col[...], other[...], NT), k, 1 - place[3], outs)
+
+
+def stream(rows, width):
+    return pl.BlockSpec((rows, width), lambda s: (s, 0))
+
+
+def keep_whole(shape):
+    return pl.BlockSpec(shape, lambda s: (0,) * len(shape))
 
 
 def inner_terms(place, col, source):
-    hidden, rows = col.shape[0], source[0].shape[0]
+    hidden, width = col.shape
+    rows = source[0].shape[0] // NY
     shape = (ZH, hidden, rows)
     outs = [struct(shape, F32)] + [struct(shape, BF)] * (NY - 1)
-    return call(inner_body, place, (col, *source), outs, 2 * col.size * rows * len(source))
-
-
-def col_body(place, *refs):
-    source, back, out, held = refs[:2 * NX], refs[2 * NX:2 * NX + NY], refs[-2], refs[-1]
-    for k in range(NY):
-        held[k] = back[k][...]
-    total = jnp.zeros(out.shape, F32)
-    for k in range(NX):
-        for c in range(NC):
-            at = lax.rem(place[0] - place[2] + k + NY, NY)
-            total += dot(held[at, place[3] ^ c], source[2 * k + c][...], NN)
-    out[...] = total
+    return call(
+        inner_body, place, (col, *source), outs, 4 * source[0].size * hidden,
+        grid=(NY,),
+        in_specs=[keep_whole(col.shape), stream(rows, width), stream(rows, width)],
+        out_specs=[keep_whole(shape)] * NY,
+    )
+
+
+def col_body(place, mine, other, *refs):
+    back, out, held = refs[:NY], refs[NY], refs[NY + 1]
+    block = pl.program_id(0)
+
+    @pl.when(block == 0)
+    def _():
+        for k in range(NY):
+            held[k] = back[k][...]
+        out[...] = jnp.zeros(out.shape, F32)
+
+    k = lax.rem(place[0] - block + NY, NY)
+    out[...] += dot(held[k, place[3]], mine[...], NN) + dot(held[k, 1 - place[3]], other[...], NN)
 
 
 def col_grad(place, source, back):
     hidden, rows = back[0].shape[1:]
-    return call(
-        col_body, place, (*source, *back), struct((hidden, source[0].shape[1]), F32),
-        2 * hidden * sum(s.size for s in source),
+    width = source[0].shape[1]
+    return call(
+        col_body, place, (*source, *back), struct((hidden, width), F32),
+        4 * source[0].size * hidden,
         scratch=[pltpu.VMEM((NY, *back[0].shape), BF)],
+        grid=(NY,),
+        in_specs=[stream(rows, width)] * 2 + [keep_whole(back[0].shape)] * NY,
+        out_specs=keep_whole((hidden, width)),
     )
 
 
@@ -190,21 +194,25 @@
     )
 
 
-def out_body(place, mixed, *refs):
+def out_body(place, mine, other, *refs):
     inner, out = refs[:NY], refs[NY]
     total = jnp.zeros(out.shape, F32)
     for k in range(NY):
-        for h in range(ZH):
-            rows = mixed[:, h, k]
-            total += dot(inner[k][h], rows.reshape(-1, rows.shape[-1]), NN)
+        for rows, h in ((mine, place[3]), (other, 1 - place[3])):
+            total += dot(inner[k][h], rows[:, k].reshape(-1, out.shape[1]), NN)
     out[...] = total.astype(out.dtype)
 
 
 def grown_output(place, mixed, inner):
-    hidden = inner[0].shape[1]
-    return call(
-        out_body, place, (mixed, *inner), struct((hidden, mixed.shape[-1]), BF),
-        2 * mixed.size * hidden,
+    hidden, count = inner[0].shape[1], mixed[0].shape[-1]
+    part = count // 4
+    rows = pl.BlockSpec((*mixed[0].shape[:-1], part), lambda s: (0, 0, 0, s))
+    return call(
+        out_body, place, (*mixed, *inner), struct((hidden, count), BF),
+        4 * mixed[0].size * hidden,
+        grid=(count // part,),
+        in_specs=[rows] * 2 + [keep_whole(inner[0].shape)] * NY,
+        out_specs=pl.BlockSpec((hidden, part), lambda s: (0, s)),
     )
 
 
@@ -238,26 +246,22 @@
     return lax.all_to_all(mine, "mp", 0, 0)
 
 
-def panel_strip(slots, slot_of, z_hi, y):
+def panel_rows(slots, slot_of, z_hi, y):
     sub, width = slots.shape[1:]
     panels = jnp.take(slots, slot_of, axis=0).reshape(ZH, NY, -1, sub, width)
     panels = pick(panels, z_hi)
     got = exchange_y(lambda k: pick(panels, (y + k) % NY))
     got[0] = pick(panels, y)
     chunk = jnp.stack([choose((y - j) % NY, got) for j in range(NY)])
-    chunk = chunk.transpose(0, 2, 1, 3).reshape(NY * sub, -1)
-    z = lax.axis_index("mp") // NC % NZ
-    got = [chunk] + [lax.ppermute(chunk, "mp", flip_z(k)) for k in (1, 2, 3)]
-    return jnp.concatenate([choose(z ^ j, got) for j in range(NZ)])
-
-
-def source_blocks(strip):
-    got = {k: lax.ppermute(strip, "mp", shift_x(k)) for k in (2, 1, 3)}
-    got[0] = strip
-    blocks = []
-    for k in range(NX):
-        blocks += [got[k], lax.ppermute(got[k], "mp", SWAP_CORE)]
-    return blocks
+    return chunk.transpose(0, 2, 1, 3).reshape(NY * sub, -1)
+
+
+def gather_plane(block):
+    return lax.all_gather(block, "mp", axis=0, tiled=True, axis_index_groups=PLANE_GROUPS)
+
+
+def both_cores(half):
+    return [half, lax.ppermute(half, "mp", SWAP_CORE)]
 
 
 def mixed_strips(tokens, row_growth, z_hi, mp_index):
@@ -280,14 +284,15 @@
     slots = panel_slots(saved_panels, y)
     terms = grad_terms(place, tokens, cotangent.T)
     mixed = mixed_strips(tokens, row_growth, z_hi, mp_index)
-    mixed_all = lax.all_gather(mixed, "mp", axis=0, tiled=True)
-    mixed_all = mixed_all.reshape(NX * NZ, NC, NY, -1, mixed.shape[1])
-
-    strip = panel_strip(after(slots, terms), slot_of, z_hi, y)
-    part = sum_y(terms)
-    source = source_blocks(after(strip, part, mixed))
-
-    grads = sum_z(part)
+
+    half = gather_plane(panel_rows(after(slots, terms), slot_of, z_hi, y))
+    grads = sum_z(sum_y(terms))
+    half = after(half, grads, mixed)
+    source = both_cores(half)
+
+    mixed = gather_plane(after(mixed, half)).reshape(NX * NZ, NY, -1, mixed.shape[1])
+    mixed = both_cores(mixed)
+
     grad = pick(grads, z_hi).T
     grads = gather_y(grads.astype(BF))
     back = back_block(place, row_growth, grads)
@@ -297,13 +302,13 @@
     backs = gather_y(pair)
     grad_col = col_grad(place, source, backs)
 
-    inners = inner_terms(place, col_growth, after(source, grads))
+    inners = inner_terms(place, col_growth, source)
     inners = sum_z(after(sum_y(inners), pair)).astype(BF)
     keep, give = row_terms(place, pick(inners, z_hi), grads)
     keep = keep + lax.ppermute(give, "mp", SWAP_CORE).astype(F32)
     keep = lax.all_to_all(keep.astype(BF), "mp", 0, 0, axis_index_groups=PLANE_GROUPS)
     grad_row = keep.astype(F32).sum(axis=0)
-    grown_out = grown_output(place, mixed_all, gather_y(after(inners, backs))).T
+    grown_out = grown_output(place, mixed, gather_y(after(inners, backs))).T
     return (grown_out, grad, grad_row, grad_col)
 
 

time: 280 us -> 302 us (1.079)
  waiting for transfers between devices: 106 us -> 154 us
  starting transfers between devices: 96.4 us -> 63.2 us
    all_gather x1 -> x2, waiting for transfers between devices: 0.02 us -> 56.8 us  [gather_plane(): lax.all_gather(block, 'mp', axis=0, tiled=True, axis_index_groups=PLANE_G...]
    ppermute x2, waiting for transfers between devices: 13.9 us -> 43.5 us  [sum_z(): return part + lax.ppermute(part.astype(BF), 'dp', SWAP_ZH).astype(F32)]
    ppermute x21, waiting for transfers between devices: 65.7 us -> 40.8 us  [exchange_y(): got = {k: lax.ppermute(block_for(k), 'dp', shift_y(k)) for k in (2, 1, 3)}]
    ppermute x10 -> x2, starting transfers between devices: 21.6 us -> 0.28 us  [both_cores(): return [half, lax.ppermute(half, 'mp', SWAP_CORE)]]
    ppermute x10 -> x2, waiting for transfers between devices: 18 us -> 0.01 us  [both_cores(): return [half, lax.ppermute(half, 'mp', SWAP_CORE)]]
    ppermute x21, starting transfers between devices: 19 us -> 30.4 us  [exchange_y(): got = {k: lax.ppermute(block_for(k), 'dp', shift_y(k)) for k in (2, 1, 3)}]
    ppermute x2, starting transfers between devices: 15.6 us -> 4.57 us  [sum_z(): return part + lax.ppermute(part.astype(BF), 'dp', SWAP_ZH).astype(F32)]
    ppermute x1, waiting for transfers between devices: 3.56 us -> 11.2 us  [shards(): other = lax.ppermute(back, 'dp', SWAP_ZH)]
  transfers between devices with their start and end apart: 39 -> 32, of which waited for: 18 -> 15; matrix products, arithmetic and copies ran while one was open for 6% -> 7% of each run, Pallas kernels for 6% -> 6%
where the time goes in v2:
time: 302 us; the launch traced here: 298 us
  waiting for transfers between devices  154 us (51%)
  starting transfers between devices  63.2 us (21%)
  local copies, waits for them, and re-layouts  25.1 us (8%)
  Pallas kernels  22.8 us (8%)
  between operations  14.5 us (5%)
  other arithmetic  13.3 us (4%)
  matrix products  4.85 us (2%)
    all_gather x2, waiting for transfers between devices, gather_plane(): lax.all_gather(block, 'mp', axis=0, tiled=True, axis_index_groups=PLANE_G...  56.8 us
    ppermute x2, waiting for transfers between devices, sum_z(): return part + lax.ppermute(part.astype(BF), 'dp', SWAP_ZH).astype(F32)  43.5 us
    ppermute x21, waiting for transfers between devices, exchange_y(): got = {k: lax.ppermute(block_for(k), 'dp', shift_y(k)) for k in (2, 1, 3)}  40.8 us
    ppermute x21, starting transfers between devices, exchange_y(): got = {k: lax.ppermute(block_for(k), 'dp', shift_y(k)) for k in (2, 1, 3)}  30.4 us
    pallas_call x6, Pallas kernels, call(): pl.pallas_call(body, out_shape=outs, grid=grid or (), in_specs=[pl.BlockS...  22.8 us
    unnamed x66, local copies, waits for them, and re-layouts  20.5 us
    ppermute x1, waiting for transfers between devices, shards(): other = lax.ppermute(back, 'dp', SWAP_ZH)  11.2 us
    all_to_all x1, starting transfers between devices, shards(): lax.all_to_all(keep.astype(BF), 'mp', 0, 0, axis_index_groups=PLANE_GROUPS)  10.8 us
  transfers between devices with their start and end apart: 32, of which 15 were waited for; matrix products, arithmetic and copies ran while one was open for 7% of the time, Pallas kernels for 6%

profile of v2, /device:TPU:30, one launch (start us, length us, event | category | flops | bytes accessed | tf_op | source)
XLA Modules:
  0.0 298.2 jit_solution(12173804222004584951)
XLA Ops:
  9.1 9.1 %all-to-all-start = ((bf16[32,16,256]{2,1,0:T(8,128)(2,1)}), bf16[32,16,256]{2,1,0:T(8,128)(2,1)}, u32[]{:S(2)}, u32[]{:S(2)}) async-start(bf16[32,16,256]{2,1,0:T(8,128)(2,1)} %bitcast.10), calls=%async_computation | async-start | bytes 524288 | tf_op jit(solution)/shard_map/all_to_all | solution.py:246
  21.1 4.6 %shard_map.93 = (f32[2,320,320]{2,1,0:T(8,128)S(1)}, bf16[2,320,320]{2,1,0:T(8,128)(2,1)S(1)}, bf16[2,320,320]{2,1,0:T(8,128)(2,1)S(1)}, bf16[2,320,320]{2,1,0:T(8,128)(2,1)S(1)}) custom-call(s32[4]{0:T(128)S(1)} %pad_add_fusion.place, bf16[1024,2560]{1,0:T(8,128)(2,1)S(1)} %copy-done.1, bf16[320,1024]{1,0:T(8,128)(2,1)S(1)} %bitcast.83), custom_call_target="tpu_custom_call" | custom-call | flops 1677721600 | bytes 7946240 | tf_op jit(solution)/shard_map/pallas_call | solution.py:41
  37.8 3.0 %collective-permute-done.6 = bf16[4,16,256]{2,1,0:T(8,128)(2,1)S(1)} collective-permute-done((bf16[4,16,256]{2,1,0:T(8,128)(2,1)S(1)}, bf16[4,16,256]{2,1,0:T(8,128)(2,1)S(1)}, u32[]{:S(2)}, u32[]{:S(2)}) %collective-permute-start.6) | collective-permute-done | bytes 32800 | tf_op jit(solution)/shard_map/ppermute | solution.py:224
  45.0 4.5 %collective-permute-start = (bf16[16,2560]{1,0:T(8,128)(2,1)S(1)}, bf16[16,2560]{1,0:T(8,128)(2,1)}, u32[]{:S(2)}, u32[]{:S(2)}) collective-permute-start(bf16[16,2560]{1,0:T(8,128)(2,1)S(1)} %dynamic-slice_bitcast_fusion.2), channel_id=1, source_target_pairs={{0,128},{32,160},{64,192},{96,224},{128,0},{160,32},{192,64},{224,... | collective-permute-start | bytes 245768 | tf_op jit(solution)/shard_map/ppermute | solution.py:271
  56.7 7.2 %collective-permute-done.7 = bf16[2,320,320]{2,1,0:T(8,128)(2,1)} collective-permute-done((bf16[2,320,320]{2,1,0:T(8,128)(2,1)}, bf16[2,320,320]{2,1,0:T(8,128)(2,1)}, u32[]{:S(2)}, u32[]{:S(2)}) %collective-permute-start.7) | collective-permute-done | bytes 409632 | tf_op jit(solution)/shard_map/ppermute | solution.py:224
  63.9 6.3 %collective-permute-start.3 = (bf16[16,2560]{1,0:T(8,128)(2,1)S(1)}, bf16[16,2560]{1,0:T(8,128)(2,1)S(1)}, u32[]{:S(2)}, u32[]{:S(2)}) collective-permute-start(bf16[16,2560]{1,0:T(8,128)(2,1)S(1)} %broadcast_select_fusion.1), channel_id=1, source_target_pairs={{0,96},{32,0},{64,32},{96,64},{128,224},{160,128},{192,160},{224,1... | collective-permute-start | bytes 245768 | tf_op jit(solution)/shard_map/ppermute | solution.py:224
  70.2 3.9 %collective-permute-done.9 = bf16[2,320,320]{2,1,0:T(8,128)(2,1)} collective-permute-done((bf16[2,320,320]{2,1,0:T(8,128)(2,1)}, bf16[2,320,320]{2,1,0:T(8,128)(2,1)}, u32[]{:S(2)}, u32[]{:S(2)}) %collective-permute-start.9) | collective-permute-done | bytes 409632 | tf_op jit(solution)/shard_map/ppermute | solution.py:224
  77.9 4.8 %convolution_convert_fusion = bf16[64,1024]{1,0:T(8,128)(2,1)} fusion(bf16[1024,2560]{1,0:T(8,128)(2,1)} %tokens.1, bf16[16,2560]{1,0:T(8,128)(2,1)S(1)} %collective-permute-done.3, bf16[16,2560]{1,0:T(8,128)(2,1)S(1)} %collective-permute-done.2, bf16[16,2560]{1,0:T(8,128)(2,1)S(1)} %collective-permute-done.1, bf16[16,2560]{1,0:T(8,128)(2,1)S(1)} %broadcast_select_fusion.1), kind=kOutput, calls=%fused_computation.3 | convolution fusion | flops 336920576 | bytes 5701632 | tf_op jit(solution)/shard_map/dot_general | solution.py:24
  82.7 25.9 %collective-permute-done.10 = bf16[2,320,320]{2,1,0:T(8,128)(2,1)S(1)} collective-permute-done((bf16[2,320,320]{2,1,0:T(8,128)(2,1)}, bf16[2,320,320]{2,1,0:T(8,128)(2,1)S(1)}, u32[]{:S(2)}, u32[]{:S(2)}) %collective-permute-start.10) | collective-permute-done | bytes 409632 | tf_op jit(solution)/shard_map/ppermute | solution.py:234
  108.6 2.9 fusion.21
  111.5 24.7 %all-gather.3.cloned.1.call-done.mine = bf16[1024,1024]{1,0:T(8,128)(2,1)} async-done(((bf16[64,1024]{1,0:T(8,128)(2,1)}), bf16[1024,1024]{1,0:T(8,128)(2,1)}) %all-gather.3.cloned.1.call-update) | async-done | bytes 2097168 | tf_op jit(solution)/shard_map/all_gather | solution.py:260
  137.6 3.7 %collective-permute-start.17 = (bf16[2,320,320]{2,1,0:T(8,128)(2,1)S(1)}, bf16[2,320,320]{2,1,0:T(8,128)(2,1)S(1)}, u32[]{:S(2)}, u32[]{:S(2)}) collective-permute-start(bf16[2,320,320]{2,1,0:T(8,128)(2,1)S(1)} %get-tuple-element.42.refs_0_), channel_id=1, source_target_pairs={{0,64},{32,96},{64,0},{96,32},{128,192},{160,224},{192,128},{224,1... | collective-permute-start | bytes 1228808 | tf_op jit(solution)/shard_map/ppermute | solution.py:224
  145.3 5.8 %shard_map.94 = (f32[2,320,256]{2,1,0:T(8,128)S(1)}, bf16[2,320,256]{2,1,0:T(8,128)(2,1)}, bf16[2,320,256]{2,1,0:T(8,128)(2,1)}, bf16[2,320,256]{2,1,0:T(8,128)(2,1)S(1)}) custom-call(s32[4]{0:T(128)S(1)} %pad_add_fusion.place, bf16[320,1024]{1,0:T(8,128)(2,1)S(1)} %copy-done.25, bf16[1024,1024]{1,0:T(8,128)(2,1)S(1)} %copy-done.5, ...), custom_call_target="tpu_custom_call" | custom-call | flops 1342177280 | bytes 6488064 | tf_op jit(solution)/shard_map/pallas_call | solution.py:41
  155.4 8.5 %collective-permute-done.18.refs_3_ = bf16[2,320,320]{2,1,0:T(8,128)(2,1)S(1)} collective-permute-done((bf16[2,320,320]{2,1,0:T(8,128)(2,1)S(1)}, bf16[2,320,320]{2,1,0:T(8,128)(2,1)S(1)}, u32[]{:S(2)}, u32[]{:S(2)}) %collective-permute-start.18) | collective-permute-done | bytes 409632 | tf_op jit(solution)/shard_map/ppermute | solution.py:224
  165.3 3.4 %collective-permute-start.19 = (bf16[320,256]{1,0:T(8,128)(2,1)S(1)}, bf16[320,256]{1,0:T(8,128)(2,1)S(1)}, u32[]{:S(2)}, u32[]{:S(2)}) collective-permute-start(bf16[320,256]{1,0:T(8,128)(2,1)S(1)} %shard_map.95), channel_id=1, source_target_pairs={{0,128},{32,160},{64,192},{96,224},{128,0},{160,32},{192,64},{224,... | collective-permute-start | bytes 491528 | tf_op jit(solution)/shard_map/ppermute | solution.py:300
  168.7 11.2 %collective-permute-done.19 = bf16[320,256]{1,0:T(8,128)(2,1)S(1)} collective-permute-done((bf16[320,256]{1,0:T(8,128)(2,1)S(1)}, bf16[320,256]{1,0:T(8,128)(2,1)S(1)}, u32[]{:S(2)}, u32[]{:S(2)}) %collective-permute-start.19) | collective-permute-done | bytes 163872 | tf_op jit(solution)/shard_map/ppermute | solution.py:300
  182.3 3.1 %collective-permute-start.20 = (bf16[2,320,256]{2,1,0:T(8,128)(2,1)S(1)}, bf16[2,320,256]{2,1,0:T(8,128)(2,1)S(1)}, u32[]{:S(2)}, u32[]{:S(2)}) collective-permute-start(bf16[2,320,256]{2,1,0:T(8,128)(2,1)S(1)} %convert_element_type.58), channel_id=1, source_target_pairs={{0,128},{32,160},{64,192},{96,224},{128,0},{160,32},{192,64},{224,... | collective-permute-start | bytes 983048 | tf_op jit(solution)/shard_map/ppermute | solution.py:234
  185.4 17.6 %collective-permute-done.20 = bf16[2,320,256]{2,1,0:T(8,128)(2,1)S(1)} collective-permute-done((bf16[2,320,256]{2,1,0:T(8,128)(2,1)S(1)}, bf16[2,320,256]{2,1,0:T(8,128)(2,1)S(1)}, u32[]{:S(2)}, u32[]{:S(2)}) %collective-permute-start.20) | collective-permute-done | bytes 327712 | tf_op jit(solution)/shard_map/ppermute | solution.py:234
  205.5 32.2 %all-gather.5.cloned.1.call-done = bf16[1024,1024]{1,0:T(8,128)(2,1)} async-done(((bf16[64,1024]{1,0:T(8,128)(2,1)}), bf16[1024,1024]{1,0:T(8,128)(2,1)}) %all-gather.5.cloned.1.call-update) | async-done | bytes 2097168 | tf_op jit(solution)/shard_map/all_gather | solution.py:260
  238.6 10.8 %all-to-all-start.1 = ((bf16[16,80,256]{2,1,0:T(8,128)(2,1)}), bf16[16,80,256]{2,1,0:T(8,128)(2,1)}, u32[]{:S(2)}, u32[]{:S(2)}) async-start(bf16[16,80,256]{2,1,0:T(8,128)(2,1)} %add_convert_fusion), calls=%async_computation.1 | async-start | bytes 1310720 | tf_op jit(solution)/shard_map/all_to_all | solution.py:309
  252.4 7.8 %collective-permute-done.21.refs_1_ = bf16[2,320,256]{2,1,0:T(8,128)(2,1)S(1)} collective-permute-done((bf16[2,320,256]{2,1,0:T(8,128)(2,1)S(1)}, bf16[2,320,256]{2,1,0:T(8,128)(2,1)S(1)}, u32[]{:S(2)}, u32[]{:S(2)}) %collective-permute-start.21) | collective-permute-done | bytes 327712 | tf_op jit(solution)/shard_map/ppermute | solution.py:224
  262.5 5.6 %collective-permute-done.23.refs_3_ = bf16[2,320,256]{2,1,0:T(8,128)(2,1)S(1)} collective-permute-done((bf16[2,320,256]{2,1,0:T(8,128)(2,1)S(1)}, bf16[2,320,256]{2,1,0:T(8,128)(2,1)S(1)}, u32[]{:S(2)}, u32[]{:S(2)}) %collective-permute-start.23) | collective-permute-done | bytes 327712 | tf_op jit(solution)/shard_map/ppermute | solution.py:224
  280.5 3.9 %shard_map.98 = f32[320,1024]{1,0:T(8,128)} custom-call(s32[4]{0:T(128)S(1)} %pad_add_fusion.place, bf16[1024,1024]{1,0:T(8,128)(2,1)S(1)} %copy-done.6, bf16[1024,1024]{1,0:T(8,128)(2,1)S(1)} %copy-done.8, bf16[2,320,256]{2,1,0:T(8,128)(2,1)S(1)} %copy-done.16, bf16[2,320,256]{2,1,0:T(8,128)(2,1)S(1)} %copy-done.19, bf16[2,320,256]{2,1,0:T(8,128)(2,1)S(1)} %copy-done.21, ...), custom_call_target="tpu_custom_call" | custom-call | flops 1342177280 | bytes 6815744 | tf_op jit(solution)/shard_map/pallas_call | solution.py:41
  286.4 4.9 %shard_map.96 = bf16[320,1024]{1,0:T(8,128)(2,1)} custom-call(s32[4]{0:T(128)S(1)} %pad_add_fusion.place, bf16[16,4,16,1024]{3,2,1,0:T(8,128)(2,1)S(1)} %bitcast.81, bf16[16,4,16,1024]{3,2,1,0:T(8,128)(2,1)} %collective-permute-done.11.other, bf16[2,320,256]{2,1,0:T(8,128)(2,1)S(1)} %add_convert_fusion.1.refs_0_, ...), custom_call_target="tpu_custom_call" | custom-call | flops 1342177280 | bytes 6160384 | tf_op jit(solution)/shard_map/pallas_call | solution.py:41
  (138 shorter events, 68.2 us)
Async XLA Ops:
  9.1 18.9 %all-to-all-start = ((bf16[32,16,256]{2,1,0:T(8,128)(2,1)}), bf16[32,16,256]{2,1,0:T(8,128)(2,1)}, u32[]{:S(2)}, u32[]{:S(2)}) async-start(bf16[32,16,256]{2,1,0:T(8,128)(2,1)} %bitcast.10), calls=%async_computation | async-start | bytes 524288 | tf_op jit(solution)/shard_map/all_to_all | solution.py:246
  18.2 117.9 %all-gather.3.cloned.1.call-start = ((), (), s32[]{:S(2)}) async-start(), calls=%async_computation.2 | async-start | bytes 2228224 | tf_op jit(solution)/shard_map/all_gather | solution.py:260
  42.4 195.2 %all-gather.5.cloned.1.call-start = ((), (), s32[]{:S(2)}) async-start(), calls=%async_computation.3 | async-start | bytes 2228224 | tf_op jit(solution)/shard_map/all_gather | solution.py:260
  49.5 14.5 %collective-permute-start.7 = (bf16[2,320,320]{2,1,0:T(8,128)(2,1)}, bf16[2,320,320]{2,1,0:T(8,128)(2,1)}, u32[]{:S(2)}, u32[]{:S(2)}) collective-permute-start(bf16[2,320,320]{2,1,0:T(8,128)(2,1)} %copy-done.28), channel_id=1, source_target_pairs={{0,32},{32,64},{64,96},{96,0},{128,160},{160,192},{192,224},{224,1... | collective-permute-start | bytes 1228808 | tf_op jit(solution)/shard_map/ppermute | solution.py:224
  49.5 20.7 %collective-permute-start.8 = (bf16[2,320,320]{2,1,0:T(8,128)(2,1)}, bf16[2,320,320]{2,1,0:T(8,128)(2,1)}, u32[]{:S(2)}, u32[]{:S(2)}) collective-permute-start(bf16[2,320,320]{2,1,0:T(8,128)(2,1)} %copy-done.27), channel_id=1, source_target_pairs={{0,64},{32,96},{64,0},{96,32},{128,192},{160,224},{192,128},{224,1... | collective-permute-start | bytes 1228808 | tf_op jit(solution)/shard_map/ppermute | solution.py:224
  50.3 23.8 %collective-permute-start.9 = (bf16[2,320,320]{2,1,0:T(8,128)(2,1)}, bf16[2,320,320]{2,1,0:T(8,128)(2,1)}, u32[]{:S(2)}, u32[]{:S(2)}) collective-permute-start(bf16[2,320,320]{2,1,0:T(8,128)(2,1)} %copy-done.26), channel_id=1, source_target_pairs={{0,96},{32,0},{64,32},{96,64},{128,224},{160,128},{192,160},{224,1... | collective-permute-start | bytes 1228808 | tf_op jit(solution)/shard_map/ppermute | solution.py:224
  54.4 23.4 %collective-permute-start.1 = (bf16[16,2560]{1,0:T(8,128)(2,1)S(1)}, bf16[16,2560]{1,0:T(8,128)(2,1)S(1)}, u32[]{:S(2)}, u32[]{:S(2)}) collective-permute-start(bf16[16,2560]{1,0:T(8,128)(2,1)S(1)} %broadcast_select_fusion.1), channel_id=1, source_target_pairs={{0,32},{32,64},{64,96},{96,0},{128,160},{160,192},{192,224},{224,1... | collective-permute-start | bytes 245768 | tf_op jit(solution)/shard_map/ppermute | solution.py:224
  55.2 22.7 %collective-permute-start.2 = (bf16[16,2560]{1,0:T(8,128)(2,1)S(1)}, bf16[16,2560]{1,0:T(8,128)(2,1)S(1)}, u32[]{:S(2)}, u32[]{:S(2)}) collective-permute-start(bf16[16,2560]{1,0:T(8,128)(2,1)S(1)} %broadcast_select_fusion.1), channel_id=1, source_target_pairs={{0,64},{32,96},{64,0},{96,32},{128,192},{160,224},{192,128},{224,1... | collective-permute-start | bytes 245768 | tf_op jit(solution)/shard_map/ppermute | solution.py:224
  76.4 32.2 %collective-permute-start.10 = (bf16[2,320,320]{2,1,0:T(8,128)(2,1)}, bf16[2,320,320]{2,1,0:T(8,128)(2,1)S(1)}, u32[]{:S(2)}, u32[]{:S(2)}) collective-permute-start(bf16[2,320,320]{2,1,0:T(8,128)(2,1)} %fusion.7), channel_id=1, source_target_pairs={{0,128},{32,160},{64,192},{96,224},{128,0},{160,32},{192,64},{224,... | collective-permute-start | bytes 1228808 | tf_op jit(solution)/shard_map/ppermute | solution.py:234
  136.5 17.5 %collective-permute-start.16 = (bf16[2,320,320]{2,1,0:T(8,128)(2,1)S(1)}, bf16[2,320,320]{2,1,0:T(8,128)(2,1)S(1)}, u32[]{:S(2)}, u32[]{:S(2)}) collective-permute-start(bf16[2,320,320]{2,1,0:T(8,128)(2,1)S(1)} %get-tuple-element.42.refs_0_), channel_id=1, source_target_pairs={{0,32},{32,64},{64,96},{96,0},{128,160},{160,192},{192,224},{224,1... | collective-permute-start | bytes 1228808 | tf_op jit(solution)/shard_map/ppermute | solution.py:224
  137.6 17.8 %collective-permute-start.17 = (bf16[2,320,320]{2,1,0:T(8,128)(2,1)S(1)}, bf16[2,320,320]{2,1,0:T(8,128)(2,1)S(1)}, u32[]{:S(2)}, u32[]{:S(2)}) collective-permute-start(bf16[2,320,320]{2,1,0:T(8,128)(2,1)S(1)} %get-tuple-element.42.refs_0_), channel_id=1, source_target_pairs={{0,64},{32,96},{64,0},{96,32},{128,192},{160,224},{192,128},{224,1... | collective-permute-start | bytes 1228808 | tf_op jit(solution)/shard_map/ppermute | solution.py:224
  141.3 22.6 %collective-permute-start.18 = (bf16[2,320,320]{2,1,0:T(8,128)(2,1)S(1)}, bf16[2,320,320]{2,1,0:T(8,128)(2,1)S(1)}, u32[]{:S(2)}, u32[]{:S(2)}) collective-permute-start(bf16[2,320,320]{2,1,0:T(8,128)(2,1)S(1)} %get-tuple-element.42.refs_0_), channel_id=1, source_target_pairs={{0,96},{32,0},{64,32},{96,64},{128,224},{160,128},{192,160},{224,1... | collective-permute-start | bytes 1228808 | tf_op jit(solution)/shard_map/ppermute | solution.py:224
  151.1 29.6 %collective-permute-start.13 = (bf16[2,320,256]{2,1,0:T(8,128)(2,1)}, bf16[2,320,256]{2,1,0:T(8,128)(2,1)}, u32[]{:S(2)}, u32[]{:S(2)}) collective-permute-start(bf16[2,320,256]{2,1,0:T(8,128)(2,1)} %get-tuple-element.27), channel_id=1, source_target_pairs={{0,32},{32,64},{64,96},{96,0},{128,160},{160,192},{192,224},{224,1... | collective-permute-start | bytes 983048 | tf_op jit(solution)/shard_map/ppermute | solution.py:224
  153.0 27.7 %collective-permute-start.14 = (bf16[2,320,256]{2,1,0:T(8,128)(2,1)}, bf16[2,320,256]{2,1,0:T(8,128)(2,1)}, u32[]{:S(2)}, u32[]{:S(2)}) collective-permute-start(bf16[2,320,256]{2,1,0:T(8,128)(2,1)} %get-tuple-element.28), channel_id=1, source_target_pairs={{0,64},{32,96},{64,0},{96,32},{128,192},{160,224},{192,128},{224,1... | collective-permute-start | bytes 983048 | tf_op jit(solution)/shard_map/ppermute | solution.py:224
  154.0 26.7 %collective-permute-start.15 = (bf16[2,320,256]{2,1,0:T(8,128)(2,1)S(1)}, bf16[2,320,256]{2,1,0:T(8,128)(2,1)}, u32[]{:S(2)}, u32[]{:S(2)}) collective-permute-start(bf16[2,320,256]{2,1,0:T(8,128)(2,1)S(1)} %get-tuple-element.29), channel_id=1, source_target_pairs={{0,96},{32,0},{64,32},{96,64},{128,224},{160,128},{192,160},{224,1... | collective-permute-start | bytes 983048 | tf_op jit(solution)/shard_map/ppermute | solution.py:224
  165.3 14.6 %collective-permute-start.19 = (bf16[320,256]{1,0:T(8,128)(2,1)S(1)}, bf16[320,256]{1,0:T(8,128)(2,1)S(1)}, u32[]{:S(2)}, u32[]{:S(2)}) collective-permute-start(bf16[320,256]{1,0:T(8,128)(2,1)S(1)} %shard_map.95), channel_id=1, source_target_pairs={{0,128},{32,160},{64,192},{96,224},{128,0},{160,32},{192,64},{224,... | collective-permute-start | bytes 491528 | tf_op jit(solution)/shard_map/ppermute | solution.py:300
  182.3 20.8 %collective-permute-start.20 = (bf16[2,320,256]{2,1,0:T(8,128)(2,1)S(1)}, bf16[2,320,256]{2,1,0:T(8,128)(2,1)S(1)}, u32[]{:S(2)}, u32[]{:S(2)}) collective-permute-start(bf16[2,320,256]{2,1,0:T(8,128)(2,1)S(1)} %convert_element_type.58), channel_id=1, source_target_pairs={{0,128},{32,160},{64,192},{96,224},{128,0},{160,32},{192,64},{224,... | collective-permute-start | bytes 983048 | tf_op jit(solution)/shard_map/ppermute | solution.py:234
  205.4 32.2 %collective-permute-start.27 = (bf16[16,80,256]{2,1,0:T(8,128)(2,1)}, bf16[16,80,256]{2,1,0:T(8,128)(2,1)S(1)}, u32[]{:S(2)}, u32[]{:S(2)}) collective-permute-start(bf16[16,80,256]{2,1,0:T(8,128)(2,1)} %get-tuple-element.33), channel_id=1, source_target_pairs={{0,1},{1,0},{2,3},{3,2},{4,5},{5,4},{6,7},{7,6},{8,9},{9,8},{10,11... | collective-permute-start | bytes 1966088 | tf_op jit(solution)/shard_map/ppermute | solution.py:308
  237.6 48.8 %collective-permute-start.11 = (bf16[16,4,16,1024]{3,2,1,0:T(8,128)(2,1)}, bf16[16,4,16,1024]{3,2,1,0:T(8,128)(2,1)}, u32[]{:S(2)}, u32[]{:S(2)}) collective-permute-start(bf16[16,4,16,1024]{3,2,1,0:T(8,128)(2,1)} %bitcast.80), channel_id=1, source_target_pairs={{0,1},{1,0},{2,3},{3,2},{4,5},{5,4},{6,7},{7,6},{8,9},{9,8},{10,11... | collective-permute-start | bytes 6291464 | tf_op jit(solution)/shard_map/ppermute | solution.py:264
  238.6 45.7 %all-to-all-start.1 = ((bf16[16,80,256]{2,1,0:T(8,128)(2,1)}), bf16[16,80,256]{2,1,0:T(8,128)(2,1)}, u32[]{:S(2)}, u32[]{:S(2)}) async-start(bf16[16,80,256]{2,1,0:T(8,128)(2,1)} %add_convert_fusion), calls=%async_computation.1 | async-start | bytes 1310720 | tf_op jit(solution)/shard_map/all_to_all | solution.py:309
  252.3 15.8 %collective-permute-start.23 = (bf16[2,320,256]{2,1,0:T(8,128)(2,1)S(1)}, bf16[2,320,256]{2,1,0:T(8,128)(2,1)S(1)}, u32[]{:S(2)}, u32[]{:S(2)}) collective-permute-start(bf16[2,320,256]{2,1,0:T(8,128)(2,1)S(1)} %copy-done.15), channel_id=1, source_target_pairs={{0,96},{32,0},{64,32},{96,64},{128,224},{160,128},{192,160},{224,1... | collective-permute-start | bytes 983048 | tf_op jit(solution)/shard_map/ppermute | solution.py:224
  268.1 18.0 %collective-permute-start.24 = (bf16[2,320,256]{2,1,0:T(8,128)(2,1)S(1)}, bf16[2,320,256]{2,1,0:T(8,128)(2,1)}, u32[]{:S(2)}, u32[]{:S(2)}) collective-permute-start(bf16[2,320,256]{2,1,0:T(8,128)(2,1)S(1)} %add_convert_fusion.1.refs_0_), channel_id=1, source_target_pairs={{0,32},{32,64},{64,96},{96,0},{128,160},{160,192},{192,224},{224,1... | collective-permute-start | bytes 983048 | tf_op jit(solution)/shard_map/ppermute | solution.py:224
  268.9 17.3 %collective-permute-start.25 = (bf16[2,320,256]{2,1,0:T(8,128)(2,1)S(1)}, bf16[2,320,256]{2,1,0:T(8,128)(2,1)}, u32[]{:S(2)}, u32[]{:S(2)}) collective-permute-start(bf16[2,320,256]{2,1,0:T(8,128)(2,1)S(1)} %add_convert_fusion.1.refs_0_), channel_id=1, source_target_pairs={{0,64},{32,96},{64,0},{96,32},{128,192},{160,224},{192,128},{224,1... | collective-permute-start | bytes 983048 | tf_op jit(solution)/shard_map/ppermute | solution.py:224
  270.8 15.6 %collective-permute-start.26 = (bf16[2,320,256]{2,1,0:T(8,128)(2,1)S(1)}, bf16[2,320,256]{2,1,0:T(8,128)(2,1)}, u32[]{:S(2)}, u32[]{:S(2)}) collective-permute-start(bf16[2,320,256]{2,1,0:T(8,128)(2,1)S(1)} %add_convert_fusion.1.refs_0_), channel_id=1, source_target_pairs={{0,96},{32,0},{64,32},{96,64},{128,224},{160,128},{192,160},{224,1... | collective-permute-start | bytes 983048 | tf_op jit(solution)/shard_map/ppermute | solution.py:224
  (39 other events, 314.7 us)
Sparse Core Ops, SparseCore 0:
  42.5 93.5 all-gather.2
  138.0 99.6 all-gather.4

commit v3 on v2

--- a/solution.py
+++ b/solution.py
@@ -10,6 +10,8 @@
 NX, NZ, NC = 4, 4, 2
 MP = NX * NZ * NC
 PLANE_GROUPS = [[(x * NZ + z) * NC + c for x in range(NX) for z in range(NZ)] for c in range(NC)]
+X_GROUPS = [[(x * NZ + z) * NC + c for x in range(NX)] for z in range(NZ) for c in range(NC)]
+Z_GROUPS = [[(x * NZ + z) * NC + c for z in range(NZ)] for x in range(NX) for c in range(NC)]
 SWAP_ZH = [(i, (i + NY) % (ZH * NY)) for i in range(ZH * NY)]
 SWAP_CORE = [(m, m ^ 1) for m in range(MP)]
 BF, F32 = jnp.bfloat16, jnp.float32
@@ -35,17 +37,17 @@
     return out
 
 
-def call(body, place, arrays, outs, flops, scratch=(), grid=None, in_specs=None, out_specs=None):
+def call(body, place, arrays, outs, flops, scratch=(), limit=40, **specs):
     size = lambda s: s.size * s.dtype.itemsize
     whole = pl.BlockSpec(memory_space=pltpu.VMEM)
     return pl.pallas_call(
         body,
         out_shape=outs,
-        grid=grid or (),
-        in_specs=[pl.BlockSpec(memory_space=pltpu.SMEM)] + (in_specs or [whole] * len(arrays)),
-        out_specs=out_specs or jax.tree.map(lambda _: whole, outs),
+        grid=specs.get("grid", ()),
+        in_specs=[pl.BlockSpec(memory_space=pltpu.SMEM)] + specs.get("in_specs", [whole] * len(arrays)),
+        out_specs=specs.get("out_specs", jax.tree.map(lambda _: whole, outs)),
         scratch_shapes=list(scratch),
-        compiler_params=pltpu.CompilerParams(vmem_limit_bytes=40 * 2**20),
+        compiler_params=pltpu.CompilerParams(vmem_limit_bytes=limit * 2**20),
         cost_estimate=pl.CostEstimate(
             flops=flops,
             bytes_accessed=sum(map(size, arrays)) + sum(map(size, jax.tree.leaves(outs))),
@@ -164,6 +166,7 @@
         col_body, place, (*source, *back), struct((hidden, width), F32),
         4 * source[0].size * hidden,
         scratch=[pltpu.VMEM((NY, *back[0].shape), BF)],
+        limit=56,
         grid=(NY,),
         in_specs=[stream(rows, width)] * 2 + [keep_whole(back[0].shape)] * NY,
         out_specs=keep_whole((hidden, width)),
@@ -210,6 +213,7 @@
     return call(
         out_body, place, (*mixed, *inner), struct((hidden, count), BF),
         4 * mixed[0].size * hidden,
+        limit=56,
         grid=(count // part,),
         in_specs=[rows] * 2 + [keep_whole(inner[0].shape)] * NY,
         out_specs=pl.BlockSpec((hidden, part), lambda s: (0, s)),
@@ -256,18 +260,20 @@
     return chunk.transpose(0, 2, 1, 3).reshape(NY * sub, -1)
 
 
-def gather_plane(block):
-    return lax.all_gather(block, "mp", axis=0, tiled=True, axis_index_groups=PLANE_GROUPS)
+def gather(block, groups):
+    blocks = jnp.broadcast_to(block[None], (len(groups[0]), *block.shape))
+    return lax.all_to_all(blocks, "mp", 0, 0, axis_index_groups=groups).reshape(-1, *block.shape[1:])
 
 
 def both_cores(half):
     return [half, lax.ppermute(half, "mp", SWAP_CORE)]
 
 
-def mixed_strips(tokens, row_growth, z_hi, mp_index):
+def mixed_strips(tokens, row_growth, z_hi, mp_index, *done):
     old = row_growth.shape[1]
     strip = old // (NX * NZ)
     mine = pick(row_growth.T.reshape(NX * NZ, strip, -1), mp_index // NC)
+    mine = after(mine, *done)
     other = lax.ppermute(mine, "dp", SWAP_ZH)
     mine = jnp.where(z_hi == mp_index % NC, mine, other)
     strips = jnp.concatenate(gather_y(mine))
@@ -283,32 +289,35 @@
 
     slots = panel_slots(saved_panels, y)
     terms = grad_terms(place, tokens, cotangent.T)
-    mixed = mixed_strips(tokens, row_growth, z_hi, mp_index)
-
-    half = gather_plane(panel_rows(after(slots, terms), slot_of, z_hi, y))
-    grads = sum_z(sum_y(terms))
-    half = after(half, grads, mixed)
+    rows = panel_rows(after(slots, terms), slot_of, z_hi, y)
+    terms = after(terms, rows)
+    half = gather(gather(rows, Z_GROUPS), X_GROUPS)
     source = both_cores(half)
 
-    mixed = gather_plane(after(mixed, half)).reshape(NX * NZ, NY, -1, mixed.shape[1])
-    mixed = both_cores(mixed)
-
+    part = sum_y(terms)
+    grads = sum_z(part)
+    mixed = mixed_strips(tokens, row_growth, z_hi, mp_index, part)
     grad = pick(grads, z_hi).T
     grads = gather_y(grads.astype(BF))
     back = back_block(place, row_growth, grads)
-
     other = lax.ppermute(back, "dp", SWAP_ZH)
     pair = jnp.where(z_hi == 0, jnp.stack([back, other]), jnp.stack([other, back]))
+
+    mixed = gather(after(mixed, half), Z_GROUPS)
+    inners = inner_terms(place, col_growth, source)
+    part = after(sum_y(inners), pair, mixed)
+    mixed = gather(mixed, X_GROUPS).reshape(NX * NZ, NY, -1, mixed.shape[1])
+    mixed = both_cores(mixed)
+    inners = sum_z(part).astype(BF)
     backs = gather_y(pair)
     grad_col = col_grad(place, source, backs)
 
-    inners = inner_terms(place, col_growth, source)
-    inners = sum_z(after(sum_y(inners), pair)).astype(BF)
     keep, give = row_terms(place, pick(inners, z_hi), grads)
     keep = keep + lax.ppermute(give, "mp", SWAP_CORE).astype(F32)
     keep = lax.all_to_all(keep.astype(BF), "mp", 0, 0, axis_index_groups=PLANE_GROUPS)
     grad_row = keep.astype(F32).sum(axis=0)
-    grown_out = grown_output(place, mixed, gather_y(after(inners, backs))).T
+    inners = gather_y(after(inners, backs, mixed))
+    grown_out = grown_output(place, after(mixed, grad_col, grad_row), inners).T
     return (grown_out, grad, grad_row, grad_col)
 
 

time: 302 us -> 280 us (0.927)
  waiting for transfers between devices: 154 us -> 119 us
  blocking collectives: 0 us -> 16.4 us
  starting transfers between devices: 63.2 us -> 77.5 us
  between operations: 14.5 us -> 1.13 us
  local copies, waits for them, and re-layouts: 25.1 us -> 21.1 us
    all_gather x2 -> x0, waiting for transfers between devices: 56.8 us -> none  [gather_plane(): lax.all_gather(block, 'mp', axis=0, tiled=True, axis_index_groups=PLANE_G...]
    ppermute x2, waiting for transfers between devices: 43.5 us -> 13.7 us  [sum_z(): return part + lax.ppermute(part.astype(BF), 'dp', SWAP_ZH).astype(F32)]
    all_to_all x0 -> x3, waiting for transfers between devices: none -> 28.4 us  [gather(): lax.all_to_all(blocks, 'mp', 0, 0, axis_index_groups=groups)]
    ppermute x21, waiting for transfers between devices: 40.8 us -> 57.7 us  [exchange_y(): got = {k: lax.ppermute(block_for(k), 'dp', shift_y(k)) for k in (2, 1, 3)}]
    all_to_all x0 -> x1, blocking collectives: none -> 16.4 us  [gather(): lax.all_to_all(blocks, 'mp', 0, 0, axis_index_groups=groups)]
    all_to_all x0 -> x3, starting transfers between devices: none -> 14.9 us  [gather(): lax.all_to_all(blocks, 'mp', 0, 0, axis_index_groups=groups)]
    all_to_all x1, waiting for transfers between devices: 0.01 us -> 7.9 us  [panel_slots(): return lax.all_to_all(mine, 'mp', 0, 0)]
    ppermute x1, waiting for transfers between devices: 11.2 us -> 3.3 us  [shards(): other = lax.ppermute(back, 'dp', SWAP_ZH)]
  transfers between devices with their start and end apart: 32 -> 33, of which waited for: 15 -> 18; matrix products, arithmetic and copies ran while one was open for 7% -> 9% of each run, Pallas kernels for 6% -> 7%
where the time goes in v3:
time: 280 us; the launch traced here: 276 us
  waiting for transfers between devices  119 us (42%)
  starting transfers between devices  77.5 us (28%)
  Pallas kernels  25.7 us (9%)
  local copies, waits for them, and re-layouts  21.1 us (8%)
  blocking collectives  16.4 us (6%)
  other arithmetic  11.8 us (4%)
  matrix products  4.17 us (1%)
    ppermute x21, waiting for transfers between devices, exchange_y(): got = {k: lax.ppermute(block_for(k), 'dp', shift_y(k)) for k in (2, 1, 3)}  57.7 us
    all_to_all x3, waiting for transfers between devices, gather(): lax.all_to_all(blocks, 'mp', 0, 0, axis_index_groups=groups)  28.4 us
    pallas_call x6, Pallas kernels, call(): pl.pallas_call(body, out_shape=outs, grid=specs.get('grid', ()), in_specs...  25.7 us
    ppermute x21, starting transfers between devices, exchange_y(): got = {k: lax.ppermute(block_for(k), 'dp', shift_y(k)) for k in (2, 1, 3)}  24.7 us
    all_to_all x1, blocking collectives, gather(): lax.all_to_all(blocks, 'mp', 0, 0, axis_index_groups=groups)  16.4 us
    all_to_all x3, starting transfers between devices, gather(): lax.all_to_all(blocks, 'mp', 0, 0, axis_index_groups=groups)  14.9 us
    ppermute x2, waiting for transfers between devices, sum_z(): return part + lax.ppermute(part.astype(BF), 'dp', SWAP_ZH).astype(F32)  13.7 us
    unnamed x60, local copies, waits for them, and re-layouts  13.4 us
  transfers between devices with their start and end apart: 33, of which 18 were waited for; matrix products, arithmetic and copies ran while one was open for 9% of the time, Pallas kernels for 7%

profile of v3, /device:TPU:30, one launch (start us, length us, event | category | flops | bytes accessed | tf_op | source)
XLA Modules:
  0.0 276.4 jit_solution(9718143136473112648)
XLA Ops:
  2.6 9.0 %all-to-all-start = ((bf16[32,16,256]{2,1,0:T(8,128)(2,1)}), bf16[32,16,256]{2,1,0:T(8,128)(2,1)S(1)}, u32[]{:S(2)}, u32[]{:S(2)}) async-start(bf16[32,16,256]{2,1,0:T(8,128)(2,1)} %bitcast.11), calls=%async_computation | async-start | bytes 524288 | tf_op jit(solution)/shard_map/all_to_all | solution.py:250
  12.6 7.9 %all-to-all-done = bf16[32,16,256]{2,1,0:T(8,128)(2,1)S(1)} async-done(((bf16[32,16,256]{2,1,0:T(8,128)(2,1)}), bf16[32,16,256]{2,1,0:T(8,128)(2,1)S(1)}, u32[]{:S(2)}, u32[]{:S(2)}) %all-to-all-start) | async-done | bytes 262176 | tf_op jit(solution)/shard_map/all_to_all | solution.py:250
  30.2 16.4 %all_to_all.30 = bf16[4,64,1024]{2,1,0:T(8,128)(2,1)S(1)} all-to-all(bf16[4,64,1024]{2,1,0:T(8,128)(2,1)S(1)} %broadcast_in_dim.43), channel_id=1, replica_groups={{0,2,4,6},{1,3,5,7},{8,10,12,14},{9,11,13,15},{16,18,20,22},{17,19,21,2..., dimensions={0} | all-to-all | bytes 1048576 | tf_op jit(solution)/shard_map/all_to_all | solution.py:265
  48.2 5.9 %all-to-all-start.2 = ((bf16[4,256,1024]{2,1,0:T(8,128)(2,1)}), bf16[4,256,1024]{2,1,0:T(8,128)(2,1)S(1)}, u32[]{:S(2)}, u32[]{:S(2)}) async-start(bf16[4,256,1024]{2,1,0:T(8,128)(2,1)} %broadcast_in_dim.45), calls=%async_computation.2 | async-start | bytes 4194304 | tf_op jit(solution)/shard_map/all_to_all | solution.py:265
  57.8 5.7 %shard_map.93 = (f32[2,320,320]{2,1,0:T(8,128)S(1)}, bf16[2,320,320]{2,1,0:T(8,128)(2,1)}, bf16[2,320,320]{2,1,0:T(8,128)(2,1)}, bf16[2,320,320]{2,1,0:T(8,128)(2,1)}) custom-call(s32[4]{0:T(128)S(1)} %pad_add_fusion.place, bf16[1024,2560]{1,0:T(8,128)(2,1)S(1)} %copy-done.2, bf16[320,1024]{1,0:T(8,128)(2,1)S(1)} %bitcast.85), custom_call_target="tpu_custom_call" | custom-call | flops 1677721600 | bytes 7946240 | tf_op jit(solution)/shard_map/pallas_call | solution.py:43
  69.8 9.1 %collective-permute-done = bf16[2,320,320]{2,1,0:T(8,128)(2,1)} collective-permute-done((bf16[2,320,320]{2,1,0:T(8,128)(2,1)}, bf16[2,320,320]{2,1,0:T(8,128)(2,1)}, u32[]{:S(2)}, u32[]{:S(2)}) %collective-permute-start) | collective-permute-done | bytes 409632 | tf_op jit(solution)/shard_map/ppermute | solution.py:228
  81.1 8.0 %collective-permute-done.2 = bf16[2,320,320]{2,1,0:T(8,128)(2,1)} collective-permute-done((bf16[2,320,320]{2,1,0:T(8,128)(2,1)}, bf16[2,320,320]{2,1,0:T(8,128)(2,1)}, u32[]{:S(2)}, u32[]{:S(2)}) %collective-permute-start.2) | collective-permute-done | bytes 409632 | tf_op jit(solution)/shard_map/ppermute | solution.py:228
  92.1 4.5 %collective-permute-start.3 = (bf16[16,2560]{1,0:T(8,128)(2,1)S(1)}, bf16[16,2560]{1,0:T(8,128)(2,1)S(1)}, u32[]{:S(2)}, u32[]{:S(2)}) collective-permute-start(bf16[16,2560]{1,0:T(8,128)(2,1)S(1)} %dynamic-slice_bitcast_fusion.2), channel_id=1, source_target_pairs={{0,128},{32,160},{64,192},{96,224},{128,0},{160,32},{192,64},{224,... | collective-permute-start | bytes 245768 | tf_op jit(solution)/shard_map/ppermute | solution.py:277
  96.6 5.6 %collective-permute-done.3 = bf16[16,2560]{1,0:T(8,128)(2,1)S(1)} collective-permute-done((bf16[16,2560]{1,0:T(8,128)(2,1)S(1)}, bf16[16,2560]{1,0:T(8,128)(2,1)S(1)}, u32[]{:S(2)}, u32[]{:S(2)}) %collective-permute-start.3) | collective-permute-done | bytes 81952 | tf_op jit(solution)/shard_map/ppermute | solution.py:277
  109.7 4.2 %convolution_convert_fusion = bf16[64,1024]{1,0:T(8,128)(2,1)S(1)} fusion(bf16[1024,2560]{1,0:T(8,128)(2,1)} %tokens.1, bf16[16,2560]{1,0:T(8,128)(2,1)S(1)} %collective-permute-done.6, bf16[16,2560]{1,0:T(8,128)(2,1)S(1)} %collective-permute-done.5, bf16[16,2560]{1,0:T(8,128)(2,1)S(1)} %collective-permute-done.4, ...), kind=kOutput, calls=%fused_computation.3 | convolution fusion | flops 336920576 | bytes 5701632 | tf_op jit(solution)/shard_map/dot_general | solution.py:26
  114.7 4.1 %all-to-all-start.3 = ((bf16[4,64,1024]{2,1,0:T(8,128)(2,1)}), bf16[4,64,1024]{2,1,0:T(8,128)(2,1)}, u32[]{:S(2)}, u32[]{:S(2)}) async-start(bf16[4,64,1024]{2,1,0:T(8,128)(2,1)} %broadcast_in_dim.46), calls=%async_computation.3 | async-start | bytes 1048576 | tf_op jit(solution)/shard_map/all_to_all | solution.py:265
  122.3 28.4 %all-to-all-done.3 = bf16[4,64,1024]{2,1,0:T(8,128)(2,1)} async-done(((bf16[4,64,1024]{2,1,0:T(8,128)(2,1)}), bf16[4,64,1024]{2,1,0:T(8,128)(2,1)}, u32[]{:S(2)}, u32[]{:S(2)}) %all-to-all-start.3) | async-done | bytes 524320 | tf_op jit(solution)/shard_map/all_to_all | solution.py:265
  153.3 4.8 %all-to-all-start.4 = ((bf16[4,256,1024]{2,1,0:T(8,128)(2,1)}), bf16[4,256,1024]{2,1,0:T(8,128)(2,1)}, u32[]{:S(2)}, u32[]{:S(2)}) async-start(bf16[4,256,1024]{2,1,0:T(8,128)(2,1)} %broadcast_in_dim.48), calls=%async_computation.4 | async-start | bytes 4194304 | tf_op jit(solution)/shard_map/all_to_all | solution.py:265
  164.5 6.3 %shard_map.96 = (f32[2,320,256]{2,1,0:T(8,128)S(1)}, bf16[2,320,256]{2,1,0:T(8,128)(2,1)}, bf16[2,320,256]{2,1,0:T(8,128)(2,1)}, bf16[2,320,256]{2,1,0:T(8,128)(2,1)S(1)}) custom-call(s32[4]{0:T(128)S(1)} %pad_add_fusion.place, bf16[320,1024]{1,0:T(8,128)(2,1)S(1)} %copy-done.16, bf16[1024,1024]{1,0:T(8,128)(2,1)S(1)} %bitcast.82, ...), custom_call_target="tpu_custom_call" | custom-call | flops 1342177280 | bytes 6488064 | tf_op jit(solution)/shard_map/pallas_call | solution.py:43
  174.8 6.0 %collective-permute-done.15.refs_3_ = bf16[2,320,320]{2,1,0:T(8,128)(2,1)S(1)} collective-permute-done((bf16[2,320,320]{2,1,0:T(8,128)(2,1)S(1)}, bf16[2,320,320]{2,1,0:T(8,128)(2,1)S(1)}, u32[]{:S(2)}, u32[]{:S(2)}) %collective-permute-start.15) | collective-permute-done | bytes 409632 | tf_op jit(solution)/shard_map/ppermute | solution.py:228
  185.3 10.0 %collective-permute-start.16 = (bf16[320,256]{1,0:T(8,128)(2,1)S(1)}, bf16[320,256]{1,0:T(8,128)(2,1)S(1)}, u32[]{:S(2)}, u32[]{:S(2)}) collective-permute-start(bf16[320,256]{1,0:T(8,128)(2,1)S(1)} %shard_map.94), channel_id=1, source_target_pairs={{0,128},{32,160},{64,192},{96,224},{128,0},{160,32},{192,64},{224,... | collective-permute-start | bytes 491528 | tf_op jit(solution)/shard_map/ppermute | solution.py:303
  203.5 6.0 %collective-permute-start.23 = (bf16[2,320,256]{2,1,0:T(8,128)(2,1)S(1)}, bf16[2,320,256]{2,1,0:T(8,128)(2,1)}, u32[]{:S(2)}, u32[]{:S(2)}) collective-permute-start(bf16[2,320,256]{2,1,0:T(8,128)(2,1)S(1)} %convert_element_type.58), channel_id=1, source_target_pairs={{0,128},{32,160},{64,192},{96,224},{128,0},{160,32},{192,64},{224,... | collective-permute-start | bytes 983048 | tf_op jit(solution)/shard_map/ppermute | solution.py:238
  209.5 13.7 %collective-permute-done.23 = bf16[2,320,256]{2,1,0:T(8,128)(2,1)} collective-permute-done((bf16[2,320,256]{2,1,0:T(8,128)(2,1)S(1)}, bf16[2,320,256]{2,1,0:T(8,128)(2,1)}, u32[]{:S(2)}, u32[]{:S(2)}) %collective-permute-start.23) | collective-permute-done | bytes 327712 | tf_op jit(solution)/shard_map/ppermute | solution.py:238
  229.2 4.8 %all-to-all-start.5 = ((bf16[16,80,256]{2,1,0:T(8,128)(2,1)}), bf16[16,80,256]{2,1,0:T(8,128)(2,1)S(1)}, u32[]{:S(2)}, u32[]{:S(2)}) async-start(bf16[16,80,256]{2,1,0:T(8,128)(2,1)} %add_convert_fusion), calls=%async_computation.5 | async-start | bytes 1310720 | tf_op jit(solution)/shard_map/all_to_all | solution.py:317
  238.6 6.3 %collective-permute-done.19.refs_3_ = bf16[2,320,256]{2,1,0:T(8,128)(2,1)S(1)} collective-permute-done((bf16[2,320,256]{2,1,0:T(8,128)(2,1)S(1)}, bf16[2,320,256]{2,1,0:T(8,128)(2,1)S(1)}, u32[]{:S(2)}, u32[]{:S(2)}) %collective-permute-start.19) | collective-permute-done | bytes 327712 | tf_op jit(solution)/shard_map/ppermute | solution.py:228
  244.8 7.9 %collective-permute-done.18.refs_2_ = bf16[2,320,256]{2,1,0:T(8,128)(2,1)S(1)} collective-permute-done((bf16[2,320,256]{2,1,0:T(8,128)(2,1)S(1)}, bf16[2,320,256]{2,1,0:T(8,128)(2,1)S(1)}, u32[]{:S(2)}, u32[]{:S(2)}) %collective-permute-start.18) | collective-permute-done | bytes 327712 | tf_op jit(solution)/shard_map/ppermute | solution.py:228
  259.3 5.7 %shard_map.95 = f32[320,1024]{1,0:T(8,128)} custom-call(s32[4]{0:T(128)} %copy-done.14, bf16[1024,1024]{1,0:T(8,128)(2,1)} %bitcast.83, bf16[1024,1024]{1,0:T(8,128)(2,1)} %collective-permute-done.11.other, bf16[2,320,256]{2,1,0:T(8,128)(2,1)} %maximum_select_fusion.refs_0_, bf16[2,320,256]{2,1,0:T(8,128)(2,1)} %copy-done.27, ...), custom_call_target="tpu_custom_call" | custom-call | flops 1342177280 | bytes 6815744 | tf_op jit(solution)/shard_map/pallas_call | solution.py:43
  265.7 5.4 %collective-permute-done.26.refs_2_ = bf16[2,320,256]{2,1,0:T(8,128)(2,1)} collective-permute-done((bf16[2,320,256]{2,1,0:T(8,128)(2,1)S(1)}, bf16[2,320,256]{2,1,0:T(8,128)(2,1)}, u32[]{:S(2)}, u32[]{:S(2)}) %collective-permute-start.26) | collective-permute-done | bytes 327712 | tf_op jit(solution)/shard_map/ppermute | solution.py:228
  271.1 5.3 %shard_map.98 = bf16[320,1024]{1,0:T(8,128)(2,1)} custom-call(s32[4]{0:T(128)} %copy-done.14, bf16[16,4,16,1024]{3,2,1,0:T(8,128)(2,1)} %bitcast.26.mine, bf16[16,4,16,1024]{3,2,1,0:T(8,128)(2,1)} %collective-permute-done.10.other, bf16[2,320,256]{2,1,0:T(8,128)(2,1)} %copy-done.19, bf16[2,320,256]{2,1,0:T(8,128)(2,1)} %collective-permute-done.25.refs_1_, ...), custom_call_target="tpu_custom_call" | custom-call | flops 1342177280 | bytes 6160384 | tf_op jit(solution)/shard_map/pallas_call | solution.py:43
  (137 shorter events, 84.3 us)
Async XLA Ops:
  2.6 17.9 %all-to-all-start = ((bf16[32,16,256]{2,1,0:T(8,128)(2,1)}), bf16[32,16,256]{2,1,0:T(8,128)(2,1)S(1)}, u32[]{:S(2)}, u32[]{:S(2)}) async-start(bf16[32,16,256]{2,1,0:T(8,128)(2,1)} %bitcast.11), calls=%async_computation | async-start | bytes 524288 | tf_op jit(solution)/shard_map/all_to_all | solution.py:250
  48.2 48.4 %all-to-all-start.2 = ((bf16[4,256,1024]{2,1,0:T(8,128)(2,1)}), bf16[4,256,1024]{2,1,0:T(8,128)(2,1)S(1)}, u32[]{:S(2)}, u32[]{:S(2)}) async-start(bf16[4,256,1024]{2,1,0:T(8,128)(2,1)} %broadcast_in_dim.45), calls=%async_computation.2 | async-start | bytes 4194304 | tf_op jit(solution)/shard_map/all_to_all | solution.py:265
  64.4 14.5 %collective-permute-start = (bf16[2,320,320]{2,1,0:T(8,128)(2,1)}, bf16[2,320,320]{2,1,0:T(8,128)(2,1)}, u32[]{:S(2)}, u32[]{:S(2)}) collective-permute-start(bf16[2,320,320]{2,1,0:T(8,128)(2,1)} %get-tuple-element.21), channel_id=1, source_target_pairs={{0,32},{32,64},{64,96},{96,0},{128,160},{160,192},{192,224},{224,1... | collective-permute-start | bytes 1228808 | tf_op jit(solution)/shard_map/ppermute | solution.py:228
  65.2 16.0 %collective-permute-start.1 = (bf16[2,320,320]{2,1,0:T(8,128)(2,1)}, bf16[2,320,320]{2,1,0:T(8,128)(2,1)}, u32[]{:S(2)}, u32[]{:S(2)}) collective-permute-start(bf16[2,320,320]{2,1,0:T(8,128)(2,1)} %get-tuple-element.22), channel_id=1, source_target_pairs={{0,64},{32,96},{64,0},{96,32},{128,192},{160,224},{192,128},{224,1... | collective-permute-start | bytes 1228808 | tf_op jit(solution)/shard_map/ppermute | solution.py:228
  66.0 23.2 %collective-permute-start.2 = (bf16[2,320,320]{2,1,0:T(8,128)(2,1)}, bf16[2,320,320]{2,1,0:T(8,128)(2,1)}, u32[]{:S(2)}, u32[]{:S(2)}) collective-permute-start(bf16[2,320,320]{2,1,0:T(8,128)(2,1)} %get-tuple-element.23), channel_id=1, source_target_pairs={{0,96},{32,0},{64,32},{96,64},{128,224},{160,128},{192,160},{224,1... | collective-permute-start | bytes 1228808 | tf_op jit(solution)/shard_map/ppermute | solution.py:228
  96.6 67.9 %collective-permute-start.11 = (bf16[1024,1024]{1,0:T(8,128)(2,1)S(1)}, bf16[1024,1024]{1,0:T(8,128)(2,1)}, u32[]{:S(2)}, u32[]{:S(2)}) collective-permute-start(bf16[1024,1024]{1,0:T(8,128)(2,1)S(1)} %bitcast.81), channel_id=1, source_target_pairs={{0,1},{1,0},{2,3},{3,2},{4,5},{5,4},{6,7},{7,6},{8,9},{9,8},{10,11... | collective-permute-start | bytes 6291464 | tf_op jit(solution)/shard_map/ppermute | solution.py:269
  114.7 35.9 %all-to-all-start.3 = ((bf16[4,64,1024]{2,1,0:T(8,128)(2,1)}), bf16[4,64,1024]{2,1,0:T(8,128)(2,1)}, u32[]{:S(2)}, u32[]{:S(2)}) async-start(bf16[4,64,1024]{2,1,0:T(8,128)(2,1)} %broadcast_in_dim.46), calls=%async_computation.3 | async-start | bytes 1048576 | tf_op jit(solution)/shard_map/all_to_all | solution.py:265
  118.9 39.3 %collective-permute-start.12 = (bf16[2,320,320]{2,1,0:T(8,128)(2,1)}, bf16[2,320,320]{2,1,0:T(8,128)(2,1)}, u32[]{:S(2)}, u32[]{:S(2)}) collective-permute-start(bf16[2,320,320]{2,1,0:T(8,128)(2,1)} %get-tuple-element.50), channel_id=1, source_target_pairs={{0,128},{32,160},{64,192},{96,224},{128,0},{160,32},{192,64},{224,... | collective-permute-start | bytes 1228808 | tf_op jit(solution)/shard_map/ppermute | solution.py:238
  153.3 56.2 %all-to-all-start.4 = ((bf16[4,256,1024]{2,1,0:T(8,128)(2,1)}), bf16[4,256,1024]{2,1,0:T(8,128)(2,1)}, u32[]{:S(2)}, u32[]{:S(2)}) async-start(bf16[4,256,1024]{2,1,0:T(8,128)(2,1)} %broadcast_in_dim.48), calls=%async_computation.4 | async-start | bytes 4194304 | tf_op jit(solution)/shard_map/all_to_all | solution.py:265
  160.6 20.2 %collective-permute-start.15 = (bf16[2,320,320]{2,1,0:T(8,128)(2,1)S(1)}, bf16[2,320,320]{2,1,0:T(8,128)(2,1)S(1)}, u32[]{:S(2)}, u32[]{:S(2)}) collective-permute-start(bf16[2,320,320]{2,1,0:T(8,128)(2,1)S(1)} %get-tuple-element.48.refs_0_), channel_id=1, source_target_pairs={{0,96},{32,0},{64,32},{96,64},{128,224},{160,128},{192,160},{224,1... | collective-permute-start | bytes 1228808 | tf_op jit(solution)/shard_map/ppermute | solution.py:228
  161.7 22.2 %collective-permute-start.14 = (bf16[2,320,320]{2,1,0:T(8,128)(2,1)S(1)}, bf16[2,320,320]{2,1,0:T(8,128)(2,1)S(1)}, u32[]{:S(2)}, u32[]{:S(2)}) collective-permute-start(bf16[2,320,320]{2,1,0:T(8,128)(2,1)S(1)} %get-tuple-element.48.refs_0_), channel_id=1, source_target_pairs={{0,64},{32,96},{64,0},{96,32},{128,192},{160,224},{192,128},{224,1... | collective-permute-start | bytes 1228808 | tf_op jit(solution)/shard_map/ppermute | solution.py:228
  164.4 19.5 %collective-permute-start.13 = (bf16[2,320,320]{2,1,0:T(8,128)(2,1)S(1)}, bf16[2,320,320]{2,1,0:T(8,128)(2,1)S(1)}, u32[]{:S(2)}, u32[]{:S(2)}) collective-permute-start(bf16[2,320,320]{2,1,0:T(8,128)(2,1)S(1)} %get-tuple-element.48.refs_0_), channel_id=1, source_target_pairs={{0,32},{32,64},{64,96},{96,0},{128,160},{160,192},{192,224},{224,1... | collective-permute-start | bytes 1228808 | tf_op jit(solution)/shard_map/ppermute | solution.py:228
  170.8 28.7 %collective-permute-start.20 = (bf16[2,320,256]{2,1,0:T(8,128)(2,1)}, bf16[2,320,256]{2,1,0:T(8,128)(2,1)S(1)}, u32[]{:S(2)}, u32[]{:S(2)}) collective-permute-start(bf16[2,320,256]{2,1,0:T(8,128)(2,1)} %get-tuple-element.27), channel_id=1, source_target_pairs={{0,32},{32,64},{64,96},{96,0},{128,160},{160,192},{192,224},{224,1... | collective-permute-start | bytes 983048 | tf_op jit(solution)/shard_map/ppermute | solution.py:228
  172.1 27.3 %collective-permute-start.21 = (bf16[2,320,256]{2,1,0:T(8,128)(2,1)}, bf16[2,320,256]{2,1,0:T(8,128)(2,1)S(1)}, u32[]{:S(2)}, u32[]{:S(2)}) collective-permute-start(bf16[2,320,256]{2,1,0:T(8,128)(2,1)} %get-tuple-element.28), channel_id=1, source_target_pairs={{0,64},{32,96},{64,0},{96,32},{128,192},{160,224},{192,128},{224,1... | collective-permute-start | bytes 983048 | tf_op jit(solution)/shard_map/ppermute | solution.py:228
  180.7 18.7 %collective-permute-start.22 = (bf16[2,320,256]{2,1,0:T(8,128)(2,1)S(1)}, bf16[2,320,256]{2,1,0:T(8,128)(2,1)S(1)}, u32[]{:S(2)}, u32[]{:S(2)}) collective-permute-start(bf16[2,320,256]{2,1,0:T(8,128)(2,1)S(1)} %get-tuple-element.29), channel_id=1, source_target_pairs={{0,96},{32,0},{64,32},{96,64},{128,224},{160,128},{192,160},{224,1... | collective-permute-start | bytes 983048 | tf_op jit(solution)/shard_map/ppermute | solution.py:228
  185.3 13.3 %collective-permute-start.16 = (bf16[320,256]{1,0:T(8,128)(2,1)S(1)}, bf16[320,256]{1,0:T(8,128)(2,1)S(1)}, u32[]{:S(2)}, u32[]{:S(2)}) collective-permute-start(bf16[320,256]{1,0:T(8,128)(2,1)S(1)} %shard_map.94), channel_id=1, source_target_pairs={{0,128},{32,160},{64,192},{96,224},{128,0},{160,32},{192,64},{224,... | collective-permute-start | bytes 491528 | tf_op jit(solution)/shard_map/ppermute | solution.py:303
  203.5 19.7 %collective-permute-start.23 = (bf16[2,320,256]{2,1,0:T(8,128)(2,1)S(1)}, bf16[2,320,256]{2,1,0:T(8,128)(2,1)}, u32[]{:S(2)}, u32[]{:S(2)}) collective-permute-start(bf16[2,320,256]{2,1,0:T(8,128)(2,1)S(1)} %convert_element_type.58), channel_id=1, source_target_pairs={{0,128},{32,160},{64,192},{96,224},{128,0},{160,32},{192,64},{224,... | collective-permute-start | bytes 983048 | tf_op jit(solution)/shard_map/ppermute | solution.py:238
  209.5 43.2 %collective-permute-start.10 = (bf16[16,4,16,1024]{3,2,1,0:T(8,128)(2,1)}, bf16[16,4,16,1024]{3,2,1,0:T(8,128)(2,1)}, u32[]{:S(2)}, u32[]{:S(2)}) collective-permute-start(bf16[16,4,16,1024]{3,2,1,0:T(8,128)(2,1)} %bitcast.26.mine), channel_id=1, source_target_pairs={{0,1},{1,0},{2,3},{3,2},{4,5},{5,4},{6,7},{7,6},{8,9},{9,8},{10,11... | collective-permute-start | bytes 6291464 | tf_op jit(solution)/shard_map/ppermute | solution.py:269
  229.2 35.8 %all-to-all-start.5 = ((bf16[16,80,256]{2,1,0:T(8,128)(2,1)}), bf16[16,80,256]{2,1,0:T(8,128)(2,1)S(1)}, u32[]{:S(2)}, u32[]{:S(2)}) async-start(bf16[16,80,256]{2,1,0:T(8,128)(2,1)} %add_convert_fusion), calls=%async_computation.5 | async-start | bytes 1310720 | tf_op jit(solution)/shard_map/all_to_all | solution.py:317
  234.7 18.1 %collective-permute-start.18 = (bf16[2,320,256]{2,1,0:T(8,128)(2,1)S(1)}, bf16[2,320,256]{2,1,0:T(8,128)(2,1)S(1)}, u32[]{:S(2)}, u32[]{:S(2)}) collective-permute-start(bf16[2,320,256]{2,1,0:T(8,128)(2,1)S(1)} %copy-done.20), channel_id=1, source_target_pairs={{0,64},{32,96},{64,0},{96,32},{128,192},{160,224},{192,128},{224,1... | collective-permute-start | bytes 983048 | tf_op jit(solution)/shard_map/ppermute | solution.py:228
  238.6 14.2 %collective-permute-start.17 = (bf16[2,320,256]{2,1,0:T(8,128)(2,1)S(1)}, bf16[2,320,256]{2,1,0:T(8,128)(2,1)S(1)}, u32[]{:S(2)}, u32[]{:S(2)}) collective-permute-start(bf16[2,320,256]{2,1,0:T(8,128)(2,1)S(1)} %copy-done.20), channel_id=1, source_target_pairs={{0,32},{32,64},{64,96},{96,0},{128,160},{160,192},{192,224},{224,1... | collective-permute-start | bytes 983048 | tf_op jit(solution)/shard_map/ppermute | solution.py:228
  252.8 12.9 %collective-permute-start.27 = (bf16[2,320,256]{2,1,0:T(8,128)(2,1)S(1)}, bf16[2,320,256]{2,1,0:T(8,128)(2,1)S(1)}, u32[]{:S(2)}, u32[]{:S(2)}) collective-permute-start(bf16[2,320,256]{2,1,0:T(8,128)(2,1)S(1)} %add_convert_fusion.1.refs_0_), channel_id=1, source_target_pairs={{0,96},{32,0},{64,32},{96,64},{128,224},{160,128},{192,160},{224,1... | collective-permute-start | bytes 983048 | tf_op jit(solution)/shard_map/ppermute | solution.py:228
  253.1 18.0 %collective-permute-start.26 = (bf16[2,320,256]{2,1,0:T(8,128)(2,1)S(1)}, bf16[2,320,256]{2,1,0:T(8,128)(2,1)}, u32[]{:S(2)}, u32[]{:S(2)}) collective-permute-start(bf16[2,320,256]{2,1,0:T(8,128)(2,1)S(1)} %add_convert_fusion.1.refs_0_), channel_id=1, source_target_pairs={{0,64},{32,96},{64,0},{96,32},{128,192},{160,224},{192,128},{224,1... | collective-permute-start | bytes 983048 | tf_op jit(solution)/shard_map/ppermute | solution.py:228
  256.4 14.7 %collective-permute-start.25 = (bf16[2,320,256]{2,1,0:T(8,128)(2,1)S(1)}, bf16[2,320,256]{2,1,0:T(8,128)(2,1)}, u32[]{:S(2)}, u32[]{:S(2)}) collective-permute-start(bf16[2,320,256]{2,1,0:T(8,128)(2,1)S(1)} %add_convert_fusion.1.refs_0_), channel_id=1, source_target_pairs={{0,32},{32,64},{64,96},{96,0},{128,160},{160,192},{192,224},{224,1... | collective-permute-start | bytes 983048 | tf_op jit(solution)/shard_map/ppermute | solution.py:228
  (37 other events, 569.1 us)

commit v4 on v3

--- a/solution.py
+++ b/solution.py
@@ -220,8 +220,8 @@
     )
 
 
-def after(value, *done):
-    return lax.optimization_barrier((value, done))[0]
+def together(*values):
+    return lax.optimization_barrier(values)
 
 
 def exchange_y(block_for):
@@ -269,15 +269,12 @@
     return [half, lax.ppermute(half, "mp", SWAP_CORE)]
 
 
-def mixed_strips(tokens, row_growth, z_hi, mp_index, *done):
+def own_strip(row_growth, z_hi, mp_index):
     old = row_growth.shape[1]
     strip = old // (NX * NZ)
     mine = pick(row_growth.T.reshape(NX * NZ, strip, -1), mp_index // NC)
-    mine = after(mine, *done)
     other = lax.ppermute(mine, "dp", SWAP_ZH)
-    mine = jnp.where(z_hi == mp_index % NC, mine, other)
-    strips = jnp.concatenate(gather_y(mine))
-    return dot(strips, tokens, NT).astype(BF)
+    return jnp.where(z_hi == mp_index % NC, mine, other)
 
 
 def shards(tokens, cotangent, saved_panels, owners, row_growth, col_growth):
@@ -289,35 +286,48 @@
 
     slots = panel_slots(saved_panels, y)
     terms = grad_terms(place, tokens, cotangent.T)
-    rows = panel_rows(after(slots, terms), slot_of, z_hi, y)
-    terms = after(terms, rows)
-    half = gather(gather(rows, Z_GROUPS), X_GROUPS)
-    source = both_cores(half)
-
+    strip = own_strip(row_growth, z_hi, mp_index)
+    slots, terms, strip = together(slots, terms, strip)
+
+    rows = panel_rows(slots, slot_of, z_hi, y)
+    strips = jnp.concatenate(gather_y(strip))
+    rows, terms, strips = together(rows, terms, strips)
+
+    mixed = dot(strips, tokens, NT).astype(BF)
+    rows = gather(rows, Z_GROUPS)
     part = sum_y(terms)
+    rows, part, mixed = together(rows, part, mixed)
+
+    half = gather(rows, X_GROUPS)
     grads = sum_z(part)
-    mixed = mixed_strips(tokens, row_growth, z_hi, mp_index, part)
+    half, grads, mixed = together(half, grads, mixed)
+
     grad = pick(grads, z_hi).T
     grads = gather_y(grads.astype(BF))
+    source = both_cores(half)
+    inners = inner_terms(place, col_growth, source)
+    mixed = gather(mixed, Z_GROUPS)
+    grads, inners, mixed = together(grads, inners, mixed)
+
     back = back_block(place, row_growth, grads)
     other = lax.ppermute(back, "dp", SWAP_ZH)
     pair = jnp.where(z_hi == 0, jnp.stack([back, other]), jnp.stack([other, back]))
-
-    mixed = gather(after(mixed, half), Z_GROUPS)
-    inners = inner_terms(place, col_growth, source)
-    part = after(sum_y(inners), pair, mixed)
     mixed = gather(mixed, X_GROUPS).reshape(NX * NZ, NY, -1, mixed.shape[1])
-    mixed = both_cores(mixed)
-    inners = sum_z(part).astype(BF)
+    part, pair = together(sum_y(inners), pair)
+
+    inners = sum_z(part)
     backs = gather_y(pair)
-    grad_col = col_grad(place, source, backs)
-
+    inners, backs, mixed = together(inners, backs, mixed)
+
+    inners = inners.astype(BF)
     keep, give = row_terms(place, pick(inners, z_hi), grads)
     keep = keep + lax.ppermute(give, "mp", SWAP_CORE).astype(F32)
     keep = lax.all_to_all(keep.astype(BF), "mp", 0, 0, axis_index_groups=PLANE_GROUPS)
     grad_row = keep.astype(F32).sum(axis=0)
-    inners = gather_y(after(inners, backs, mixed))
-    grown_out = grown_output(place, after(mixed, grad_col, grad_row), inners).T
+    grad_col = col_grad(place, source, backs)
+    inners = gather_y(inners)
+    mixed, grad_col = together(both_cores(mixed), grad_col)
+    grown_out = grown_output(place, mixed, inners).T
     return (grown_out, grad, grad_row, grad_col)
 
 

time: 280 us -> 240 us (0.86)
  waiting for transfers between devices: 119 us -> 82.6 us
  blocking collectives: 16.4 us -> 0 us
  local copies, waits for them, and re-layouts: 21.1 us -> 31.4 us
    all_to_all x3 -> x4, waiting for transfers between devices: 28.4 us -> 5.34 us  [gather(): lax.all_to_all(blocks, 'mp', 0, 0, axis_index_groups=groups)]
    ppermute x21, waiting for transfers between devices: 57.7 us -> 41 us  [exchange_y(): got = {k: lax.ppermute(block_for(k), 'dp', shift_y(k)) for k in (2, 1, 3)}]
    all_to_all x1 -> x0, blocking collectives: 16.4 us -> none  [gather(): lax.all_to_all(blocks, 'mp', 0, 0, axis_index_groups=groups)]
    ppermute x2, waiting for transfers between devices: 13.7 us -> 22.4 us  [sum_z(): return part + lax.ppermute(part.astype(BF), 'dp', SWAP_ZH).astype(F32)]
    all_to_all x3 -> x4, starting transfers between devices: 14.9 us -> 23.3 us  [gather(): lax.all_to_all(blocks, 'mp', 0, 0, axis_index_groups=groups)]
    all_to_all x1, waiting for transfers between devices: 7.9 us -> 0.01 us  [panel_slots(): return lax.all_to_all(mine, 'mp', 0, 0)]
    ppermute x1, starting transfers between devices: 10 us -> 2.45 us  [shards(): other = lax.ppermute(back, 'dp', SWAP_ZH)]
    unnamed x60 -> x76, local copies, waits for them, and re-layouts: 13.4 us -> 19.6 us
  transfers between devices with their start and end apart: 33 -> 34, of which waited for: 18 -> 14; matrix products, arithmetic and copies ran while one was open for 9% -> 9% of each run, Pallas kernels for 7% -> 7%
where the time goes in v4:
time: 240 us; the launch traced here: 236 us
  waiting for transfers between devices  82.6 us (34%)
  starting transfers between devices  79.2 us (33%)
  local copies, waits for them, and re-layouts  31.4 us (13%)
  Pallas kernels  23.7 us (10%)
  other arithmetic  13.4 us (6%)
  matrix products  4.95 us (2%)
    ppermute x21, waiting for transfers between devices, exchange_y(): got = {k: lax.ppermute(block_for(k), 'dp', shift_y(k)) for k in (2, 1, 3)}  41 us
    ppermute x21, starting transfers between devices, exchange_y(): got = {k: lax.ppermute(block_for(k), 'dp', shift_y(k)) for k in (2, 1, 3)}  26.7 us
    pallas_call x6, Pallas kernels, call(): pl.pallas_call(body, out_shape=outs, grid=specs.get('grid', ()), in_specs...  23.7 us
    all_to_all x4, starting transfers between devices, gather(): lax.all_to_all(blocks, 'mp', 0, 0, axis_index_groups=groups)  23.3 us
    ppermute x2, waiting for transfers between devices, sum_z(): return part + lax.ppermute(part.astype(BF), 'dp', SWAP_ZH).astype(F32)  22.4 us
    unnamed x76, local copies, waits for them, and re-layouts  19.6 us
    all_to_all x1, starting transfers between devices, panel_slots(): return lax.all_to_all(mine, 'mp', 0, 0)  9.09 us
    all_to_all x1, starting transfers between devices, shards(): lax.all_to_all(keep.astype(BF), 'mp', 0, 0, axis_index_groups=PLANE_GROUPS)  8.61 us
  transfers between devices with their start and end apart: 34, of which 14 were waited for; matrix products, arithmetic and copies ran while one was open for 9% of the time, Pallas kernels for 7%

profile of v4, /device:TPU:30, one launch (start us, length us, event | category | flops | bytes accessed | tf_op | source)
XLA Modules:
  0.0 236.4 jit_solution(14472754708344370090)
XLA Ops:
  2.6 9.1 %all-to-all-start = ((bf16[32,16,256]{2,1,0:T(8,128)(2,1)}), bf16[32,16,256]{2,1,0:T(8,128)(2,1)}, u32[]{:S(2)}, u32[]{:S(2)}) async-start(bf16[32,16,256]{2,1,0:T(8,128)(2,1)} %bitcast.7), calls=%async_computation | async-start | bytes 524288 | tf_op jit(solution)/shard_map/all_to_all | solution.py:250
  14.2 4.5 %collective-permute-start = (bf16[16,2560]{1,0:T(8,128)(2,1)S(1)}, bf16[16,2560]{1,0:T(8,128)(2,1)S(1)}, u32[]{:S(2)}, u32[]{:S(2)}) collective-permute-start(bf16[16,2560]{1,0:T(8,128)(2,1)S(1)} %dynamic-slice_bitcast_fusion.2), channel_id=1, source_target_pairs={{0,128},{32,160},{64,192},{96,224},{128,0},{160,32},{192,64},{224,... | collective-permute-start | bytes 245768 | tf_op jit(solution)/shard_map/ppermute | solution.py:276
  21.4 4.6 %shard_map.93 = (f32[2,320,320]{2,1,0:T(8,128)S(1)}, bf16[2,320,320]{2,1,0:T(8,128)(2,1)S(1)}, bf16[2,320,320]{2,1,0:T(8,128)(2,1)S(1)}, bf16[2,320,320]{2,1,0:T(8,128)(2,1)S(1)}) custom-call(s32[4]{0:T(128)S(1)} %pad_add_fusion.place, bf16[1024,2560]{1,0:T(8,128)(2,1)S(1)} %copy-done.2, bf16[320,1024]{1,0:T(8,128)(2,1)S(1)} %bitcast.88), custom_call_target="tpu_custom_call" | custom-call | flops 1677721600 | bytes 7946240 | tf_op jit(solution)/shard_map/pallas_call | solution.py:43
  37.9 2.7 %collective-permute-start.5 = (bf16[16,2560]{1,0:T(8,128)(2,1)}, bf16[16,2560]{1,0:T(8,128)(2,1)S(1)}, u32[]{:S(2)}, u32[]{:S(2)}) collective-permute-start(bf16[16,2560]{1,0:T(8,128)(2,1)} %broadcast_select_fusion.1), channel_id=1, source_target_pairs={{0,64},{32,96},{64,0},{96,32},{128,192},{160,224},{192,128},{224,1... | collective-permute-start | bytes 245768 | tf_op jit(solution)/shard_map/ppermute | solution.py:228
  48.1 4.6 %all-to-all-start.1 = ((bf16[4,64,1024]{2,1,0:T(8,128)(2,1)}), bf16[4,64,1024]{2,1,0:T(8,128)(2,1)}, u32[]{:S(2)}, u32[]{:S(2)}) async-start(bf16[4,64,1024]{2,1,0:T(8,128)(2,1)} %broadcast_in_dim.39), calls=%async_computation.1 | async-start | bytes 1048576 | tf_op jit(solution)/shard_map/all_to_all | solution.py:265
  52.7 3.5 %collective-permute-start.7 = (bf16[2,320,320]{2,1,0:T(8,128)(2,1)S(1)}, bf16[2,320,320]{2,1,0:T(8,128)(2,1)S(1)}, u32[]{:S(2)}, u32[]{:S(2)}) collective-permute-start(bf16[2,320,320]{2,1,0:T(8,128)(2,1)S(1)} %copy-done.22), channel_id=1, source_target_pairs={{0,32},{32,64},{64,96},{96,0},{128,160},{160,192},{192,224},{224,1... | collective-permute-start | bytes 1228808 | tf_op jit(solution)/shard_map/ppermute | solution.py:228
  57.1 5.0 %convolution_convert_fusion = bf16[64,1024]{1,0:T(8,128)(2,1)} fusion(bf16[64,2560]{1,0:T(8,128)(2,1)} %pad_maximum_fusion, bf16[1024,2560]{1,0:T(8,128)(2,1)} %tokens.1), kind=kOutput, calls=%fused_computation.3 | convolution fusion | flops 335609856 | bytes 5701632 | tf_op jit(solution)/shard_map/dot_general | solution.py:26
  62.1 13.1 %collective-permute-done.7 = bf16[2,320,320]{2,1,0:T(8,128)(2,1)S(1)} collective-permute-done((bf16[2,320,320]{2,1,0:T(8,128)(2,1)S(1)}, bf16[2,320,320]{2,1,0:T(8,128)(2,1)S(1)}, u32[]{:S(2)}, u32[]{:S(2)}) %collective-permute-start.7) | collective-permute-done | bytes 409632 | tf_op jit(solution)/shard_map/ppermute | solution.py:228
  75.2 3.4 %collective-permute-done.9 = bf16[2,320,320]{2,1,0:T(8,128)(2,1)S(1)} collective-permute-done((bf16[2,320,320]{2,1,0:T(8,128)(2,1)S(1)}, bf16[2,320,320]{2,1,0:T(8,128)(2,1)S(1)}, u32[]{:S(2)}, u32[]{:S(2)}) %collective-permute-start.9) | collective-permute-done | bytes 409632 | tf_op jit(solution)/shard_map/ppermute | solution.py:228
  82.4 4.7 %all-to-all-start.2 = ((bf16[4,256,1024]{2,1,0:T(8,128)(2,1)}), bf16[4,256,1024]{2,1,0:T(8,128)(2,1)S(1)}, u32[]{:S(2)}, u32[]{:S(2)}) async-start(bf16[4,256,1024]{2,1,0:T(8,128)(2,1)} %broadcast_in_dim.40), calls=%async_computation.2 | async-start | bytes 4194304 | tf_op jit(solution)/shard_map/all_to_all | solution.py:265
  90.0 14.8 %collective-permute-done.10 = bf16[2,320,320]{2,1,0:T(8,128)(2,1)S(1)} collective-permute-done((bf16[2,320,320]{2,1,0:T(8,128)(2,1)S(1)}, bf16[2,320,320]{2,1,0:T(8,128)(2,1)S(1)}, u32[]{:S(2)}, u32[]{:S(2)}) %collective-permute-start.10) | collective-permute-done | bytes 409632 | tf_op jit(solution)/shard_map/ppermute | solution.py:238
  105.9 5.3 %all-to-all-done.2 = bf16[4,256,1024]{2,1,0:T(8,128)(2,1)S(1)} async-done(((bf16[4,256,1024]{2,1,0:T(8,128)(2,1)}), bf16[4,256,1024]{2,1,0:T(8,128)(2,1)S(1)}, u32[]{:S(2)}, u32[]{:S(2)}) %all-to-all-start.2) | async-done | bytes 2097184 | tf_op jit(solution)/shard_map/all_to_all | solution.py:265
  112.1 9.1 %all-to-all-start.3 = ((bf16[4,64,1024]{2,1,0:T(8,128)(2,1)}), bf16[4,64,1024]{2,1,0:T(8,128)(2,1)}, u32[]{:S(2)}, u32[]{:S(2)}) async-start(bf16[4,64,1024]{2,1,0:T(8,128)(2,1)} %broadcast_in_dim.41), calls=%async_computation.3 | async-start | bytes 1048576 | tf_op jit(solution)/shard_map/all_to_all | solution.py:265
  127.2 5.4 %shard_map.94 = (f32[2,320,256]{2,1,0:T(8,128)S(1)}, bf16[2,320,256]{2,1,0:T(8,128)(2,1)S(1)}, bf16[2,320,256]{2,1,0:T(8,128)(2,1)S(1)}, bf16[2,320,256]{2,1,0:T(8,128)(2,1)S(1)}) custom-call(s32[4]{0:T(128)S(1)} %pad_add_fusion.place, bf16[320,1024]{1,0:T(8,128)(2,1)S(1)} %copy-done.18, bf16[1024,1024]{1,0:T(8,128)(2,1)S(1)} %bitcast.85, ...), custom_call_target="tpu_custom_call" | custom-call | flops 1342177280 | bytes 6488064 | tf_op jit(solution)/shard_map/pallas_call | solution.py:43
  134.2 13.4 %collective-permute-done.13.refs_3_ = bf16[2,320,320]{2,1,0:T(8,128)(2,1)S(1)} collective-permute-done((bf16[2,320,320]{2,1,0:T(8,128)(2,1)S(1)}, bf16[2,320,320]{2,1,0:T(8,128)(2,1)S(1)}, u32[]{:S(2)}, u32[]{:S(2)}) %collective-permute-start.13) | collective-permute-done | bytes 409632 | tf_op jit(solution)/shard_map/ppermute | solution.py:228
  152.7 4.9 %all-to-all-start.4 = ((bf16[4,256,1024]{2,1,0:T(8,128)(2,1)}), bf16[4,256,1024]{2,1,0:T(8,128)(2,1)}, u32[]{:S(2)}, u32[]{:S(2)}) async-start(bf16[4,256,1024]{2,1,0:T(8,128)(2,1)} %broadcast_in_dim.42), calls=%async_computation.4 | async-start | bytes 4194304 | tf_op jit(solution)/shard_map/all_to_all | solution.py:265
  165.8 7.1 %collective-permute-done.18 = bf16[320,256]{1,0:T(8,128)(2,1)S(1)} collective-permute-done((bf16[320,256]{1,0:T(8,128)(2,1)S(1)}, bf16[320,256]{1,0:T(8,128)(2,1)S(1)}, u32[]{:S(2)}, u32[]{:S(2)}) %collective-permute-start.18) | collective-permute-done | bytes 163872 | tf_op jit(solution)/shard_map/ppermute | solution.py:313
  173.0 3.4 %collective-permute-done.17 = bf16[2,320,256]{2,1,0:T(8,128)(2,1)} collective-permute-done((bf16[2,320,256]{2,1,0:T(8,128)(2,1)}, bf16[2,320,256]{2,1,0:T(8,128)(2,1)}, u32[]{:S(2)}, u32[]{:S(2)}) %collective-permute-start.17) | collective-permute-done | bytes 327712 | tf_op jit(solution)/shard_map/ppermute | solution.py:228
  183.7 7.6 %collective-permute-done.19 = bf16[2,320,256]{2,1,0:T(8,128)(2,1)S(1)} collective-permute-done((bf16[2,320,256]{2,1,0:T(8,128)(2,1)S(1)}, bf16[2,320,256]{2,1,0:T(8,128)(2,1)S(1)}, u32[]{:S(2)}, u32[]{:S(2)}) %collective-permute-start.19) | collective-permute-done | bytes 327712 | tf_op jit(solution)/shard_map/ppermute | solution.py:238
  191.4 6.2 %collective-permute-done.22.refs_3_ = bf16[2,320,256]{2,1,0:T(8,128)(2,1)S(1)} collective-permute-done((bf16[2,320,256]{2,1,0:T(8,128)(2,1)S(1)}, bf16[2,320,256]{2,1,0:T(8,128)(2,1)S(1)}, u32[]{:S(2)}, u32[]{:S(2)}) %collective-permute-start.22) | collective-permute-done | bytes 327712 | tf_op jit(solution)/shard_map/ppermute | solution.py:228
  203.7 8.6 %all-to-all-start.5 = ((bf16[16,80,256]{2,1,0:T(8,128)(2,1)}), bf16[16,80,256]{2,1,0:T(8,128)(2,1)S(1)}, u32[]{:S(2)}, u32[]{:S(2)}) async-start(bf16[16,80,256]{2,1,0:T(8,128)(2,1)} %add_convert_fusion), calls=%async_computation.5 | async-start | bytes 1310720 | tf_op jit(solution)/shard_map/all_to_all | solution.py:325
  218.7 5.7 %shard_map.96 = f32[320,1024]{1,0:T(8,128)} custom-call(s32[4]{0:T(128)} %copy-done.16, bf16[1024,1024]{1,0:T(8,128)(2,1)} %bitcast.86, bf16[1024,1024]{1,0:T(8,128)(2,1)} %collective-permute-done.14.other, bf16[2,320,256]{2,1,0:T(8,128)(2,1)} %copy-done.29, bf16[2,320,256]{2,1,0:T(8,128)(2,1)} %collective-permute-done.20.refs_1_, ...), custom_call_target="tpu_custom_call" | custom-call | flops 1342177280 | bytes 6815744 | tf_op jit(solution)/shard_map/pallas_call | solution.py:43
  224.4 5.2 %all-to-all-done.5 = bf16[16,80,256]{2,1,0:T(8,128)(2,1)S(1)} async-done(((bf16[16,80,256]{2,1,0:T(8,128)(2,1)}), bf16[16,80,256]{2,1,0:T(8,128)(2,1)S(1)}, u32[]{:S(2)}, u32[]{:S(2)}) %all-to-all-start.5) | async-done | bytes 655392 | tf_op jit(solution)/shard_map/all_to_all | solution.py:325
  231.1 5.2 %shard_map.97 = bf16[320,1024]{1,0:T(8,128)(2,1)} custom-call(s32[4]{0:T(128)} %copy-done.16, bf16[16,4,16,1024]{3,2,1,0:T(8,128)(2,1)} %bitcast.28.mine, bf16[16,4,16,1024]{3,2,1,0:T(8,128)(2,1)} %collective-permute-done.23.other, bf16[2,320,256]{2,1,0:T(8,128)(2,1)} %copy-done.28, bf16[2,320,256]{2,1,0:T(8,128)(2,1)} %collective-permute-done.24.refs_1_, ...), custom_call_target="tpu_custom_call" | custom-call | flops 1342177280 | bytes 6160384 | tf_op jit(solution)/shard_map/pallas_call | solution.py:43
  (157 shorter events, 78.2 us)
Async XLA Ops:
  2.6 26.5 %all-to-all-start = ((bf16[32,16,256]{2,1,0:T(8,128)(2,1)}), bf16[32,16,256]{2,1,0:T(8,128)(2,1)}, u32[]{:S(2)}, u32[]{:S(2)}) async-start(bf16[32,16,256]{2,1,0:T(8,128)(2,1)} %bitcast.7), calls=%async_computation | async-start | bytes 524288 | tf_op jit(solution)/shard_map/all_to_all | solution.py:250
  48.1 31.6 %all-to-all-start.1 = ((bf16[4,64,1024]{2,1,0:T(8,128)(2,1)}), bf16[4,64,1024]{2,1,0:T(8,128)(2,1)}, u32[]{:S(2)}, u32[]{:S(2)}) async-start(bf16[4,64,1024]{2,1,0:T(8,128)(2,1)} %broadcast_in_dim.39), calls=%async_computation.1 | async-start | bytes 1048576 | tf_op jit(solution)/shard_map/all_to_all | solution.py:265
  52.7 22.5 %collective-permute-start.7 = (bf16[2,320,320]{2,1,0:T(8,128)(2,1)S(1)}, bf16[2,320,320]{2,1,0:T(8,128)(2,1)S(1)}, u32[]{:S(2)}, u32[]{:S(2)}) collective-permute-start(bf16[2,320,320]{2,1,0:T(8,128)(2,1)S(1)} %copy-done.22), channel_id=1, source_target_pairs={{0,32},{32,64},{64,96},{96,0},{128,160},{160,192},{192,224},{224,1... | collective-permute-start | bytes 1228808 | tf_op jit(solution)/shard_map/ppermute | solution.py:228
  56.2 19.0 %collective-permute-start.8 = (bf16[2,320,320]{2,1,0:T(8,128)(2,1)S(1)}, bf16[2,320,320]{2,1,0:T(8,128)(2,1)S(1)}, u32[]{:S(2)}, u32[]{:S(2)}) collective-permute-start(bf16[2,320,320]{2,1,0:T(8,128)(2,1)S(1)} %copy-done.20), channel_id=1, source_target_pairs={{0,64},{32,96},{64,0},{96,32},{128,192},{160,224},{192,128},{224,1... | collective-permute-start | bytes 1228808 | tf_op jit(solution)/shard_map/ppermute | solution.py:228
  56.2 22.4 %collective-permute-start.9 = (bf16[2,320,320]{2,1,0:T(8,128)(2,1)S(1)}, bf16[2,320,320]{2,1,0:T(8,128)(2,1)S(1)}, u32[]{:S(2)}, u32[]{:S(2)}) collective-permute-start(bf16[2,320,320]{2,1,0:T(8,128)(2,1)S(1)} %get-tuple-element.66), channel_id=1, source_target_pairs={{0,96},{32,0},{64,32},{96,64},{128,224},{160,128},{192,160},{224,1... | collective-permute-start | bytes 1228808 | tf_op jit(solution)/shard_map/ppermute | solution.py:228
  82.4 28.8 %all-to-all-start.2 = ((bf16[4,256,1024]{2,1,0:T(8,128)(2,1)}), bf16[4,256,1024]{2,1,0:T(8,128)(2,1)S(1)}, u32[]{:S(2)}, u32[]{:S(2)}) async-start(bf16[4,256,1024]{2,1,0:T(8,128)(2,1)} %broadcast_in_dim.40), calls=%async_computation.2 | async-start | bytes 4194304 | tf_op jit(solution)/shard_map/all_to_all | solution.py:265
  88.5 16.4 %collective-permute-start.10 = (bf16[2,320,320]{2,1,0:T(8,128)(2,1)S(1)}, bf16[2,320,320]{2,1,0:T(8,128)(2,1)S(1)}, u32[]{:S(2)}, u32[]{:S(2)}) collective-permute-start(bf16[2,320,320]{2,1,0:T(8,128)(2,1)S(1)} %convert_element_type.52), channel_id=1, source_target_pairs={{0,128},{32,160},{64,192},{96,224},{128,0},{160,32},{192,64},{224,... | collective-permute-start | bytes 1228808 | tf_op jit(solution)/shard_map/ppermute | solution.py:238
  111.2 14.9 %collective-permute-start.14 = (bf16[1024,1024]{1,0:T(8,128)(2,1)S(1)}, bf16[1024,1024]{1,0:T(8,128)(2,1)}, u32[]{:S(2)}, u32[]{:S(2)}) collective-permute-start(bf16[1024,1024]{1,0:T(8,128)(2,1)S(1)} %bitcast.84), channel_id=1, source_target_pairs={{0,1},{1,0},{2,3},{3,2},{4,5},{5,4},{6,7},{7,6},{8,9},{9,8},{10,11... | collective-permute-start | bytes 6291464 | tf_op jit(solution)/shard_map/ppermute | solution.py:269
  112.1 37.8 %all-to-all-start.3 = ((bf16[4,64,1024]{2,1,0:T(8,128)(2,1)}), bf16[4,64,1024]{2,1,0:T(8,128)(2,1)}, u32[]{:S(2)}, u32[]{:S(2)}) async-start(bf16[4,64,1024]{2,1,0:T(8,128)(2,1)} %broadcast_in_dim.41), calls=%async_computation.3 | async-start | bytes 1048576 | tf_op jit(solution)/shard_map/all_to_all | solution.py:265
  122.5 25.1 %collective-permute-start.13 = (bf16[2,320,320]{2,1,0:T(8,128)(2,1)S(1)}, bf16[2,320,320]{2,1,0:T(8,128)(2,1)S(1)}, u32[]{:S(2)}, u32[]{:S(2)}) collective-permute-start(bf16[2,320,320]{2,1,0:T(8,128)(2,1)S(1)} %convert_element_type.54.refs_0_), channel_id=1, source_target_pairs={{0,96},{32,0},{64,32},{96,64},{128,224},{160,128},{192,160},{224,1... | collective-permute-start | bytes 1228808 | tf_op jit(solution)/shard_map/ppermute | solution.py:228
  122.5 25.8 %collective-permute-start.12 = (bf16[2,320,320]{2,1,0:T(8,128)(2,1)S(1)}, bf16[2,320,320]{2,1,0:T(8,128)(2,1)S(1)}, u32[]{:S(2)}, u32[]{:S(2)}) collective-permute-start(bf16[2,320,320]{2,1,0:T(8,128)(2,1)S(1)} %convert_element_type.54.refs_0_), channel_id=1, source_target_pairs={{0,64},{32,96},{64,0},{96,32},{128,192},{160,224},{192,128},{224,1... | collective-permute-start | bytes 1228808 | tf_op jit(solution)/shard_map/ppermute | solution.py:228
  123.6 25.6 %collective-permute-start.11 = (bf16[2,320,320]{2,1,0:T(8,128)(2,1)S(1)}, bf16[2,320,320]{2,1,0:T(8,128)(2,1)S(1)}, u32[]{:S(2)}, u32[]{:S(2)}) collective-permute-start(bf16[2,320,320]{2,1,0:T(8,128)(2,1)S(1)} %convert_element_type.54.refs_0_), channel_id=1, source_target_pairs={{0,32},{32,64},{64,96},{96,0},{128,160},{160,192},{192,224},{224,1... | collective-permute-start | bytes 1228808 | tf_op jit(solution)/shard_map/ppermute | solution.py:228
  152.7 46.3 %all-to-all-start.4 = ((bf16[4,256,1024]{2,1,0:T(8,128)(2,1)}), bf16[4,256,1024]{2,1,0:T(8,128)(2,1)}, u32[]{:S(2)}, u32[]{:S(2)}) async-start(bf16[4,256,1024]{2,1,0:T(8,128)(2,1)} %broadcast_in_dim.42), calls=%async_computation.4 | async-start | bytes 4194304 | tf_op jit(solution)/shard_map/all_to_all | solution.py:265
  157.6 15.3 %collective-permute-start.15 = (bf16[2,320,256]{2,1,0:T(8,128)(2,1)}, bf16[2,320,256]{2,1,0:T(8,128)(2,1)}, u32[]{:S(2)}, u32[]{:S(2)}) collective-permute-start(bf16[2,320,256]{2,1,0:T(8,128)(2,1)} %copy-done.25), channel_id=1, source_target_pairs={{0,32},{32,64},{64,96},{96,0},{128,160},{160,192},{192,224},{224,1... | collective-permute-start | bytes 983048 | tf_op jit(solution)/shard_map/ppermute | solution.py:228
  159.0 13.9 %collective-permute-start.16 = (bf16[2,320,256]{2,1,0:T(8,128)(2,1)}, bf16[2,320,256]{2,1,0:T(8,128)(2,1)}, u32[]{:S(2)}, u32[]{:S(2)}) collective-permute-start(bf16[2,320,256]{2,1,0:T(8,128)(2,1)} %copy-done.24), channel_id=1, source_target_pairs={{0,64},{32,96},{64,0},{96,32},{128,192},{160,224},{192,128},{224,1... | collective-permute-start | bytes 983048 | tf_op jit(solution)/shard_map/ppermute | solution.py:228
  159.0 17.3 %collective-permute-start.17 = (bf16[2,320,256]{2,1,0:T(8,128)(2,1)}, bf16[2,320,256]{2,1,0:T(8,128)(2,1)}, u32[]{:S(2)}, u32[]{:S(2)}) collective-permute-start(bf16[2,320,256]{2,1,0:T(8,128)(2,1)} %copy-done.23), channel_id=1, source_target_pairs={{0,96},{32,0},{64,32},{96,64},{128,224},{160,128},{192,160},{224,1... | collective-permute-start | bytes 983048 | tf_op jit(solution)/shard_map/ppermute | solution.py:228
  180.3 17.2 %collective-permute-start.22 = (bf16[2,320,256]{2,1,0:T(8,128)(2,1)S(1)}, bf16[2,320,256]{2,1,0:T(8,128)(2,1)S(1)}, u32[]{:S(2)}, u32[]{:S(2)}) collective-permute-start(bf16[2,320,256]{2,1,0:T(8,128)(2,1)S(1)} %maximum_select_fusion.refs_0_), channel_id=1, source_target_pairs={{0,96},{32,0},{64,32},{96,64},{128,224},{160,128},{192,160},{224,1... | collective-permute-start | bytes 983048 | tf_op jit(solution)/shard_map/ppermute | solution.py:228
  180.3 17.2 %collective-permute-start.21 = (bf16[2,320,256]{2,1,0:T(8,128)(2,1)S(1)}, bf16[2,320,256]{2,1,0:T(8,128)(2,1)S(1)}, u32[]{:S(2)}, u32[]{:S(2)}) collective-permute-start(bf16[2,320,256]{2,1,0:T(8,128)(2,1)S(1)} %maximum_select_fusion.refs_0_), channel_id=1, source_target_pairs={{0,64},{32,96},{64,0},{96,32},{128,192},{160,224},{192,128},{224,1... | collective-permute-start | bytes 983048 | tf_op jit(solution)/shard_map/ppermute | solution.py:228
  182.7 16.3 %collective-permute-start.20 = (bf16[2,320,256]{2,1,0:T(8,128)(2,1)S(1)}, bf16[2,320,256]{2,1,0:T(8,128)(2,1)}, u32[]{:S(2)}, u32[]{:S(2)}) collective-permute-start(bf16[2,320,256]{2,1,0:T(8,128)(2,1)S(1)} %maximum_select_fusion.refs_0_), channel_id=1, source_target_pairs={{0,32},{32,64},{64,96},{96,0},{128,160},{160,192},{192,224},{224,1... | collective-permute-start | bytes 983048 | tf_op jit(solution)/shard_map/ppermute | solution.py:228
  200.6 29.8 %collective-permute-start.23 = (bf16[16,4,16,1024]{3,2,1,0:T(8,128)(2,1)}, bf16[16,4,16,1024]{3,2,1,0:T(8,128)(2,1)}, u32[]{:S(2)}, u32[]{:S(2)}) collective-permute-start(bf16[16,4,16,1024]{3,2,1,0:T(8,128)(2,1)} %bitcast.28.mine), channel_id=1, source_target_pairs={{0,1},{1,0},{2,3},{3,2},{4,5},{5,4},{6,7},{7,6},{8,9},{9,8},{10,11... | collective-permute-start | bytes 6291464 | tf_op jit(solution)/shard_map/ppermute | solution.py:269
  203.7 25.9 %all-to-all-start.5 = ((bf16[16,80,256]{2,1,0:T(8,128)(2,1)}), bf16[16,80,256]{2,1,0:T(8,128)(2,1)S(1)}, u32[]{:S(2)}, u32[]{:S(2)}) async-start(bf16[16,80,256]{2,1,0:T(8,128)(2,1)} %add_convert_fusion), calls=%async_computation.5 | async-start | bytes 1310720 | tf_op jit(solution)/shard_map/all_to_all | solution.py:325
  212.3 18.1 %collective-permute-start.26 = (bf16[2,320,256]{2,1,0:T(8,128)(2,1)S(1)}, bf16[2,320,256]{2,1,0:T(8,128)(2,1)S(1)}, u32[]{:S(2)}, u32[]{:S(2)}) collective-permute-start(bf16[2,320,256]{2,1,0:T(8,128)(2,1)S(1)} %convert_add_fusion.2.refs_0_), channel_id=1, source_target_pairs={{0,96},{32,0},{64,32},{96,64},{128,224},{160,128},{192,160},{224,1... | collective-permute-start | bytes 983048 | tf_op jit(solution)/shard_map/ppermute | solution.py:228
  212.3 18.0 %collective-permute-start.25 = (bf16[2,320,256]{2,1,0:T(8,128)(2,1)S(1)}, bf16[2,320,256]{2,1,0:T(8,128)(2,1)}, u32[]{:S(2)}, u32[]{:S(2)}) collective-permute-start(bf16[2,320,256]{2,1,0:T(8,128)(2,1)S(1)} %convert_add_fusion.2.refs_0_), channel_id=1, source_target_pairs={{0,64},{32,96},{64,0},{96,32},{128,192},{160,224},{192,128},{224,1... | collective-permute-start | bytes 983048 | tf_op jit(solution)/shard_map/ppermute | solution.py:228
  214.7 15.7 %collective-permute-start.24 = (bf16[2,320,256]{2,1,0:T(8,128)(2,1)S(1)}, bf16[2,320,256]{2,1,0:T(8,128)(2,1)}, u32[]{:S(2)}, u32[]{:S(2)}) collective-permute-start(bf16[2,320,256]{2,1,0:T(8,128)(2,1)S(1)} %convert_add_fusion.2.refs_0_), channel_id=1, source_target_pairs={{0,32},{32,64},{64,96},{96,0},{128,160},{160,192},{192,224},{224,1... | collective-permute-start | bytes 983048 | tf_op jit(solution)/shard_map/ppermute | solution.py:228
  (46 other events, 600.3 us)

commit v5 on v4

--- a/solution.py
+++ b/solution.py
@@ -197,25 +197,26 @@
     )
 
 
-def out_body(place, mine, other, *refs):
+def out_body(place, mixed, *refs):
     inner, out = refs[:NY], refs[NY]
     total = jnp.zeros(out.shape, F32)
     for k in range(NY):
-        for rows, h in ((mine, place[3]), (other, 1 - place[3])):
-            total += dot(inner[k][h], rows[:, k].reshape(-1, out.shape[1]), NN)
+        for h in range(ZH):
+            rows = mixed[:, h, k]
+            total += dot(inner[k][h], rows.reshape(-1, out.shape[1]), NN)
     out[...] = total.astype(out.dtype)
 
 
 def grown_output(place, mixed, inner):
-    hidden, count = inner[0].shape[1], mixed[0].shape[-1]
+    hidden, count = inner[0].shape[1], mixed.shape[-1]
     part = count // 4
-    rows = pl.BlockSpec((*mixed[0].shape[:-1], part), lambda s: (0, 0, 0, s))
-    return call(
-        out_body, place, (*mixed, *inner), struct((hidden, count), BF),
-        4 * mixed[0].size * hidden,
+    return call(
+        out_body, place, (mixed, *inner), struct((hidden, count), BF),
+        2 * mixed.size * hidden,
         limit=56,
         grid=(count // part,),
-        in_specs=[rows] * 2 + [keep_whole(inner[0].shape)] * NY,
+        in_specs=[pl.BlockSpec((*mixed.shape[:-1], part), lambda s: (0, 0, 0, 0, s))]
+        + [keep_whole(inner[0].shape)] * NY,
         out_specs=pl.BlockSpec((hidden, part), lambda s: (0, s)),
     )
 
@@ -285,39 +286,35 @@
     slot_of = owners[:, 1] * (MP // SECTIONS) + owners[:, 0]
 
     slots = panel_slots(saved_panels, y)
-    terms = grad_terms(place, tokens, cotangent.T)
+    part = sum_y(grad_terms(place, tokens, cotangent.T))
+    slots, part = together(slots, part)
+
+    grads = sum_z(part)
     strip = own_strip(row_growth, z_hi, mp_index)
-    slots, terms, strip = together(slots, terms, strip)
-
-    rows = panel_rows(slots, slot_of, z_hi, y)
-    strips = jnp.concatenate(gather_y(strip))
-    rows, terms, strips = together(rows, terms, strips)
-
-    mixed = dot(strips, tokens, NT).astype(BF)
-    rows = gather(rows, Z_GROUPS)
-    part = sum_y(terms)
-    rows, part, mixed = together(rows, part, mixed)
-
-    half = gather(rows, X_GROUPS)
-    grads = sum_z(part)
-    half, grads, mixed = together(half, grads, mixed)
+    rows = gather(panel_rows(slots, slot_of, z_hi, y), Z_GROUPS)
+    rows, grads, strip = together(rows, grads, strip)
 
     grad = pick(grads, z_hi).T
     grads = gather_y(grads.astype(BF))
-    source = both_cores(half)
-    inners = inner_terms(place, col_growth, source)
-    mixed = gather(mixed, Z_GROUPS)
-    grads, inners, mixed = together(grads, inners, mixed)
-
+    strips = jnp.concatenate(gather_y(strip))
+    mixed = dot(strips, tokens, NT).astype(BF)
+    half = gather(rows, X_GROUPS)
+    half, grads, mixed = together(half, grads, mixed)
+
+    mixed = lax.all_gather(mixed, "mp", axis=0, tiled=True)
+    mixed = mixed.reshape(NX * NZ, NC, NY, -1, tokens.shape[0])
     back = back_block(place, row_growth, grads)
     other = lax.ppermute(back, "dp", SWAP_ZH)
     pair = jnp.where(z_hi == 0, jnp.stack([back, other]), jnp.stack([other, back]))
-    mixed = gather(mixed, X_GROUPS).reshape(NX * NZ, NY, -1, mixed.shape[1])
+    source = both_cores(half)
+    inners = inner_terms(place, col_growth, source)
+    inners, pair = together(inners, pair)
+
     part, pair = together(sum_y(inners), pair)
 
     inners = sum_z(part)
     backs = gather_y(pair)
-    inners, backs, mixed = together(inners, backs, mixed)
+    inners, backs = together(inners, backs)
 
     inners = inners.astype(BF)
     keep, give = row_terms(place, pick(inners, z_hi), grads)
@@ -326,7 +323,7 @@
     grad_row = keep.astype(F32).sum(axis=0)
     grad_col = col_grad(place, source, backs)
     inners = gather_y(inners)
-    mixed, grad_col = together(both_cores(mixed), grad_col)
+    mixed, grad_col = together(mixed, grad_col)
     grown_out = grown_output(place, mixed, inners).T
     return (grown_out, grad, grad_row, grad_col)
 

time: 240 us -> 243 us (1.012)
  waiting for transfers between devices: 82.6 us -> 107 us
  starting transfers between devices: 79.2 us -> 62.9 us
  local copies, waits for them, and re-layouts: 31.4 us -> 15.3 us
  between operations: 1.07 us -> 14.4 us
  other arithmetic: 13.4 us -> 8.59 us
  Pallas kernels: 23.7 us -> 26.9 us
    all_to_all x4 -> x2, starting transfers between devices: 23.3 us -> 9.29 us  [gather(): lax.all_to_all(blocks, 'mp', 0, 0, axis_index_groups=groups)]
    ppermute x2, waiting for transfers between devices: 22.4 us -> 36 us  [sum_z(): return part + lax.ppermute(part.astype(BF), 'dp', SWAP_ZH).astype(F32)]
    unnamed x76 -> x34, local copies, waits for them, and re-layouts: 19.6 us -> 10.2 us
    broadcast_in_dim x4 -> x2, local copies, waits for them, and re-layouts: 7.09 us -> 2.45 us  [gather(): blocks = jnp.broadcast_to(block[None], (len(groups[0]), *block.shape))]
    all_to_all x1, starting transfers between devices: 8.61 us -> 4.53 us  [shards(): lax.all_to_all(keep.astype(BF), 'mp', 0, 0, axis_index_groups=PLANE_GROUPS)]
    ppermute x1, waiting for transfers between devices: 7.12 us -> 10.8 us  [shards(): other = lax.ppermute(back, 'dp', SWAP_ZH)]
    pallas_call x6, Pallas kernels: 23.7 us -> 26.9 us  [call(): pl.pallas_call(body, out_shape=outs, grid=specs.get('grid', ()), in_specs...]
    all_to_all x1, waiting for transfers between devices: 5.23 us -> 8.2 us  [shards(): lax.all_to_all(keep.astype(BF), 'mp', 0, 0, axis_index_groups=PLANE_GROUPS)]
  transfers between devices with their start and end apart: 34 -> 32, of which waited for: 14 -> 15; matrix products, arithmetic and copies ran while one was open for 9% -> 8% of each run, Pallas kernels for 7% -> 7%
where the time goes in v5:
time: 243 us; the launch traced here: 240 us
  waiting for transfers between devices  107 us (44%)
  starting transfers between devices  62.9 us (26%)
  Pallas kernels  26.9 us (11%)
  local copies, waits for them, and re-layouts  15.3 us (6%)
  between operations  14.4 us (6%)
  other arithmetic  8.59 us (4%)
  matrix products  4.83 us (2%)
    ppermute x21, waiting for transfers between devices, exchange_y(): got = {k: lax.ppermute(block_for(k), 'dp', shift_y(k)) for k in (2, 1, 3)}  43.8 us
    ppermute x2, waiting for transfers between devices, sum_z(): return part + lax.ppermute(part.astype(BF), 'dp', SWAP_ZH).astype(F32)  36 us
    pallas_call x6, Pallas kernels, call(): pl.pallas_call(body, out_shape=outs, grid=specs.get('grid', ()), in_specs...  26.9 us
    ppermute x21, starting transfers between devices, exchange_y(): got = {k: lax.ppermute(block_for(k), 'dp', shift_y(k)) for k in (2, 1, 3)}  24.7 us
    ppermute x1, waiting for transfers between devices, shards(): other = lax.ppermute(back, 'dp', SWAP_ZH)  10.8 us
    unnamed x34, local copies, waits for them, and re-layouts  10.2 us
    all_to_all x2, starting transfers between devices, gather(): lax.all_to_all(blocks, 'mp', 0, 0, axis_index_groups=groups)  9.29 us
    all_to_all x1, starting transfers between devices, panel_slots(): return lax.all_to_all(mine, 'mp', 0, 0)  9.09 us
  transfers between devices with their start and end apart: 32, of which 15 were waited for; matrix products, arithmetic and copies ran while one was open for 8% of the time, Pallas kernels for 7%

profile of v5, /device:TPU:30, one launch (start us, length us, event | category | flops | bytes accessed | tf_op | source)
XLA Modules:
  0.0 240.4 jit_solution(16883338109411756519)
XLA Ops:
  10.9 5.7 %shard_map.93 = (f32[2,320,320]{2,1,0:T(8,128)S(1)}, bf16[2,320,320]{2,1,0:T(8,128)(2,1)}, bf16[2,320,320]{2,1,0:T(8,128)(2,1)}, bf16[2,320,320]{2,1,0:T(8,128)(2,1)}) custom-call(s32[4]{0:T(128)S(1)} %pad_add_fusion.place, bf16[1024,2560]{1,0:T(8,128)(2,1)S(1)} %copy-done.2, bf16[320,1024]{1,0:T(8,128)(2,1)S(1)} %bitcast.86), custom_call_target="tpu_custom_call" | custom-call | flops 1677721600 | bytes 7946240 | tf_op jit(solution)/shard_map/pallas_call | solution.py:43
  20.1 9.1 %all-to-all-start = ((bf16[32,16,256]{2,1,0:T(8,128)(2,1)}), bf16[32,16,256]{2,1,0:T(8,128)(2,1)}, u32[]{:S(2)}, u32[]{:S(2)}) async-start(bf16[32,16,256]{2,1,0:T(8,128)(2,1)} %bitcast.92), calls=%async_computation | async-start | bytes 524288 | tf_op jit(solution)/shard_map/all_to_all | solution.py:251
  32.7 9.3 %collective-permute-done.2 = bf16[2,320,320]{2,1,0:T(8,128)(2,1)} collective-permute-done((bf16[2,320,320]{2,1,0:T(8,128)(2,1)}, bf16[2,320,320]{2,1,0:T(8,128)(2,1)}, u32[]{:S(2)}, u32[]{:S(2)}) %collective-permute-start.2) | collective-permute-done | bytes 409632 | tf_op jit(solution)/shard_map/ppermute | solution.py:229
  50.0 7.2 %collective-permute-start.7 = (bf16[16,2560]{1,0:T(8,128)(2,1)S(1)}, bf16[16,2560]{1,0:T(8,128)(2,1)S(1)}, u32[]{:S(2)}, u32[]{:S(2)}) collective-permute-start(bf16[16,2560]{1,0:T(8,128)(2,1)S(1)} %dynamic-slice_bitcast_fusion.2), channel_id=1, source_target_pairs={{0,128},{32,160},{64,192},{96,224},{128,0},{160,32},{192,64},{224,... | collective-permute-start | bytes 245768 | tf_op jit(solution)/shard_map/ppermute | solution.py:277
  59.1 4.5 %all-to-all-start.1 = ((bf16[4,64,1024]{2,1,0:T(8,128)(2,1)}), bf16[4,64,1024]{2,1,0:T(8,128)(2,1)S(1)}, u32[]{:S(2)}, u32[]{:S(2)}) async-start(bf16[4,64,1024]{2,1,0:T(8,128)(2,1)} %broadcast_in_dim.29), calls=%async_computation.1 | async-start | bytes 1048576 | tf_op jit(solution)/shard_map/all_to_all | solution.py:266
  64.6 21.8 %collective-permute-done.6 = bf16[2,320,320]{2,1,0:T(8,128)(2,1)S(1)} collective-permute-done((bf16[2,320,320]{2,1,0:T(8,128)(2,1)}, bf16[2,320,320]{2,1,0:T(8,128)(2,1)S(1)}, u32[]{:S(2)}, u32[]{:S(2)}) %collective-permute-start.6) | collective-permute-done | bytes 409632 | tf_op jit(solution)/shard_map/ppermute | solution.py:239
  87.4 6.6 %all-to-all-done.1 = bf16[4,64,1024]{2,1,0:T(8,128)(2,1)S(1)} async-done(((bf16[4,64,1024]{2,1,0:T(8,128)(2,1)}), bf16[4,64,1024]{2,1,0:T(8,128)(2,1)S(1)}, u32[]{:S(2)}, u32[]{:S(2)}) %all-to-all-start.1) | async-done | bytes 524320 | tf_op jit(solution)/shard_map/all_to_all | solution.py:266
  95.6 4.8 %all-to-all-start.2 = ((bf16[4,256,1024]{2,1,0:T(8,128)(2,1)}), bf16[4,256,1024]{2,1,0:T(8,128)(2,1)S(1)}, u32[]{:S(2)}, u32[]{:S(2)}) async-start(bf16[4,256,1024]{2,1,0:T(8,128)(2,1)} %broadcast_in_dim.30), calls=%async_computation.2 | async-start | bytes 4194304 | tf_op jit(solution)/shard_map/all_to_all | solution.py:266
  105.7 2.6 %collective-permute-start.10 = (bf16[2,320,320]{2,1,0:T(8,128)(2,1)}, bf16[2,320,320]{2,1,0:T(8,128)(2,1)}, u32[]{:S(2)}, u32[]{:S(2)}) collective-permute-start(bf16[2,320,320]{2,1,0:T(8,128)(2,1)} %convert_element_type.53.refs_0_), channel_id=1, source_target_pairs={{0,96},{32,0},{64,32},{96,64},{128,224},{160,128},{192,160},{224,1... | collective-permute-start | bytes 1228808 | tf_op jit(solution)/shard_map/ppermute | solution.py:229
  110.6 4.8 %convolution_convert_fusion = bf16[64,1024]{1,0:T(8,128)(2,1)} fusion(bf16[1024,2560]{1,0:T(8,128)(2,1)} %tokens.1, bf16[16,2560]{1,0:T(8,128)(2,1)S(1)} %collective-permute-done.13, bf16[16,2560]{1,0:T(8,128)(2,1)S(1)} %collective-permute-done.12, bf16[16,2560]{1,0:T(8,128)(2,1)S(1)} %collective-permute-done.11, bf16[16,2560]{1,0:T(8,128)(2,1)S(1)} %broadcast_select_fusion.1), kind=kOutput, calls=%fused_computation.3 | convolution fusion | flops 336920576 | bytes 5701632 | tf_op jit(solution)/shard_map/dot_general | solution.py:26
  115.5 5.9 %collective-permute-done.10.refs_3_ = bf16[2,320,320]{2,1,0:T(8,128)(2,1)} collective-permute-done((bf16[2,320,320]{2,1,0:T(8,128)(2,1)}, bf16[2,320,320]{2,1,0:T(8,128)(2,1)}, u32[]{:S(2)}, u32[]{:S(2)}) %collective-permute-start.10) | collective-permute-done | bytes 409632 | tf_op jit(solution)/shard_map/ppermute | solution.py:229
  122.8 8.0 %collective-permute-done.9.refs_2_ = bf16[2,320,320]{2,1,0:T(8,128)(2,1)} collective-permute-done((bf16[2,320,320]{2,1,0:T(8,128)(2,1)}, bf16[2,320,320]{2,1,0:T(8,128)(2,1)}, u32[]{:S(2)}, u32[]{:S(2)}) %collective-permute-start.9) | collective-permute-done | bytes 409632 | tf_op jit(solution)/shard_map/ppermute | solution.py:229
  135.2 3.7 %collective-permute-start.15 = (bf16[320,256]{1,0:T(8,128)(2,1)S(1)}, bf16[320,256]{1,0:T(8,128)(2,1)S(1)}, u32[]{:S(2)}, u32[]{:S(2)}) collective-permute-start(bf16[320,256]{1,0:T(8,128)(2,1)S(1)} %shard_map.95), channel_id=1, source_target_pairs={{0,128},{32,160},{64,192},{96,224},{128,0},{160,32},{192,64},{224,... | collective-permute-start | bytes 491528 | tf_op jit(solution)/shard_map/ppermute | solution.py:307
  138.8 10.8 %collective-permute-done.15 = bf16[320,256]{1,0:T(8,128)(2,1)S(1)} collective-permute-done((bf16[320,256]{1,0:T(8,128)(2,1)S(1)}, bf16[320,256]{1,0:T(8,128)(2,1)S(1)}, u32[]{:S(2)}, u32[]{:S(2)}) %collective-permute-start.15) | collective-permute-done | bytes 163872 | tf_op jit(solution)/shard_map/ppermute | solution.py:307
  150.9 5.4 %shard_map.94 = (f32[2,320,256]{2,1,0:T(8,128)S(1)}, bf16[2,320,256]{2,1,0:T(8,128)(2,1)S(1)}, bf16[2,320,256]{2,1,0:T(8,128)(2,1)S(1)}, bf16[2,320,256]{2,1,0:T(8,128)(2,1)S(1)}) custom-call(s32[4]{0:T(128)S(1)} %pad_add_fusion.place, bf16[320,1024]{1,0:T(8,128)(2,1)S(1)} %copy-done.7, bf16[1024,1024]{1,0:T(8,128)(2,1)S(1)} %bitcast.83, ...), custom_call_target="tpu_custom_call" | custom-call | flops 1342177280 | bytes 6488064 | tf_op jit(solution)/shard_map/pallas_call | solution.py:43
  156.3 4.6 %collective-permute-start.16 = (bf16[2,320,256]{2,1,0:T(8,128)(2,1)S(1)}, bf16[2,320,256]{2,1,0:T(8,128)(2,1)S(1)}, u32[]{:S(2)}, u32[]{:S(2)}) collective-permute-start(bf16[2,320,256]{2,1,0:T(8,128)(2,1)S(1)} %get-tuple-element.59), channel_id=1, source_target_pairs={{0,32},{32,64},{64,96},{96,0},{128,160},{160,192},{192,224},{224,1... | collective-permute-start | bytes 983048 | tf_op jit(solution)/shard_map/ppermute | solution.py:229
  161.9 12.1 %collective-permute-done.16 = bf16[2,320,256]{2,1,0:T(8,128)(2,1)S(1)} collective-permute-done((bf16[2,320,256]{2,1,0:T(8,128)(2,1)S(1)}, bf16[2,320,256]{2,1,0:T(8,128)(2,1)S(1)}, u32[]{:S(2)}, u32[]{:S(2)}) %collective-permute-start.16) | collective-permute-done | bytes 327712 | tf_op jit(solution)/shard_map/ppermute | solution.py:229
  174.0 3.4 %collective-permute-done.18 = bf16[2,320,256]{2,1,0:T(8,128)(2,1)S(1)} collective-permute-done((bf16[2,320,256]{2,1,0:T(8,128)(2,1)S(1)}, bf16[2,320,256]{2,1,0:T(8,128)(2,1)S(1)}, u32[]{:S(2)}, u32[]{:S(2)}) %collective-permute-start.18) | collective-permute-done | bytes 327712 | tf_op jit(solution)/shard_map/ppermute | solution.py:229
  177.6 4.1 %collective-permute-start.19 = (bf16[2,320,256]{2,1,0:T(8,128)(2,1)S(1)}, bf16[2,320,256]{2,1,0:T(8,128)(2,1)S(1)}, u32[]{:S(2)}, u32[]{:S(2)}) collective-permute-start(bf16[2,320,256]{2,1,0:T(8,128)(2,1)S(1)} %convert_element_type.58), channel_id=1, source_target_pairs={{0,128},{32,160},{64,192},{96,224},{128,0},{160,32},{192,64},{224,... | collective-permute-start | bytes 983048 | tf_op jit(solution)/shard_map/ppermute | solution.py:239
  183.7 14.2 %collective-permute-done.19 = bf16[2,320,256]{2,1,0:T(8,128)(2,1)S(1)} collective-permute-done((bf16[2,320,256]{2,1,0:T(8,128)(2,1)S(1)}, bf16[2,320,256]{2,1,0:T(8,128)(2,1)S(1)}, u32[]{:S(2)}, u32[]{:S(2)}) %collective-permute-start.19) | collective-permute-done | bytes 327712 | tf_op jit(solution)/shard_map/ppermute | solution.py:239
  205.0 4.5 %all-to-all-start.3 = ((bf16[16,80,256]{2,1,0:T(8,128)(2,1)}), bf16[16,80,256]{2,1,0:T(8,128)(2,1)S(1)}, u32[]{:S(2)}, u32[]{:S(2)}) async-start(bf16[16,80,256]{2,1,0:T(8,128)(2,1)} %add_convert_fusion), calls=%async_computation.3 | async-start | bytes 1310720 | tf_op jit(solution)/shard_map/all_to_all | solution.py:322
  213.0 5.7 %shard_map.96 = f32[320,1024]{1,0:T(8,128)} custom-call(s32[4]{0:T(128)} %copy-done.5, bf16[1024,1024]{1,0:T(8,128)(2,1)} %bitcast.84, bf16[1024,1024]{1,0:T(8,128)(2,1)} %collective-permute-done.14.other, bf16[2,320,256]{2,1,0:T(8,128)(2,1)} %copy-done.10, bf16[2,320,256]{2,1,0:T(8,128)(2,1)} %copy-done.11, bf16[2,320,256]{2,1,0:T(8,128)(2,1)} %copy-done.12, ...), custom_call_target="tpu_custom_call" | custom-call | flops 1342177280 | bytes 6815744 | tf_op jit(solution)/shard_map/pallas_call | solution.py:43
  218.7 8.2 %all-to-all-done.3 = bf16[16,80,256]{2,1,0:T(8,128)(2,1)S(1)} async-done(((bf16[16,80,256]{2,1,0:T(8,128)(2,1)}), bf16[16,80,256]{2,1,0:T(8,128)(2,1)S(1)}, u32[]{:S(2)}, u32[]{:S(2)}) %all-to-all-start.3) | async-done | bytes 655392 | tf_op jit(solution)/shard_map/all_to_all | solution.py:322
  228.3 5.3 %shard_map.97 = bf16[320,1024]{1,0:T(8,128)(2,1)} custom-call(s32[4]{0:T(128)} %copy-done.5, bf16[16,2,4,16,1024]{4,3,2,1,0:T(8,128)(2,1)} %bitcast.87, bf16[2,320,256]{2,1,0:T(8,128)(2,1)} %copy-done.9, bf16[2,320,256]{2,1,0:T(8,128)(2,1)} %collective-permute-done.23.refs_1_, bf16[2,320,256]{2,1,0:T(8,128)(2,1)} %collective-permute-done.24.refs_2_, ...), custom_call_target="tpu_custom_call" | custom-call | flops 1342177280 | bytes 6160384 | tf_op jit(solution)/shard_map/pallas_call | solution.py:43
  (109 shorter events, 53.7 us)
Async XLA Ops:
  16.6 14.4 %collective-permute-start = (bf16[2,320,320]{2,1,0:T(8,128)(2,1)}, bf16[2,320,320]{2,1,0:T(8,128)(2,1)}, u32[]{:S(2)}, u32[]{:S(2)}) collective-permute-start(bf16[2,320,320]{2,1,0:T(8,128)(2,1)} %get-tuple-element.40), channel_id=1, source_target_pairs={{0,32},{32,64},{64,96},{96,0},{128,160},{160,192},{192,224},{224,1... | collective-permute-start | bytes 1228808 | tf_op jit(solution)/shard_map/ppermute | solution.py:229
  16.8 16.0 %collective-permute-start.1 = (bf16[2,320,320]{2,1,0:T(8,128)(2,1)}, bf16[2,320,320]{2,1,0:T(8,128)(2,1)}, u32[]{:S(2)}, u32[]{:S(2)}) collective-permute-start(bf16[2,320,320]{2,1,0:T(8,128)(2,1)} %get-tuple-element.41), channel_id=1, source_target_pairs={{0,64},{32,96},{64,0},{96,32},{128,192},{160,224},{192,128},{224,1... | collective-permute-start | bytes 1228808 | tf_op jit(solution)/shard_map/ppermute | solution.py:229
  19.4 22.7 %collective-permute-start.2 = (bf16[2,320,320]{2,1,0:T(8,128)(2,1)}, bf16[2,320,320]{2,1,0:T(8,128)(2,1)}, u32[]{:S(2)}, u32[]{:S(2)}) collective-permute-start(bf16[2,320,320]{2,1,0:T(8,128)(2,1)} %get-tuple-element.42), channel_id=1, source_target_pairs={{0,96},{32,0},{64,32},{96,64},{128,224},{160,128},{192,160},{224,1... | collective-permute-start | bytes 1228808 | tf_op jit(solution)/shard_map/ppermute | solution.py:229
  20.1 23.4 %all-to-all-start = ((bf16[32,16,256]{2,1,0:T(8,128)(2,1)}), bf16[32,16,256]{2,1,0:T(8,128)(2,1)}, u32[]{:S(2)}, u32[]{:S(2)}) async-start(bf16[32,16,256]{2,1,0:T(8,128)(2,1)} %bitcast.92), calls=%async_computation | async-start | bytes 524288 | tf_op jit(solution)/shard_map/all_to_all | solution.py:251
  50.0 13.7 %collective-permute-start.7 = (bf16[16,2560]{1,0:T(8,128)(2,1)S(1)}, bf16[16,2560]{1,0:T(8,128)(2,1)S(1)}, u32[]{:S(2)}, u32[]{:S(2)}) collective-permute-start(bf16[16,2560]{1,0:T(8,128)(2,1)S(1)} %dynamic-slice_bitcast_fusion.2), channel_id=1, source_target_pairs={{0,128},{32,160},{64,192},{96,224},{128,0},{160,32},{192,64},{224,... | collective-permute-start | bytes 245768 | tf_op jit(solution)/shard_map/ppermute | solution.py:277
  58.0 28.4 %collective-permute-start.6 = (bf16[2,320,320]{2,1,0:T(8,128)(2,1)}, bf16[2,320,320]{2,1,0:T(8,128)(2,1)S(1)}, u32[]{:S(2)}, u32[]{:S(2)}) collective-permute-start(bf16[2,320,320]{2,1,0:T(8,128)(2,1)} %convert_element_type.51), channel_id=1, source_target_pairs={{0,128},{32,160},{64,192},{96,224},{128,0},{160,32},{192,64},{224,... | collective-permute-start | bytes 1228808 | tf_op jit(solution)/shard_map/ppermute | solution.py:239
  59.1 34.9 %all-to-all-start.1 = ((bf16[4,64,1024]{2,1,0:T(8,128)(2,1)}), bf16[4,64,1024]{2,1,0:T(8,128)(2,1)S(1)}, u32[]{:S(2)}, u32[]{:S(2)}) async-start(bf16[4,64,1024]{2,1,0:T(8,128)(2,1)} %broadcast_in_dim.29), calls=%async_computation.1 | async-start | bytes 1048576 | tf_op jit(solution)/shard_map/all_to_all | solution.py:266
  95.6 35.2 %all-to-all-start.2 = ((bf16[4,256,1024]{2,1,0:T(8,128)(2,1)}), bf16[4,256,1024]{2,1,0:T(8,128)(2,1)S(1)}, u32[]{:S(2)}, u32[]{:S(2)}) async-start(bf16[4,256,1024]{2,1,0:T(8,128)(2,1)} %broadcast_in_dim.30), calls=%async_computation.2 | async-start | bytes 4194304 | tf_op jit(solution)/shard_map/all_to_all | solution.py:266
  100.4 127.2 %all-gather.2.cloned.1.call-start = ((), (), s32[]{:S(2)}) async-start(), calls=%async_computation.4 | async-start | bytes 4325376 | tf_op jit(solution)/shard_map/all_gather | solution.py:304
  105.7 15.7 %collective-permute-start.10 = (bf16[2,320,320]{2,1,0:T(8,128)(2,1)}, bf16[2,320,320]{2,1,0:T(8,128)(2,1)}, u32[]{:S(2)}, u32[]{:S(2)}) collective-permute-start(bf16[2,320,320]{2,1,0:T(8,128)(2,1)} %convert_element_type.53.refs_0_), channel_id=1, source_target_pairs={{0,96},{32,0},{64,32},{96,64},{128,224},{160,128},{192,160},{224,1... | collective-permute-start | bytes 1228808 | tf_op jit(solution)/shard_map/ppermute | solution.py:229
  108.3 14.5 %collective-permute-start.8 = (bf16[2,320,320]{2,1,0:T(8,128)(2,1)}, bf16[2,320,320]{2,1,0:T(8,128)(2,1)}, u32[]{:S(2)}, u32[]{:S(2)}) collective-permute-start(bf16[2,320,320]{2,1,0:T(8,128)(2,1)} %convert_element_type.53.refs_0_), channel_id=1, source_target_pairs={{0,32},{32,64},{64,96},{96,0},{128,160},{160,192},{192,224},{224,1... | collective-permute-start | bytes 1228808 | tf_op jit(solution)/shard_map/ppermute | solution.py:229
  108.9 21.9 %collective-permute-start.9 = (bf16[2,320,320]{2,1,0:T(8,128)(2,1)}, bf16[2,320,320]{2,1,0:T(8,128)(2,1)}, u32[]{:S(2)}, u32[]{:S(2)}) collective-permute-start(bf16[2,320,320]{2,1,0:T(8,128)(2,1)} %convert_element_type.53.refs_0_), channel_id=1, source_target_pairs={{0,64},{32,96},{64,0},{96,32},{128,192},{160,224},{192,128},{224,1... | collective-permute-start | bytes 1228808 | tf_op jit(solution)/shard_map/ppermute | solution.py:229
  130.8 18.9 %collective-permute-start.14 = (bf16[1024,1024]{1,0:T(8,128)(2,1)S(1)}, bf16[1024,1024]{1,0:T(8,128)(2,1)}, u32[]{:S(2)}, u32[]{:S(2)}) collective-permute-start(bf16[1024,1024]{1,0:T(8,128)(2,1)S(1)} %bitcast.82), channel_id=1, source_target_pairs={{0,1},{1,0},{2,3},{3,2},{4,5},{5,4},{6,7},{7,6},{8,9},{9,8},{10,11... | collective-permute-start | bytes 6291464 | tf_op jit(solution)/shard_map/ppermute | solution.py:270
  135.2 14.5 %collective-permute-start.15 = (bf16[320,256]{1,0:T(8,128)(2,1)S(1)}, bf16[320,256]{1,0:T(8,128)(2,1)S(1)}, u32[]{:S(2)}, u32[]{:S(2)}) collective-permute-start(bf16[320,256]{1,0:T(8,128)(2,1)S(1)} %shard_map.95), channel_id=1, source_target_pairs={{0,128},{32,160},{64,192},{96,224},{128,0},{160,32},{192,64},{224,... | collective-permute-start | bytes 491528 | tf_op jit(solution)/shard_map/ppermute | solution.py:307
  156.3 17.6 %collective-permute-start.16 = (bf16[2,320,256]{2,1,0:T(8,128)(2,1)S(1)}, bf16[2,320,256]{2,1,0:T(8,128)(2,1)S(1)}, u32[]{:S(2)}, u32[]{:S(2)}) collective-permute-start(bf16[2,320,256]{2,1,0:T(8,128)(2,1)S(1)} %get-tuple-element.59), channel_id=1, source_target_pairs={{0,32},{32,64},{64,96},{96,0},{128,160},{160,192},{192,224},{224,1... | collective-permute-start | bytes 983048 | tf_op jit(solution)/shard_map/ppermute | solution.py:229
  160.9 16.5 %collective-permute-start.18 = (bf16[2,320,256]{2,1,0:T(8,128)(2,1)S(1)}, bf16[2,320,256]{2,1,0:T(8,128)(2,1)S(1)}, u32[]{:S(2)}, u32[]{:S(2)}) collective-permute-start(bf16[2,320,256]{2,1,0:T(8,128)(2,1)S(1)} %get-tuple-element.61), channel_id=1, source_target_pairs={{0,96},{32,0},{64,32},{96,64},{128,224},{160,128},{192,160},{224,1... | collective-permute-start | bytes 983048 | tf_op jit(solution)/shard_map/ppermute | solution.py:229
  177.6 20.4 %collective-permute-start.19 = (bf16[2,320,256]{2,1,0:T(8,128)(2,1)S(1)}, bf16[2,320,256]{2,1,0:T(8,128)(2,1)S(1)}, u32[]{:S(2)}, u32[]{:S(2)}) collective-permute-start(bf16[2,320,256]{2,1,0:T(8,128)(2,1)S(1)} %convert_element_type.58), channel_id=1, source_target_pairs={{0,128},{32,160},{64,192},{96,224},{128,0},{160,32},{192,64},{224,... | collective-permute-start | bytes 983048 | tf_op jit(solution)/shard_map/ppermute | solution.py:239
  181.7 16.3 %collective-permute-start.20 = (bf16[2,320,256]{2,1,0:T(8,128)(2,1)S(1)}, bf16[2,320,256]{2,1,0:T(8,128)(2,1)S(1)}, u32[]{:S(2)}, u32[]{:S(2)}) collective-permute-start(bf16[2,320,256]{2,1,0:T(8,128)(2,1)S(1)} %maximum_select_fusion.refs_0_), channel_id=1, source_target_pairs={{0,32},{32,64},{64,96},{96,0},{128,160},{160,192},{192,224},{224,1... | collective-permute-start | bytes 983048 | tf_op jit(solution)/shard_map/ppermute | solution.py:229
  182.6 15.4 %collective-permute-start.21 = (bf16[2,320,256]{2,1,0:T(8,128)(2,1)S(1)}, bf16[2,320,256]{2,1,0:T(8,128)(2,1)S(1)}, u32[]{:S(2)}, u32[]{:S(2)}) collective-permute-start(bf16[2,320,256]{2,1,0:T(8,128)(2,1)S(1)} %maximum_select_fusion.refs_0_), channel_id=1, source_target_pairs={{0,64},{32,96},{64,0},{96,32},{128,192},{160,224},{192,128},{224,1... | collective-permute-start | bytes 983048 | tf_op jit(solution)/shard_map/ppermute | solution.py:229
  182.9 16.4 %collective-permute-start.22 = (bf16[2,320,256]{2,1,0:T(8,128)(2,1)S(1)}, bf16[2,320,256]{2,1,0:T(8,128)(2,1)S(1)}, u32[]{:S(2)}, u32[]{:S(2)}) collective-permute-start(bf16[2,320,256]{2,1,0:T(8,128)(2,1)S(1)} %maximum_select_fusion.refs_0_), channel_id=1, source_target_pairs={{0,96},{32,0},{64,32},{96,64},{128,224},{160,128},{192,160},{224,1... | collective-permute-start | bytes 983048 | tf_op jit(solution)/shard_map/ppermute | solution.py:229
  205.0 21.9 %all-to-all-start.3 = ((bf16[16,80,256]{2,1,0:T(8,128)(2,1)}), bf16[16,80,256]{2,1,0:T(8,128)(2,1)S(1)}, u32[]{:S(2)}, u32[]{:S(2)}) async-start(bf16[16,80,256]{2,1,0:T(8,128)(2,1)} %add_convert_fusion), calls=%async_computation.3 | async-start | bytes 1310720 | tf_op jit(solution)/shard_map/all_to_all | solution.py:322
  209.6 18.1 %collective-permute-start.23 = (bf16[2,320,256]{2,1,0:T(8,128)(2,1)S(1)}, bf16[2,320,256]{2,1,0:T(8,128)(2,1)}, u32[]{:S(2)}, u32[]{:S(2)}) collective-permute-start(bf16[2,320,256]{2,1,0:T(8,128)(2,1)S(1)} %convert_add_fusion.2.refs_0_), channel_id=1, source_target_pairs={{0,32},{32,64},{64,96},{96,0},{128,160},{160,192},{192,224},{224,1... | collective-permute-start | bytes 983048 | tf_op jit(solution)/shard_map/ppermute | solution.py:229
  210.8 16.8 %collective-permute-start.24 = (bf16[2,320,256]{2,1,0:T(8,128)(2,1)S(1)}, bf16[2,320,256]{2,1,0:T(8,128)(2,1)}, u32[]{:S(2)}, u32[]{:S(2)}) collective-permute-start(bf16[2,320,256]{2,1,0:T(8,128)(2,1)S(1)} %convert_add_fusion.2.refs_0_), channel_id=1, source_target_pairs={{0,64},{32,96},{64,0},{96,32},{128,192},{160,224},{192,128},{224,1... | collective-permute-start | bytes 983048 | tf_op jit(solution)/shard_map/ppermute | solution.py:229
  211.1 17.1 %collective-permute-start.25 = (bf16[2,320,256]{2,1,0:T(8,128)(2,1)S(1)}, bf16[2,320,256]{2,1,0:T(8,128)(2,1)}, u32[]{:S(2)}, u32[]{:S(2)}) collective-permute-start(bf16[2,320,256]{2,1,0:T(8,128)(2,1)S(1)} %convert_add_fusion.2.refs_0_), channel_id=1, source_target_pairs={{0,96},{32,0},{64,32},{96,64},{128,224},{160,128},{192,160},{224,1... | collective-permute-start | bytes 983048 | tf_op jit(solution)/shard_map/ppermute | solution.py:229
  (23 other events, 400.0 us)
Sparse Core Ops, SparseCore 0:
  130.9 75.6 all-gather.1

commit v6 on v5

--- a/solution.py
+++ b/solution.py
@@ -290,26 +290,27 @@
     slots, part = together(slots, part)
 
     grads = sum_z(part)
-    strip = own_strip(row_growth, z_hi, mp_index)
-    rows = gather(panel_rows(slots, slot_of, z_hi, y), Z_GROUPS)
-    rows, grads, strip = together(rows, grads, strip)
+    rows = panel_rows(slots, slot_of, z_hi, y)
+    rows, grads = together(rows, grads)
 
     grad = pick(grads, z_hi).T
     grads = gather_y(grads.astype(BF))
+    strip = own_strip(row_growth, z_hi, mp_index)
+    rows = gather(rows, Z_GROUPS)
+    rows, grads, strip = together(rows, grads, strip)
+
+    back = back_block(place, row_growth, grads)
+    other = lax.ppermute(back, "dp", SWAP_ZH)
+    pair = jnp.where(z_hi == 0, jnp.stack([back, other]), jnp.stack([other, back]))
     strips = jnp.concatenate(gather_y(strip))
     mixed = dot(strips, tokens, NT).astype(BF)
     half = gather(rows, X_GROUPS)
-    half, grads, mixed = together(half, grads, mixed)
+    half, pair, mixed = together(half, pair, mixed)
 
     mixed = lax.all_gather(mixed, "mp", axis=0, tiled=True)
     mixed = mixed.reshape(NX * NZ, NC, NY, -1, tokens.shape[0])
-    back = back_block(place, row_growth, grads)
-    other = lax.ppermute(back, "dp", SWAP_ZH)
-    pair = jnp.where(z_hi == 0, jnp.stack([back, other]), jnp.stack([other, back]))
     source = both_cores(half)
     inners = inner_terms(place, col_growth, source)
-    inners, pair = together(inners, pair)
-
     part, pair = together(sum_y(inners), pair)
 
     inners = sum_z(part)

time: 243 us -> 242 us (level)
  waiting for transfers between devices: 107 us -> 93.5 us
  local copies, waits for them, and re-layouts: 15.3 us -> 24.2 us
  starting transfers between devices: 62.9 us -> 67.8 us
  Pallas kernels: 26.9 us -> 24.2 us
    ppermute x2, waiting for transfers between devices: 36 us -> 21.7 us  [sum_z(): return part + lax.ppermute(part.astype(BF), 'dp', SWAP_ZH).astype(F32)]
    unnamed x34 -> x62, local copies, waits for them, and re-layouts: 10.2 us -> 18.3 us
    ppermute x1, waiting for transfers between devices: 0.01 us -> 7.77 us  [own_strip(): other = lax.ppermute(mine, 'dp', SWAP_ZH)]
    all_to_all x2, starting transfers between devices: 9.29 us -> 16.2 us  [gather(): lax.all_to_all(blocks, 'mp', 0, 0, axis_index_groups=groups)]
    ppermute x1, waiting for transfers between devices: 10.8 us -> 4.03 us  [shards(): other = lax.ppermute(back, 'dp', SWAP_ZH)]
    ppermute x21, starting transfers between devices: 24.7 us -> 19.1 us  [exchange_y(): got = {k: lax.ppermute(block_for(k), 'dp', shift_y(k)) for k in (2, 1, 3)}]
    ppermute x1, waiting for transfers between devices: 0.01 us -> 4.15 us  [both_cores(): return [half, lax.ppermute(half, 'mp', SWAP_CORE)]]
    all_to_all x1, starting transfers between devices: 4.53 us -> 8.67 us  [shards(): lax.all_to_all(keep.astype(BF), 'mp', 0, 0, axis_index_groups=PLANE_GROUPS)]
  transfers between devices with their start and end apart: 32 -> 32, of which waited for: 15 -> 19; matrix products, arithmetic and copies ran while one was open for 8% -> 8% of each run, Pallas kernels for 7% -> 6%
where the time goes in v6:
time: 242 us; the launch traced here: 239 us
  waiting for transfers between devices  93.5 us (39%)
  starting transfers between devices  67.8 us (28%)
  local copies, waits for them, and re-layouts  24.2 us (10%)
  Pallas kernels  24.2 us (10%)
  between operations  14.5 us (6%)
  other arithmetic  10.1 us (4%)
  matrix products  4.93 us (2%)
    ppermute x21, waiting for transfers between devices, exchange_y(): got = {k: lax.ppermute(block_for(k), 'dp', shift_y(k)) for k in (2, 1, 3)}  42.4 us
    pallas_call x6, Pallas kernels, call(): pl.pallas_call(body, out_shape=outs, grid=specs.get('grid', ()), in_specs...  24.2 us
    ppermute x2, waiting for transfers between devices, sum_z(): return part + lax.ppermute(part.astype(BF), 'dp', SWAP_ZH).astype(F32)  21.7 us
    ppermute x21, starting transfers between devices, exchange_y(): got = {k: lax.ppermute(block_for(k), 'dp', shift_y(k)) for k in (2, 1, 3)}  19.1 us
    unnamed x62, local copies, waits for them, and re-layouts  18.3 us
    all_to_all x2, starting transfers between devices, gather(): lax.all_to_all(blocks, 'mp', 0, 0, axis_index_groups=groups)  16.2 us
    all_to_all x1, starting transfers between devices, panel_slots(): return lax.all_to_all(mine, 'mp', 0, 0)  9.09 us
    all_to_all x1, starting transfers between devices, shards(): lax.all_to_all(keep.astype(BF), 'mp', 0, 0, axis_index_groups=PLANE_GROUPS)  8.67 us
  transfers between devices with their start and end apart: 32, of which 19 were waited for; matrix products, arithmetic and copies ran while one was open for 8% of the time, Pallas kernels for 6%

profile of v6, /device:TPU:30, one launch (start us, length us, event | category | flops | bytes accessed | tf_op | source)
XLA Modules:
  0.0 239.1 jit_solution(13417003885125025513)
XLA Ops:
  10.9 5.5 %shard_map.93 = (f32[2,320,320]{2,1,0:T(8,128)S(1)}, bf16[2,320,320]{2,1,0:T(8,128)(2,1)}, bf16[2,320,320]{2,1,0:T(8,128)(2,1)}, bf16[2,320,320]{2,1,0:T(8,128)(2,1)S(1)}) custom-call(s32[4]{0:T(128)S(1)} %pad_add_fusion.place, bf16[1024,2560]{1,0:T(8,128)(2,1)S(1)} %copy-done.2, bf16[320,1024]{1,0:T(8,128)(2,1)S(1)} %bitcast.86), custom_call_target="tpu_custom_call" | custom-call | flops 1677721600 | bytes 7946240 | tf_op jit(solution)/shard_map/pallas_call | solution.py:43
  16.6 2.6 %collective-permute-start.1 = (bf16[2,320,320]{2,1,0:T(8,128)(2,1)}, bf16[2,320,320]{2,1,0:T(8,128)(2,1)}, u32[]{:S(2)}, u32[]{:S(2)}) collective-permute-start(bf16[2,320,320]{2,1,0:T(8,128)(2,1)} %get-tuple-element.38), channel_id=1, source_target_pairs={{0,64},{32,96},{64,0},{96,32},{128,192},{160,224},{192,128},{224,1... | collective-permute-start | bytes 1228808 | tf_op jit(solution)/shard_map/ppermute | solution.py:229
  20.0 9.1 %all-to-all-start = ((bf16[32,16,256]{2,1,0:T(8,128)(2,1)}), bf16[32,16,256]{2,1,0:T(8,128)(2,1)}, u32[]{:S(2)}, u32[]{:S(2)}) async-start(bf16[32,16,256]{2,1,0:T(8,128)(2,1)} %bitcast.7), calls=%async_computation | async-start | bytes 524288 | tf_op jit(solution)/shard_map/all_to_all | solution.py:251
  32.6 9.2 %collective-permute-done.2 = bf16[2,320,320]{2,1,0:T(8,128)(2,1)} collective-permute-done((bf16[2,320,320]{2,1,0:T(8,128)(2,1)S(1)}, bf16[2,320,320]{2,1,0:T(8,128)(2,1)}, u32[]{:S(2)}, u32[]{:S(2)}) %collective-permute-start.2) | collective-permute-done | bytes 409632 | tf_op jit(solution)/shard_map/ppermute | solution.py:229
  44.1 7.2 %collective-permute-start.6 = (bf16[2,320,320]{2,1,0:T(8,128)(2,1)}, bf16[2,320,320]{2,1,0:T(8,128)(2,1)}, u32[]{:S(2)}, u32[]{:S(2)}) collective-permute-start(bf16[2,320,320]{2,1,0:T(8,128)(2,1)} %convert_element_type.51), channel_id=1, source_target_pairs={{0,128},{32,160},{64,192},{96,224},{128,0},{160,32},{192,64},{224,... | collective-permute-start | bytes 1228808 | tf_op jit(solution)/shard_map/ppermute | solution.py:239
  60.9 3.2 %collective-permute-done.5 = bf16[4,16,256]{2,1,0:T(8,128)(2,1)S(1)} collective-permute-done((bf16[4,16,256]{2,1,0:T(8,128)(2,1)S(1)}, bf16[4,16,256]{2,1,0:T(8,128)(2,1)S(1)}, u32[]{:S(2)}, u32[]{:S(2)}) %collective-permute-start.5) | collective-permute-done | bytes 32800 | tf_op jit(solution)/shard_map/ppermute | solution.py:229
  67.4 11.4 %all-to-all-start.1 = ((bf16[4,64,1024]{2,1,0:T(8,128)(2,1)}), bf16[4,64,1024]{2,1,0:T(8,128)(2,1)S(1)}, u32[]{:S(2)}, u32[]{:S(2)}) async-start(bf16[4,64,1024]{2,1,0:T(8,128)(2,1)} %broadcast_in_dim.27), calls=%async_computation.1 | async-start | bytes 1048576 | tf_op jit(solution)/shard_map/all_to_all | solution.py:266
  79.7 5.4 %collective-permute-start.10 = (bf16[16,2560]{1,0:T(8,128)(2,1)S(1)}, bf16[16,2560]{1,0:T(8,128)(2,1)S(1)}, u32[]{:S(2)}, u32[]{:S(2)}) collective-permute-start(bf16[16,2560]{1,0:T(8,128)(2,1)S(1)} %dynamic-slice_bitcast_fusion.2), channel_id=1, source_target_pairs={{0,128},{32,160},{64,192},{96,224},{128,0},{160,32},{192,64},{224,... | collective-permute-start | bytes 245768 | tf_op jit(solution)/shard_map/ppermute | solution.py:277
  88.0 7.8 %collective-permute-done.10 = bf16[16,2560]{1,0:T(8,128)(2,1)S(1)} collective-permute-done((bf16[16,2560]{1,0:T(8,128)(2,1)S(1)}, bf16[16,2560]{1,0:T(8,128)(2,1)S(1)}, u32[]{:S(2)}, u32[]{:S(2)}) %collective-permute-start.10) | collective-permute-done | bytes 81952 | tf_op jit(solution)/shard_map/ppermute | solution.py:277
  96.7 2.7 %collective-permute-done.7.refs_1_ = bf16[2,320,320]{2,1,0:T(8,128)(2,1)S(1)} collective-permute-done((bf16[2,320,320]{2,1,0:T(8,128)(2,1)S(1)}, bf16[2,320,320]{2,1,0:T(8,128)(2,1)S(1)}, u32[]{:S(2)}, u32[]{:S(2)}) %collective-permute-start.7) | collective-permute-done | bytes 409632 | tf_op jit(solution)/shard_map/ppermute | solution.py:229
  101.8 7.0 %collective-permute-done.9.refs_3_ = bf16[2,320,320]{2,1,0:T(8,128)(2,1)S(1)} collective-permute-done((bf16[2,320,320]{2,1,0:T(8,128)(2,1)S(1)}, bf16[2,320,320]{2,1,0:T(8,128)(2,1)S(1)}, u32[]{:S(2)}, u32[]{:S(2)}) %collective-permute-start.9) | collective-permute-done | bytes 409632 | tf_op jit(solution)/shard_map/ppermute | solution.py:229
  111.2 4.8 %all-to-all-start.2 = ((bf16[4,256,1024]{2,1,0:T(8,128)(2,1)}), bf16[4,256,1024]{2,1,0:T(8,128)(2,1)S(1)}, u32[]{:S(2)}, u32[]{:S(2)}) async-start(bf16[4,256,1024]{2,1,0:T(8,128)(2,1)} %broadcast_in_dim.28), calls=%async_computation.2 | async-start | bytes 4194304 | tf_op jit(solution)/shard_map/all_to_all | solution.py:266
  126.6 4.9 %convolution_convert_fusion = bf16[64,1024]{1,0:T(8,128)(2,1)} fusion(bf16[1024,2560]{1,0:T(8,128)(2,1)} %tokens.1, bf16[16,2560]{1,0:T(8,128)(2,1)} %collective-permute-done.14, bf16[16,2560]{1,0:T(8,128)(2,1)} %collective-permute-done.13, bf16[16,2560]{1,0:T(8,128)(2,1)S(1)} %collective-permute-done.12, bf16[16,2560]{1,0:T(8,128)(2,1)S(1)} %broadcast_select_fusion.1), kind=kOutput, calls=%fused_computation.3 | convolution fusion | flops 336920576 | bytes 5701632 | tf_op jit(solution)/shard_map/dot_general | solution.py:26
  131.5 4.0 %collective-permute-done.11 = bf16[320,256]{1,0:T(8,128)(2,1)} collective-permute-done((bf16[320,256]{1,0:T(8,128)(2,1)S(1)}, bf16[320,256]{1,0:T(8,128)(2,1)}, u32[]{:S(2)}, u32[]{:S(2)}) %collective-permute-start.11) | collective-permute-done | bytes 163872 | tf_op jit(solution)/shard_map/ppermute | solution.py:303
  137.3 3.1 %all-to-all-done.2 = bf16[4,256,1024]{2,1,0:T(8,128)(2,1)S(1)} async-done(((bf16[4,256,1024]{2,1,0:T(8,128)(2,1)}), bf16[4,256,1024]{2,1,0:T(8,128)(2,1)S(1)}, u32[]{:S(2)}, u32[]{:S(2)}) %all-to-all-start.2) | async-done | bytes 2097184 | tf_op jit(solution)/shard_map/all_to_all | solution.py:266
  140.6 4.1 %collective-permute-done.15.other = bf16[1024,1024]{1,0:T(8,128)(2,1)S(1)} collective-permute-done((bf16[1024,1024]{1,0:T(8,128)(2,1)S(1)}, bf16[1024,1024]{1,0:T(8,128)(2,1)S(1)}, u32[]{:S(2)}, u32[]{:S(2)}) %collective-permute-start.15) | collective-permute-done | bytes 2097184 | tf_op jit(solution)/shard_map/ppermute | solution.py:270
  145.8 4.9 %shard_map.95 = (f32[2,320,256]{2,1,0:T(8,128)S(1)}, bf16[2,320,256]{2,1,0:T(8,128)(2,1)S(1)}, bf16[2,320,256]{2,1,0:T(8,128)(2,1)S(1)}, bf16[2,320,256]{2,1,0:T(8,128)(2,1)S(1)}) custom-call(s32[4]{0:T(128)S(1)} %pad_add_fusion.place, bf16[320,1024]{1,0:T(8,128)(2,1)S(1)} %copy-done.20, bf16[1024,1024]{1,0:T(8,128)(2,1)S(1)} %bitcast.83, ...), custom_call_target="tpu_custom_call" | custom-call | flops 1342177280 | bytes 6488064 | tf_op jit(solution)/shard_map/pallas_call | solution.py:43
  153.4 7.9 %collective-permute-done.16 = bf16[2,320,256]{2,1,0:T(8,128)(2,1)S(1)} collective-permute-done((bf16[2,320,256]{2,1,0:T(8,128)(2,1)S(1)}, bf16[2,320,256]{2,1,0:T(8,128)(2,1)S(1)}, u32[]{:S(2)}, u32[]{:S(2)}) %collective-permute-start.16) | collective-permute-done | bytes 327712 | tf_op jit(solution)/shard_map/ppermute | solution.py:229
  163.0 6.2 %collective-permute-done.18 = bf16[2,320,256]{2,1,0:T(8,128)(2,1)S(1)} collective-permute-done((bf16[2,320,256]{2,1,0:T(8,128)(2,1)S(1)}, bf16[2,320,256]{2,1,0:T(8,128)(2,1)S(1)}, u32[]{:S(2)}, u32[]{:S(2)}) %collective-permute-start.18) | collective-permute-done | bytes 327712 | tf_op jit(solution)/shard_map/ppermute | solution.py:229
  173.1 21.4 %collective-permute-done.19 = bf16[2,320,256]{2,1,0:T(8,128)(2,1)S(1)} collective-permute-done((bf16[2,320,256]{2,1,0:T(8,128)(2,1)S(1)}, bf16[2,320,256]{2,1,0:T(8,128)(2,1)S(1)}, u32[]{:S(2)}, u32[]{:S(2)}) %collective-permute-start.19) | collective-permute-done | bytes 327712 | tf_op jit(solution)/shard_map/ppermute | solution.py:239
  200.3 8.7 %all-to-all-start.3 = ((bf16[16,80,256]{2,1,0:T(8,128)(2,1)}), bf16[16,80,256]{2,1,0:T(8,128)(2,1)S(1)}, u32[]{:S(2)}, u32[]{:S(2)}) async-start(bf16[16,80,256]{2,1,0:T(8,128)(2,1)} %add_convert_fusion), calls=%async_computation.3 | async-start | bytes 1310720 | tf_op jit(solution)/shard_map/all_to_all | solution.py:323
  212.3 5.7 %shard_map.96 = f32[320,1024]{1,0:T(8,128)} custom-call(s32[4]{0:T(128)} %copy-done.18, bf16[1024,1024]{1,0:T(8,128)(2,1)} %bitcast.84, bf16[1024,1024]{1,0:T(8,128)(2,1)} %copy-done.8, bf16[2,320,256]{2,1,0:T(8,128)(2,1)} %maximum_select_fusion.refs_0_, bf16[2,320,256]{2,1,0:T(8,128)(2,1)} %copy-done.26, bf16[2,320,256]{2,1,0:T(8,128)(2,1)} %copy-done.27, ...), custom_call_target="tpu_custom_call" | custom-call | flops 1342177280 | bytes 6815744 | tf_op jit(solution)/shard_map/pallas_call | solution.py:43
  218.0 8.3 %all-to-all-done.3 = bf16[16,80,256]{2,1,0:T(8,128)(2,1)S(1)} async-done(((bf16[16,80,256]{2,1,0:T(8,128)(2,1)}), bf16[16,80,256]{2,1,0:T(8,128)(2,1)S(1)}, u32[]{:S(2)}, u32[]{:S(2)}) %all-to-all-start.3) | async-done | bytes 655392 | tf_op jit(solution)/shard_map/all_to_all | solution.py:323
  227.0 5.3 %shard_map.97 = bf16[320,1024]{1,0:T(8,128)(2,1)} custom-call(s32[4]{0:T(128)} %copy-done.18, bf16[16,2,4,16,1024]{4,3,2,1,0:T(8,128)(2,1)} %bitcast.87, bf16[2,320,256]{2,1,0:T(8,128)(2,1)} %copy-done.23, bf16[2,320,256]{2,1,0:T(8,128)(2,1)} %collective-permute-done.23.refs_1_, bf16[2,320,256]{2,1,0:T(8,128)(2,1)} %collective-permute-done.24.refs_2_, ...), custom_call_target="tpu_custom_call" | custom-call | flops 1342177280 | bytes 6160384 | tf_op jit(solution)/shard_map/pallas_call | solution.py:43
  (137 shorter events, 64.3 us)
Async XLA Ops:
  16.5 14.3 %collective-permute-start = (bf16[2,320,320]{2,1,0:T(8,128)(2,1)}, bf16[2,320,320]{2,1,0:T(8,128)(2,1)S(1)}, u32[]{:S(2)}, u32[]{:S(2)}) collective-permute-start(bf16[2,320,320]{2,1,0:T(8,128)(2,1)} %get-tuple-element.37), channel_id=1, source_target_pairs={{0,32},{32,64},{64,96},{96,0},{128,160},{160,192},{192,224},{224,1... | collective-permute-start | bytes 1228808 | tf_op jit(solution)/shard_map/ppermute | solution.py:229
  16.6 16.0 %collective-permute-start.1 = (bf16[2,320,320]{2,1,0:T(8,128)(2,1)}, bf16[2,320,320]{2,1,0:T(8,128)(2,1)}, u32[]{:S(2)}, u32[]{:S(2)}) collective-permute-start(bf16[2,320,320]{2,1,0:T(8,128)(2,1)} %get-tuple-element.38), channel_id=1, source_target_pairs={{0,64},{32,96},{64,0},{96,32},{128,192},{160,224},{192,128},{224,1... | collective-permute-start | bytes 1228808 | tf_op jit(solution)/shard_map/ppermute | solution.py:229
  19.2 22.6 %collective-permute-start.2 = (bf16[2,320,320]{2,1,0:T(8,128)(2,1)S(1)}, bf16[2,320,320]{2,1,0:T(8,128)(2,1)}, u32[]{:S(2)}, u32[]{:S(2)}) collective-permute-start(bf16[2,320,320]{2,1,0:T(8,128)(2,1)S(1)} %get-tuple-element.39), channel_id=1, source_target_pairs={{0,96},{32,0},{64,32},{96,64},{128,224},{160,128},{192,160},{224,1... | collective-permute-start | bytes 1228808 | tf_op jit(solution)/shard_map/ppermute | solution.py:229
  20.0 23.3 %all-to-all-start = ((bf16[32,16,256]{2,1,0:T(8,128)(2,1)}), bf16[32,16,256]{2,1,0:T(8,128)(2,1)}, u32[]{:S(2)}, u32[]{:S(2)}) async-start(bf16[32,16,256]{2,1,0:T(8,128)(2,1)} %bitcast.7), calls=%async_computation | async-start | bytes 524288 | tf_op jit(solution)/shard_map/all_to_all | solution.py:251
  44.1 21.2 %collective-permute-start.6 = (bf16[2,320,320]{2,1,0:T(8,128)(2,1)}, bf16[2,320,320]{2,1,0:T(8,128)(2,1)}, u32[]{:S(2)}, u32[]{:S(2)}) collective-permute-start(bf16[2,320,320]{2,1,0:T(8,128)(2,1)} %convert_element_type.51), channel_id=1, source_target_pairs={{0,128},{32,160},{64,192},{96,224},{128,0},{160,32},{192,64},{224,... | collective-permute-start | bytes 1228808 | tf_op jit(solution)/shard_map/ppermute | solution.py:239
  67.4 42.2 %all-to-all-start.1 = ((bf16[4,64,1024]{2,1,0:T(8,128)(2,1)}), bf16[4,64,1024]{2,1,0:T(8,128)(2,1)S(1)}, u32[]{:S(2)}, u32[]{:S(2)}) async-start(bf16[4,64,1024]{2,1,0:T(8,128)(2,1)} %broadcast_in_dim.27), calls=%async_computation.1 | async-start | bytes 1048576 | tf_op jit(solution)/shard_map/all_to_all | solution.py:266
  79.7 16.1 %collective-permute-start.10 = (bf16[16,2560]{1,0:T(8,128)(2,1)S(1)}, bf16[16,2560]{1,0:T(8,128)(2,1)S(1)}, u32[]{:S(2)}, u32[]{:S(2)}) collective-permute-start(bf16[16,2560]{1,0:T(8,128)(2,1)S(1)} %dynamic-slice_bitcast_fusion.2), channel_id=1, source_target_pairs={{0,128},{32,160},{64,192},{96,224},{128,0},{160,32},{192,64},{224,... | collective-permute-start | bytes 245768 | tf_op jit(solution)/shard_map/ppermute | solution.py:277
  85.1 14.2 %collective-permute-start.7 = (bf16[2,320,320]{2,1,0:T(8,128)(2,1)S(1)}, bf16[2,320,320]{2,1,0:T(8,128)(2,1)S(1)}, u32[]{:S(2)}, u32[]{:S(2)}) collective-permute-start(bf16[2,320,320]{2,1,0:T(8,128)(2,1)S(1)} %convert_element_type.53.refs_0_), channel_id=1, source_target_pairs={{0,32},{32,64},{64,96},{96,0},{128,160},{160,192},{192,224},{224,1... | collective-permute-start | bytes 1228808 | tf_op jit(solution)/shard_map/ppermute | solution.py:229
  85.3 15.7 %collective-permute-start.8 = (bf16[2,320,320]{2,1,0:T(8,128)(2,1)S(1)}, bf16[2,320,320]{2,1,0:T(8,128)(2,1)S(1)}, u32[]{:S(2)}, u32[]{:S(2)}) collective-permute-start(bf16[2,320,320]{2,1,0:T(8,128)(2,1)S(1)} %convert_element_type.53.refs_0_), channel_id=1, source_target_pairs={{0,64},{32,96},{64,0},{96,32},{128,192},{160,224},{192,128},{224,1... | collective-permute-start | bytes 1228808 | tf_op jit(solution)/shard_map/ppermute | solution.py:229
  86.9 21.9 %collective-permute-start.9 = (bf16[2,320,320]{2,1,0:T(8,128)(2,1)S(1)}, bf16[2,320,320]{2,1,0:T(8,128)(2,1)S(1)}, u32[]{:S(2)}, u32[]{:S(2)}) collective-permute-start(bf16[2,320,320]{2,1,0:T(8,128)(2,1)S(1)} %convert_element_type.53.refs_0_), channel_id=1, source_target_pairs={{0,96},{32,0},{64,32},{96,64},{128,224},{160,128},{192,160},{224,1... | collective-permute-start | bytes 1228808 | tf_op jit(solution)/shard_map/ppermute | solution.py:229
  111.2 29.2 %all-to-all-start.2 = ((bf16[4,256,1024]{2,1,0:T(8,128)(2,1)}), bf16[4,256,1024]{2,1,0:T(8,128)(2,1)S(1)}, u32[]{:S(2)}, u32[]{:S(2)}) async-start(bf16[4,256,1024]{2,1,0:T(8,128)(2,1)} %broadcast_in_dim.28), calls=%async_computation.2 | async-start | bytes 4194304 | tf_op jit(solution)/shard_map/all_to_all | solution.py:266
  116.0 111.0 %all-gather.2.cloned.1.call-start = ((), (), s32[]{:S(2)}) async-start(), calls=%async_computation.4 | async-start | bytes 4325376 | tf_op jit(solution)/shard_map/all_gather | solution.py:310
  116.0 10.6 %collective-permute-start.12 = (bf16[16,2560]{1,0:T(8,128)(2,1)S(1)}, bf16[16,2560]{1,0:T(8,128)(2,1)S(1)}, u32[]{:S(2)}, u32[]{:S(2)}) collective-permute-start(bf16[16,2560]{1,0:T(8,128)(2,1)S(1)} %broadcast_select_fusion.1), channel_id=1, source_target_pairs={{0,32},{32,64},{64,96},{96,0},{128,160},{160,192},{192,224},{224,1... | collective-permute-start | bytes 245768 | tf_op jit(solution)/shard_map/ppermute | solution.py:229
  150.7 10.6 %collective-permute-start.16 = (bf16[2,320,256]{2,1,0:T(8,128)(2,1)S(1)}, bf16[2,320,256]{2,1,0:T(8,128)(2,1)S(1)}, u32[]{:S(2)}, u32[]{:S(2)}) collective-permute-start(bf16[2,320,256]{2,1,0:T(8,128)(2,1)S(1)} %get-tuple-element.53), channel_id=1, source_target_pairs={{0,32},{32,64},{64,96},{96,0},{128,160},{160,192},{192,224},{224,1... | collective-permute-start | bytes 983048 | tf_op jit(solution)/shard_map/ppermute | solution.py:229
  150.8 12.2 %collective-permute-start.17 = (bf16[2,320,256]{2,1,0:T(8,128)(2,1)S(1)}, bf16[2,320,256]{2,1,0:T(8,128)(2,1)S(1)}, u32[]{:S(2)}, u32[]{:S(2)}) collective-permute-start(bf16[2,320,256]{2,1,0:T(8,128)(2,1)S(1)} %get-tuple-element.54), channel_id=1, source_target_pairs={{0,64},{32,96},{64,0},{96,32},{128,192},{160,224},{192,128},{224,1... | collective-permute-start | bytes 983048 | tf_op jit(solution)/shard_map/ppermute | solution.py:229
  152.1 17.0 %collective-permute-start.18 = (bf16[2,320,256]{2,1,0:T(8,128)(2,1)S(1)}, bf16[2,320,256]{2,1,0:T(8,128)(2,1)S(1)}, u32[]{:S(2)}, u32[]{:S(2)}) collective-permute-start(bf16[2,320,256]{2,1,0:T(8,128)(2,1)S(1)} %get-tuple-element.55), channel_id=1, source_target_pairs={{0,96},{32,0},{64,32},{96,64},{128,224},{160,128},{192,160},{224,1... | collective-permute-start | bytes 983048 | tf_op jit(solution)/shard_map/ppermute | solution.py:229
  169.4 25.2 %collective-permute-start.19 = (bf16[2,320,256]{2,1,0:T(8,128)(2,1)S(1)}, bf16[2,320,256]{2,1,0:T(8,128)(2,1)S(1)}, u32[]{:S(2)}, u32[]{:S(2)}) collective-permute-start(bf16[2,320,256]{2,1,0:T(8,128)(2,1)S(1)} %convert_element_type.58), channel_id=1, source_target_pairs={{0,128},{32,160},{64,192},{96,224},{128,0},{160,32},{192,64},{224,... | collective-permute-start | bytes 983048 | tf_op jit(solution)/shard_map/ppermute | solution.py:239
  170.4 24.2 %collective-permute-start.20 = (bf16[2,320,256]{2,1,0:T(8,128)(2,1)S(1)}, bf16[2,320,256]{2,1,0:T(8,128)(2,1)S(1)}, u32[]{:S(2)}, u32[]{:S(2)}) collective-permute-start(bf16[2,320,256]{2,1,0:T(8,128)(2,1)S(1)} %copy-done.24), channel_id=1, source_target_pairs={{0,32},{32,64},{64,96},{96,0},{128,160},{160,192},{192,224},{224,1... | collective-permute-start | bytes 983048 | tf_op jit(solution)/shard_map/ppermute | solution.py:229
  171.5 23.2 %collective-permute-start.21 = (bf16[2,320,256]{2,1,0:T(8,128)(2,1)S(1)}, bf16[2,320,256]{2,1,0:T(8,128)(2,1)S(1)}, u32[]{:S(2)}, u32[]{:S(2)}) collective-permute-start(bf16[2,320,256]{2,1,0:T(8,128)(2,1)S(1)} %copy-done.24), channel_id=1, source_target_pairs={{0,64},{32,96},{64,0},{96,32},{128,192},{160,224},{192,128},{224,1... | collective-permute-start | bytes 983048 | tf_op jit(solution)/shard_map/ppermute | solution.py:229
  172.3 22.4 %collective-permute-start.22 = (bf16[2,320,256]{2,1,0:T(8,128)(2,1)S(1)}, bf16[2,320,256]{2,1,0:T(8,128)(2,1)}, u32[]{:S(2)}, u32[]{:S(2)}) collective-permute-start(bf16[2,320,256]{2,1,0:T(8,128)(2,1)S(1)} %copy-done.24), channel_id=1, source_target_pairs={{0,96},{32,0},{64,32},{96,64},{128,224},{160,128},{192,160},{224,1... | collective-permute-start | bytes 983048 | tf_op jit(solution)/shard_map/ppermute | solution.py:229
  200.3 26.0 %all-to-all-start.3 = ((bf16[16,80,256]{2,1,0:T(8,128)(2,1)}), bf16[16,80,256]{2,1,0:T(8,128)(2,1)S(1)}, u32[]{:S(2)}, u32[]{:S(2)}) async-start(bf16[16,80,256]{2,1,0:T(8,128)(2,1)} %add_convert_fusion), calls=%async_computation.3 | async-start | bytes 1310720 | tf_op jit(solution)/shard_map/all_to_all | solution.py:323
  208.9 18.1 %collective-permute-start.23 = (bf16[2,320,256]{2,1,0:T(8,128)(2,1)S(1)}, bf16[2,320,256]{2,1,0:T(8,128)(2,1)}, u32[]{:S(2)}, u32[]{:S(2)}) collective-permute-start(bf16[2,320,256]{2,1,0:T(8,128)(2,1)S(1)} %convert_add_fusion.2.refs_0_), channel_id=1, source_target_pairs={{0,32},{32,64},{64,96},{96,0},{128,160},{160,192},{192,224},{224,1... | collective-permute-start | bytes 983048 | tf_op jit(solution)/shard_map/ppermute | solution.py:229
  209.4 17.6 %collective-permute-start.24 = (bf16[2,320,256]{2,1,0:T(8,128)(2,1)S(1)}, bf16[2,320,256]{2,1,0:T(8,128)(2,1)}, u32[]{:S(2)}, u32[]{:S(2)}) collective-permute-start(bf16[2,320,256]{2,1,0:T(8,128)(2,1)S(1)} %convert_add_fusion.2.refs_0_), channel_id=1, source_target_pairs={{0,64},{32,96},{64,0},{96,32},{128,192},{160,224},{192,128},{224,1... | collective-permute-start | bytes 983048 | tf_op jit(solution)/shard_map/ppermute | solution.py:229
  210.2 16.9 %collective-permute-start.25 = (bf16[2,320,256]{2,1,0:T(8,128)(2,1)S(1)}, bf16[2,320,256]{2,1,0:T(8,128)(2,1)}, u32[]{:S(2)}, u32[]{:S(2)}) collective-permute-start(bf16[2,320,256]{2,1,0:T(8,128)(2,1)S(1)} %convert_add_fusion.2.refs_0_), channel_id=1, source_target_pairs={{0,96},{32,0},{64,32},{96,64},{128,224},{160,128},{192,160},{224,1... | collective-permute-start | bytes 983048 | tf_op jit(solution)/shard_map/ppermute | solution.py:229
  (37 other events, 460.6 us)
Sparse Core Ops, SparseCore 0:
  140.6 71.6 all-gather.1

commit v7 on v5

--- a/solution.py
+++ b/solution.py
@@ -89,6 +89,7 @@
     full = pl.BlockSpec(shape, lambda s: (0, 0, 0))
     return call(
         grad_body, place, (tokens, cot), outs, 2 * tokens.size * hidden,
+        limit=56,
         grid=(ZH * NY // 2,),
         in_specs=[
             pl.BlockSpec((tokens.shape[0], 2 * n), lambda s: (0, s)),
@@ -113,7 +114,7 @@
     hidden, old = grads[0].shape[1], row_growth.shape[1]
     return call(
         back_body, place, (row_growth, *grads), struct((hidden, old), BF),
-        2 * row_growth.size * hidden,
+        2 * row_growth.size * hidden, limit=56,
     )
 
 
@@ -193,7 +194,7 @@
     shape = (NX * NZ, n * ZH * NY // MP, old)
     return call(
         row_body, place, (inner, *grads), [struct(shape, F32), struct(shape, BF)],
-        2 * inner.size * n * ZH * NY,
+        2 * inner.size * n * ZH * NY, limit=56,
     )
 
 
@@ -290,8 +291,11 @@
     slots, part = together(slots, part)
 
     grads = sum_z(part)
+    rows = panel_rows(slots, slot_of, z_hi, y)
+    rows, grads = together(rows, grads)
+
     strip = own_strip(row_growth, z_hi, mp_index)
-    rows = gather(panel_rows(slots, slot_of, z_hi, y), Z_GROUPS)
+    rows = gather(rows, Z_GROUPS)
     rows, grads, strip = together(rows, grads, strip)
 
     grad = pick(grads, z_hi).T
@@ -303,13 +307,11 @@
 
     mixed = lax.all_gather(mixed, "mp", axis=0, tiled=True)
     mixed = mixed.reshape(NX * NZ, NC, NY, -1, tokens.shape[0])
+    source = both_cores(half)
+    inners = inner_terms(place, col_growth, source)
     back = back_block(place, row_growth, grads)
     other = lax.ppermute(back, "dp", SWAP_ZH)
     pair = jnp.where(z_hi == 0, jnp.stack([back, other]), jnp.stack([other, back]))
-    source = both_cores(half)
-    inners = inner_terms(place, col_growth, source)
-    inners, pair = together(inners, pair)
-
     part, pair = together(sum_y(inners), pair)
 
     inners = sum_z(part)

time: 243 us -> 243 us (level)
  waiting for transfers between devices: 107 us -> 82.3 us
  starting transfers between devices: 62.9 us -> 78.7 us
  other arithmetic: 8.59 us -> 14.2 us
  Pallas kernels: 26.9 us -> 31 us
    ppermute x2, waiting for transfers between devices: 36 us -> 13.8 us  [sum_z(): return part + lax.ppermute(part.astype(BF), 'dp', SWAP_ZH).astype(F32)]
    ppermute x21, waiting for transfers between devices: 43.8 us -> 32.1 us  [exchange_y(): got = {k: lax.ppermute(block_for(k), 'dp', shift_y(k)) for k in (2, 1, 3)}]
    ppermute x1, waiting for transfers between devices: 0.01 us -> 10.7 us  [own_strip(): other = lax.ppermute(mine, 'dp', SWAP_ZH)]
    all_to_all x2, starting transfers between devices: 9.29 us -> 16.2 us  [gather(): lax.all_to_all(blocks, 'mp', 0, 0, axis_index_groups=groups)]
    all_to_all x2, waiting for transfers between devices: 6.64 us -> 0.01 us  [gather(): lax.all_to_all(blocks, 'mp', 0, 0, axis_index_groups=groups)]
    ppermute x2, starting transfers between devices: 4.25 us -> 10.8 us  [sum_z(): return part + lax.ppermute(part.astype(BF), 'dp', SWAP_ZH).astype(F32)]
    ppermute x1, waiting for transfers between devices: 0.01 us -> 4.15 us  [both_cores(): return [half, lax.ppermute(half, 'mp', SWAP_CORE)]]
    pallas_call x6, Pallas kernels: 26.9 us -> 31 us  [call(): pl.pallas_call(body, out_shape=outs, grid=specs.get('grid', ()), in_specs...]
  transfers between devices with their start and end apart: 32 -> 32, of which waited for: 15 -> 18; matrix products, arithmetic and copies ran while one was open for 8% -> 10% of each run, Pallas kernels for 7% -> 8%
where the time goes in v7:
time: 243 us; the launch traced here: 240 us
  waiting for transfers between devices  82.3 us (34%)
  starting transfers between devices  78.7 us (32%)
  Pallas kernels  31 us (13%)
  local copies, waits for them, and re-layouts  14.6 us (6%)
  between operations  14.4 us (6%)
  other arithmetic  14.2 us (6%)
  matrix products  4.83 us (2%)
    ppermute x21, waiting for transfers between devices, exchange_y(): got = {k: lax.ppermute(block_for(k), 'dp', shift_y(k)) for k in (2, 1, 3)}  32.1 us
    pallas_call x6, Pallas kernels, call(): pl.pallas_call(body, out_shape=outs, grid=specs.get('grid', ()), in_specs...  31 us
    ppermute x21, starting transfers between devices, exchange_y(): got = {k: lax.ppermute(block_for(k), 'dp', shift_y(k)) for k in (2, 1, 3)}  25.7 us
    all_to_all x2, starting transfers between devices, gather(): lax.all_to_all(blocks, 'mp', 0, 0, axis_index_groups=groups)  16.2 us
    ppermute x2, waiting for transfers between devices, sum_z(): return part + lax.ppermute(part.astype(BF), 'dp', SWAP_ZH).astype(F32)  13.8 us
    ppermute x1, waiting for transfers between devices, shards(): other = lax.ppermute(back, 'dp', SWAP_ZH)  12.5 us
    ppermute x2, starting transfers between devices, sum_z(): return part + lax.ppermute(part.astype(BF), 'dp', SWAP_ZH).astype(F32)  10.8 us
    ppermute x1, waiting for transfers between devices, own_strip(): other = lax.ppermute(mine, 'dp', SWAP_ZH)  10.7 us
  transfers between devices with their start and end apart: 32, of which 18 were waited for; matrix products, arithmetic and copies ran while one was open for 10% of the time, Pallas kernels for 8%

profile of v7, /device:TPU:30, one launch (start us, length us, event | category | flops | bytes accessed | tf_op | source)
XLA Modules:
  0.0 240.1 jit_solution(16761771969866897915)
XLA Ops:
  7.8 7.1 %shard_map.93 = (f32[2,320,320]{2,1,0:T(8,128)}, bf16[2,320,320]{2,1,0:T(8,128)(2,1)}, bf16[2,320,320]{2,1,0:T(8,128)(2,1)}, bf16[2,320,320]{2,1,0:T(8,128)(2,1)}) custom-call(s32[4]{0:T(128)} %pad_add_fusion.place, bf16[1024,2560]{1,0:T(8,128)(2,1)} %tokens.1, bf16[320,1024]{1,0:T(8,128)(2,1)} %bitcast.96), custom_call_target="tpu_custom_call" | custom-call | flops 1677721600 | bytes 7946240 | tf_op jit(solution)/shard_map/pallas_call | solution.py:43
  18.4 9.1 %all-to-all-start = ((bf16[32,16,256]{2,1,0:T(8,128)(2,1)}), bf16[32,16,256]{2,1,0:T(8,128)(2,1)}, u32[]{:S(2)}, u32[]{:S(2)}) async-start(bf16[32,16,256]{2,1,0:T(8,128)(2,1)} %bitcast.7), calls=%async_computation | async-start | bytes 524288 | tf_op jit(solution)/shard_map/all_to_all | solution.py:252
  31.0 9.3 %collective-permute-done.2 = bf16[2,320,320]{2,1,0:T(8,128)(2,1)S(1)} collective-permute-done((bf16[2,320,320]{2,1,0:T(8,128)(2,1)}, bf16[2,320,320]{2,1,0:T(8,128)(2,1)S(1)}, u32[]{:S(2)}, u32[]{:S(2)}) %collective-permute-start.2) | collective-permute-done | bytes 409632 | tf_op jit(solution)/shard_map/ppermute | solution.py:230
  43.3 7.2 %collective-permute-start.6 = (bf16[2,320,320]{2,1,0:T(8,128)(2,1)}, bf16[2,320,320]{2,1,0:T(8,128)(2,1)}, u32[]{:S(2)}, u32[]{:S(2)}) collective-permute-start(bf16[2,320,320]{2,1,0:T(8,128)(2,1)} %convert_element_type.51), channel_id=1, source_target_pairs={{0,128},{32,160},{64,192},{96,224},{128,0},{160,32},{192,64},{224,... | collective-permute-start | bytes 1228808 | tf_op jit(solution)/shard_map/ppermute | solution.py:240
  60.2 3.0 %collective-permute-done.5 = bf16[4,16,256]{2,1,0:T(8,128)(2,1)S(1)} collective-permute-done((bf16[4,16,256]{2,1,0:T(8,128)(2,1)S(1)}, bf16[4,16,256]{2,1,0:T(8,128)(2,1)S(1)}, u32[]{:S(2)}, u32[]{:S(2)}) %collective-permute-start.5) | collective-permute-done | bytes 32800 | tf_op jit(solution)/shard_map/ppermute | solution.py:230
  67.3 11.4 %all-to-all-start.1 = ((bf16[4,64,1024]{2,1,0:T(8,128)(2,1)}), bf16[4,64,1024]{2,1,0:T(8,128)(2,1)S(1)}, u32[]{:S(2)}, u32[]{:S(2)}) async-start(bf16[4,64,1024]{2,1,0:T(8,128)(2,1)} %broadcast_in_dim.27), calls=%async_computation.1 | async-start | bytes 1048576 | tf_op jit(solution)/shard_map/all_to_all | solution.py:267
  79.7 5.4 %collective-permute-start.7 = (bf16[16,2560]{1,0:T(8,128)(2,1)S(1)}, bf16[16,2560]{1,0:T(8,128)(2,1)S(1)}, u32[]{:S(2)}, u32[]{:S(2)}) collective-permute-start(bf16[16,2560]{1,0:T(8,128)(2,1)S(1)} %dynamic-slice_bitcast_fusion.2), channel_id=1, source_target_pairs={{0,128},{32,160},{64,192},{96,224},{128,0},{160,32},{192,64},{224,... | collective-permute-start | bytes 245768 | tf_op jit(solution)/shard_map/ppermute | solution.py:278
  85.0 10.7 %collective-permute-done.7 = bf16[16,2560]{1,0:T(8,128)(2,1)S(1)} collective-permute-done((bf16[16,2560]{1,0:T(8,128)(2,1)S(1)}, bf16[16,2560]{1,0:T(8,128)(2,1)S(1)}, u32[]{:S(2)}, u32[]{:S(2)}) %collective-permute-start.7) | collective-permute-done | bytes 81952 | tf_op jit(solution)/shard_map/ppermute | solution.py:278
  98.3 4.8 %all-to-all-start.2 = ((bf16[4,256,1024]{2,1,0:T(8,128)(2,1)}), bf16[4,256,1024]{2,1,0:T(8,128)(2,1)S(1)}, u32[]{:S(2)}, u32[]{:S(2)}) async-start(bf16[4,256,1024]{2,1,0:T(8,128)(2,1)} %broadcast_in_dim.28), calls=%async_computation.2 | async-start | bytes 4194304 | tf_op jit(solution)/shard_map/all_to_all | solution.py:267
  113.3 4.8 %convolution_convert_fusion = bf16[64,1024]{1,0:T(8,128)(2,1)} fusion(bf16[1024,2560]{1,0:T(8,128)(2,1)} %tokens.1, bf16[16,2560]{1,0:T(8,128)(2,1)S(1)} %collective-permute-done.13, bf16[16,2560]{1,0:T(8,128)(2,1)S(1)} %collective-permute-done.12, bf16[16,2560]{1,0:T(8,128)(2,1)S(1)} %collective-permute-done.11, bf16[16,2560]{1,0:T(8,128)(2,1)S(1)} %broadcast_select_fusion.1), kind=kOutput, calls=%fused_computation.3 | convolution fusion | flops 336920576 | bytes 5701632 | tf_op jit(solution)/shard_map/dot_general | solution.py:26
  118.1 5.4 %collective-permute-done.10.refs_3_ = bf16[2,320,320]{2,1,0:T(8,128)(2,1)} collective-permute-done((bf16[2,320,320]{2,1,0:T(8,128)(2,1)}, bf16[2,320,320]{2,1,0:T(8,128)(2,1)}, u32[]{:S(2)}, u32[]{:S(2)}) %collective-permute-start.10) | collective-permute-done | bytes 409632 | tf_op jit(solution)/shard_map/ppermute | solution.py:230
  123.7 8.0 %collective-permute-done.9.refs_2_ = bf16[2,320,320]{2,1,0:T(8,128)(2,1)} collective-permute-done((bf16[2,320,320]{2,1,0:T(8,128)(2,1)}, bf16[2,320,320]{2,1,0:T(8,128)(2,1)}, u32[]{:S(2)}, u32[]{:S(2)}) %collective-permute-start.9) | collective-permute-done | bytes 409632 | tf_op jit(solution)/shard_map/ppermute | solution.py:230
  131.8 4.1 %collective-permute-done.14.other = bf16[1024,1024]{1,0:T(8,128)(2,1)S(1)} collective-permute-done((bf16[1024,1024]{1,0:T(8,128)(2,1)S(1)}, bf16[1024,1024]{1,0:T(8,128)(2,1)S(1)}, u32[]{:S(2)}, u32[]{:S(2)}) %collective-permute-start.14) | collective-permute-done | bytes 2097184 | tf_op jit(solution)/shard_map/ppermute | solution.py:271
  137.1 5.7 %shard_map.94 = (f32[2,320,256]{2,1,0:T(8,128)S(1)}, bf16[2,320,256]{2,1,0:T(8,128)(2,1)}, bf16[2,320,256]{2,1,0:T(8,128)(2,1)}, bf16[2,320,256]{2,1,0:T(8,128)(2,1)S(1)}) custom-call(s32[4]{0:T(128)S(1)} %copy-done.5, bf16[320,1024]{1,0:T(8,128)(2,1)S(1)} %copy-done.6, bf16[1024,1024]{1,0:T(8,128)(2,1)S(1)} %bitcast.83, ...), custom_call_target="tpu_custom_call" | custom-call | flops 1342177280 | bytes 6488064 | tf_op jit(solution)/shard_map/pallas_call | solution.py:43
  146.4 3.5 %shard_map.95 = bf16[320,256]{1,0:T(8,128)(2,1)} custom-call(s32[4]{0:T(128)} %pad_add_fusion.place, bf16[2560,256]{1,0:T(8,128)(2,1)} %grown.1, bf16[2,320,320]{2,1,0:T(8,128)(2,1)} %convert_element_type.53.refs_0_, bf16[2,320,320]{2,1,0:T(8,128)(2,1)} %collective-permute-done.8.refs_1_, bf16[2,320,320]{2,1,0:T(8,128)(2,1)} %collective-permute-done.9.refs_2_, ...), custom_call_target="tpu_custom_call" | custom-call | flops 419430400 | bytes 3112960 | tf_op jit(solution)/shard_map/pallas_call | solution.py:43
  149.9 4.7 %collective-permute-start.18 = (bf16[320,256]{1,0:T(8,128)(2,1)}, bf16[320,256]{1,0:T(8,128)(2,1)S(1)}, u32[]{:S(2)}, u32[]{:S(2)}) collective-permute-start(bf16[320,256]{1,0:T(8,128)(2,1)} %shard_map.95), channel_id=1, source_target_pairs={{0,128},{32,160},{64,192},{96,224},{128,0},{160,32},{192,64},{224,... | collective-permute-start | bytes 491528 | tf_op jit(solution)/shard_map/ppermute | solution.py:313
  154.6 12.5 %collective-permute-done.18 = bf16[320,256]{1,0:T(8,128)(2,1)S(1)} collective-permute-done((bf16[320,256]{1,0:T(8,128)(2,1)}, bf16[320,256]{1,0:T(8,128)(2,1)S(1)}, u32[]{:S(2)}, u32[]{:S(2)}) %collective-permute-start.18) | collective-permute-done | bytes 163872 | tf_op jit(solution)/shard_map/ppermute | solution.py:313
  169.2 3.6 %collective-permute-start.19 = (bf16[2,320,256]{2,1,0:T(8,128)(2,1)S(1)}, bf16[2,320,256]{2,1,0:T(8,128)(2,1)S(1)}, u32[]{:S(2)}, u32[]{:S(2)}) collective-permute-start(bf16[2,320,256]{2,1,0:T(8,128)(2,1)S(1)} %convert_element_type.58), channel_id=1, source_target_pairs={{0,128},{32,160},{64,192},{96,224},{128,0},{160,32},{192,64},{224,... | collective-permute-start | bytes 983048 | tf_op jit(solution)/shard_map/ppermute | solution.py:240
  177.0 13.5 %collective-permute-done.19 = bf16[2,320,256]{2,1,0:T(8,128)(2,1)S(1)} collective-permute-done((bf16[2,320,256]{2,1,0:T(8,128)(2,1)S(1)}, bf16[2,320,256]{2,1,0:T(8,128)(2,1)S(1)}, u32[]{:S(2)}, u32[]{:S(2)}) %collective-permute-start.19) | collective-permute-done | bytes 327712 | tf_op jit(solution)/shard_map/ppermute | solution.py:240
  193.5 3.7 %shard_map.98 = (f32[16,80,256]{2,1,0:T(8,128)}, bf16[16,80,256]{2,1,0:T(8,128)(2,1)}) custom-call(s32[4]{0:T(128)} %pad_add_fusion.place, bf16[320,256]{1,0:T(8,128)(2,1)} %dynamic-slice_bitcast_fusion.1.inner, bf16[2,320,320]{2,1,0:T(8,128)(2,1)} %convert_element_type.53.refs_0_, bf16[2,320,320]{2,1,0:T(8,128)(2,1)} %collective-permute-done.8.refs_1_, ...), custom_call_target="tpu_custom_call" | custom-call | flops 419430400 | bytes 3768320 | tf_op jit(solution)/shard_map/pallas_call | solution.py:43
  202.0 6.7 %all-to-all-start.3 = ((bf16[16,80,256]{2,1,0:T(8,128)(2,1)}), bf16[16,80,256]{2,1,0:T(8,128)(2,1)S(1)}, u32[]{:S(2)}, u32[]{:S(2)}) async-start(bf16[16,80,256]{2,1,0:T(8,128)(2,1)} %add_convert_fusion), calls=%async_computation.3 | async-start | bytes 1310720 | tf_op jit(solution)/shard_map/all_to_all | solution.py:324
  213.6 5.7 %shard_map.96 = f32[320,1024]{1,0:T(8,128)} custom-call(s32[4]{0:T(128)} %pad_add_fusion.place, bf16[1024,1024]{1,0:T(8,128)(2,1)} %bitcast.84, bf16[1024,1024]{1,0:T(8,128)(2,1)} %copy-done.2, bf16[2,320,256]{2,1,0:T(8,128)(2,1)} %copy-done.10, bf16[2,320,256]{2,1,0:T(8,128)(2,1)} %copy-done.15, bf16[2,320,256]{2,1,0:T(8,128)(2,1)} %copy-done.16, ...), custom_call_target="tpu_custom_call" | custom-call | flops 1342177280 | bytes 6815744 | tf_op jit(solution)/shard_map/pallas_call | solution.py:43
  219.3 6.7 %all-to-all-done.3 = bf16[16,80,256]{2,1,0:T(8,128)(2,1)S(1)} async-done(((bf16[16,80,256]{2,1,0:T(8,128)(2,1)}), bf16[16,80,256]{2,1,0:T(8,128)(2,1)S(1)}, u32[]{:S(2)}, u32[]{:S(2)}) %all-to-all-start.3) | async-done | bytes 655392 | tf_op jit(solution)/shard_map/all_to_all | solution.py:324
  227.9 5.3 %shard_map.97 = bf16[320,1024]{1,0:T(8,128)(2,1)} custom-call(s32[4]{0:T(128)} %pad_add_fusion.place, bf16[16,2,4,16,1024]{4,3,2,1,0:T(8,128)(2,1)} %bitcast.85, bf16[2,320,256]{2,1,0:T(8,128)(2,1)} %copy-done.9, bf16[2,320,256]{2,1,0:T(8,128)(2,1)} %collective-permute-done.23.refs_1_, bf16[2,320,256]{2,1,0:T(8,128)(2,1)} %collective-permute-done.24.refs_2_, ...), custom_call_target="tpu_custom_call" | custom-call | flops 1342177280 | bytes 6160384 | tf_op jit(solution)/shard_map/pallas_call | solution.py:43
  (119 shorter events, 63.8 us)
Async XLA Ops:
  14.9 14.3 %collective-permute-start = (bf16[2,320,320]{2,1,0:T(8,128)(2,1)}, bf16[2,320,320]{2,1,0:T(8,128)(2,1)S(1)}, u32[]{:S(2)}, u32[]{:S(2)}) collective-permute-start(bf16[2,320,320]{2,1,0:T(8,128)(2,1)} %get-tuple-element.37), channel_id=1, source_target_pairs={{0,32},{32,64},{64,96},{96,0},{128,160},{160,192},{192,224},{224,1... | collective-permute-start | bytes 1228808 | tf_op jit(solution)/shard_map/ppermute | solution.py:230
  15.1 15.9 %collective-permute-start.1 = (bf16[2,320,320]{2,1,0:T(8,128)(2,1)}, bf16[2,320,320]{2,1,0:T(8,128)(2,1)S(1)}, u32[]{:S(2)}, u32[]{:S(2)}) collective-permute-start(bf16[2,320,320]{2,1,0:T(8,128)(2,1)} %get-tuple-element.38), channel_id=1, source_target_pairs={{0,64},{32,96},{64,0},{96,32},{128,192},{160,224},{192,128},{224,1... | collective-permute-start | bytes 1228808 | tf_op jit(solution)/shard_map/ppermute | solution.py:230
  17.7 22.6 %collective-permute-start.2 = (bf16[2,320,320]{2,1,0:T(8,128)(2,1)}, bf16[2,320,320]{2,1,0:T(8,128)(2,1)S(1)}, u32[]{:S(2)}, u32[]{:S(2)}) collective-permute-start(bf16[2,320,320]{2,1,0:T(8,128)(2,1)} %get-tuple-element.39), channel_id=1, source_target_pairs={{0,96},{32,0},{64,32},{96,64},{128,224},{160,128},{192,160},{224,1... | collective-permute-start | bytes 1228808 | tf_op jit(solution)/shard_map/ppermute | solution.py:230
  18.4 24.0 %all-to-all-start = ((bf16[32,16,256]{2,1,0:T(8,128)(2,1)}), bf16[32,16,256]{2,1,0:T(8,128)(2,1)}, u32[]{:S(2)}, u32[]{:S(2)}) async-start(bf16[32,16,256]{2,1,0:T(8,128)(2,1)} %bitcast.7), calls=%async_computation | async-start | bytes 524288 | tf_op jit(solution)/shard_map/all_to_all | solution.py:252
  43.3 21.2 %collective-permute-start.6 = (bf16[2,320,320]{2,1,0:T(8,128)(2,1)}, bf16[2,320,320]{2,1,0:T(8,128)(2,1)}, u32[]{:S(2)}, u32[]{:S(2)}) collective-permute-start(bf16[2,320,320]{2,1,0:T(8,128)(2,1)} %convert_element_type.51), channel_id=1, source_target_pairs={{0,128},{32,160},{64,192},{96,224},{128,0},{160,32},{192,64},{224,... | collective-permute-start | bytes 1228808 | tf_op jit(solution)/shard_map/ppermute | solution.py:240
  67.3 29.3 %all-to-all-start.1 = ((bf16[4,64,1024]{2,1,0:T(8,128)(2,1)}), bf16[4,64,1024]{2,1,0:T(8,128)(2,1)S(1)}, u32[]{:S(2)}, u32[]{:S(2)}) async-start(bf16[4,64,1024]{2,1,0:T(8,128)(2,1)} %broadcast_in_dim.27), calls=%async_computation.1 | async-start | bytes 1048576 | tf_op jit(solution)/shard_map/all_to_all | solution.py:267
  79.7 16.1 %collective-permute-start.7 = (bf16[16,2560]{1,0:T(8,128)(2,1)S(1)}, bf16[16,2560]{1,0:T(8,128)(2,1)S(1)}, u32[]{:S(2)}, u32[]{:S(2)}) collective-permute-start(bf16[16,2560]{1,0:T(8,128)(2,1)S(1)} %dynamic-slice_bitcast_fusion.2), channel_id=1, source_target_pairs={{0,128},{32,160},{64,192},{96,224},{128,0},{160,32},{192,64},{224,... | collective-permute-start | bytes 245768 | tf_op jit(solution)/shard_map/ppermute | solution.py:278
  98.3 33.4 %all-to-all-start.2 = ((bf16[4,256,1024]{2,1,0:T(8,128)(2,1)}), bf16[4,256,1024]{2,1,0:T(8,128)(2,1)S(1)}, u32[]{:S(2)}, u32[]{:S(2)}) async-start(bf16[4,256,1024]{2,1,0:T(8,128)(2,1)} %broadcast_in_dim.28), calls=%async_computation.2 | async-start | bytes 4194304 | tf_op jit(solution)/shard_map/all_to_all | solution.py:267
  103.1 123.6 %all-gather.2.cloned.1.call-start = ((), (), s32[]{:S(2)}) async-start(), calls=%async_computation.4 | async-start | bytes 4325376 | tf_op jit(solution)/shard_map/all_gather | solution.py:308
  107.5 16.1 %collective-permute-start.10 = (bf16[2,320,320]{2,1,0:T(8,128)(2,1)}, bf16[2,320,320]{2,1,0:T(8,128)(2,1)}, u32[]{:S(2)}, u32[]{:S(2)}) collective-permute-start(bf16[2,320,320]{2,1,0:T(8,128)(2,1)} %convert_element_type.53.refs_0_), channel_id=1, source_target_pairs={{0,96},{32,0},{64,32},{96,64},{128,224},{160,128},{192,160},{224,1... | collective-permute-start | bytes 1228808 | tf_op jit(solution)/shard_map/ppermute | solution.py:230
  109.2 14.5 %collective-permute-start.8 = (bf16[2,320,320]{2,1,0:T(8,128)(2,1)}, bf16[2,320,320]{2,1,0:T(8,128)(2,1)}, u32[]{:S(2)}, u32[]{:S(2)}) collective-permute-start(bf16[2,320,320]{2,1,0:T(8,128)(2,1)} %convert_element_type.53.refs_0_), channel_id=1, source_target_pairs={{0,32},{32,64},{64,96},{96,0},{128,160},{160,192},{192,224},{224,1... | collective-permute-start | bytes 1228808 | tf_op jit(solution)/shard_map/ppermute | solution.py:230
  110.7 21.0 %collective-permute-start.9 = (bf16[2,320,320]{2,1,0:T(8,128)(2,1)}, bf16[2,320,320]{2,1,0:T(8,128)(2,1)}, u32[]{:S(2)}, u32[]{:S(2)}) collective-permute-start(bf16[2,320,320]{2,1,0:T(8,128)(2,1)} %convert_element_type.53.refs_0_), channel_id=1, source_target_pairs={{0,64},{32,96},{64,0},{96,32},{128,192},{160,224},{192,128},{224,1... | collective-permute-start | bytes 1228808 | tf_op jit(solution)/shard_map/ppermute | solution.py:230
  143.6 25.3 %collective-permute-start.15 = (bf16[2,320,256]{2,1,0:T(8,128)(2,1)}, bf16[2,320,256]{2,1,0:T(8,128)(2,1)S(1)}, u32[]{:S(2)}, u32[]{:S(2)}) collective-permute-start(bf16[2,320,256]{2,1,0:T(8,128)(2,1)} %get-tuple-element.50), channel_id=1, source_target_pairs={{0,32},{32,64},{64,96},{96,0},{128,160},{160,192},{192,224},{224,1... | collective-permute-start | bytes 983048 | tf_op jit(solution)/shard_map/ppermute | solution.py:230
  145.0 24.0 %collective-permute-start.16 = (bf16[2,320,256]{2,1,0:T(8,128)(2,1)}, bf16[2,320,256]{2,1,0:T(8,128)(2,1)S(1)}, u32[]{:S(2)}, u32[]{:S(2)}) collective-permute-start(bf16[2,320,256]{2,1,0:T(8,128)(2,1)} %get-tuple-element.51), channel_id=1, source_target_pairs={{0,64},{32,96},{64,0},{96,32},{128,192},{160,224},{192,128},{224,1... | collective-permute-start | bytes 983048 | tf_op jit(solution)/shard_map/ppermute | solution.py:230
  146.4 22.6 %collective-permute-start.17 = (bf16[2,320,256]{2,1,0:T(8,128)(2,1)S(1)}, bf16[2,320,256]{2,1,0:T(8,128)(2,1)S(1)}, u32[]{:S(2)}, u32[]{:S(2)}) collective-permute-start(bf16[2,320,256]{2,1,0:T(8,128)(2,1)S(1)} %get-tuple-element.52), channel_id=1, source_target_pairs={{0,96},{32,0},{64,32},{96,64},{128,224},{160,128},{192,160},{224,1... | collective-permute-start | bytes 983048 | tf_op jit(solution)/shard_map/ppermute | solution.py:230
  149.9 17.2 %collective-permute-start.18 = (bf16[320,256]{1,0:T(8,128)(2,1)}, bf16[320,256]{1,0:T(8,128)(2,1)S(1)}, u32[]{:S(2)}, u32[]{:S(2)}) collective-permute-start(bf16[320,256]{1,0:T(8,128)(2,1)} %shard_map.95), channel_id=1, source_target_pairs={{0,128},{32,160},{64,192},{96,224},{128,0},{160,32},{192,64},{224,... | collective-permute-start | bytes 491528 | tf_op jit(solution)/shard_map/ppermute | solution.py:313
  169.2 21.4 %collective-permute-start.19 = (bf16[2,320,256]{2,1,0:T(8,128)(2,1)S(1)}, bf16[2,320,256]{2,1,0:T(8,128)(2,1)S(1)}, u32[]{:S(2)}, u32[]{:S(2)}) collective-permute-start(bf16[2,320,256]{2,1,0:T(8,128)(2,1)S(1)} %convert_element_type.58), channel_id=1, source_target_pairs={{0,128},{32,160},{64,192},{96,224},{128,0},{160,32},{192,64},{224,... | collective-permute-start | bytes 983048 | tf_op jit(solution)/shard_map/ppermute | solution.py:240
  172.7 17.9 %collective-permute-start.20 = (bf16[2,320,256]{2,1,0:T(8,128)(2,1)S(1)}, bf16[2,320,256]{2,1,0:T(8,128)(2,1)S(1)}, u32[]{:S(2)}, u32[]{:S(2)}) collective-permute-start(bf16[2,320,256]{2,1,0:T(8,128)(2,1)S(1)} %maximum_select_fusion.refs_0_), channel_id=1, source_target_pairs={{0,32},{32,64},{64,96},{96,0},{128,160},{160,192},{192,224},{224,1... | collective-permute-start | bytes 983048 | tf_op jit(solution)/shard_map/ppermute | solution.py:230
  175.5 15.2 %collective-permute-start.21 = (bf16[2,320,256]{2,1,0:T(8,128)(2,1)S(1)}, bf16[2,320,256]{2,1,0:T(8,128)(2,1)S(1)}, u32[]{:S(2)}, u32[]{:S(2)}) collective-permute-start(bf16[2,320,256]{2,1,0:T(8,128)(2,1)S(1)} %maximum_select_fusion.refs_0_), channel_id=1, source_target_pairs={{0,64},{32,96},{64,0},{96,32},{128,192},{160,224},{192,128},{224,1... | collective-permute-start | bytes 983048 | tf_op jit(solution)/shard_map/ppermute | solution.py:230
  176.1 16.0 %collective-permute-start.22 = (bf16[2,320,256]{2,1,0:T(8,128)(2,1)S(1)}, bf16[2,320,256]{2,1,0:T(8,128)(2,1)S(1)}, u32[]{:S(2)}, u32[]{:S(2)}) collective-permute-start(bf16[2,320,256]{2,1,0:T(8,128)(2,1)S(1)} %maximum_select_fusion.refs_0_), channel_id=1, source_target_pairs={{0,96},{32,0},{64,32},{96,64},{128,224},{160,128},{192,160},{224,1... | collective-permute-start | bytes 983048 | tf_op jit(solution)/shard_map/ppermute | solution.py:230
  202.0 24.0 %all-to-all-start.3 = ((bf16[16,80,256]{2,1,0:T(8,128)(2,1)}), bf16[16,80,256]{2,1,0:T(8,128)(2,1)S(1)}, u32[]{:S(2)}, u32[]{:S(2)}) async-start(bf16[16,80,256]{2,1,0:T(8,128)(2,1)} %add_convert_fusion), calls=%async_computation.3 | async-start | bytes 1310720 | tf_op jit(solution)/shard_map/all_to_all | solution.py:324
  208.6 18.0 %collective-permute-start.23 = (bf16[2,320,256]{2,1,0:T(8,128)(2,1)S(1)}, bf16[2,320,256]{2,1,0:T(8,128)(2,1)}, u32[]{:S(2)}, u32[]{:S(2)}) collective-permute-start(bf16[2,320,256]{2,1,0:T(8,128)(2,1)S(1)} %convert_add_fusion.2.refs_0_), channel_id=1, source_target_pairs={{0,32},{32,64},{64,96},{96,0},{128,160},{160,192},{192,224},{224,1... | collective-permute-start | bytes 983048 | tf_op jit(solution)/shard_map/ppermute | solution.py:230
  210.1 16.6 %collective-permute-start.24 = (bf16[2,320,256]{2,1,0:T(8,128)(2,1)S(1)}, bf16[2,320,256]{2,1,0:T(8,128)(2,1)}, u32[]{:S(2)}, u32[]{:S(2)}) collective-permute-start(bf16[2,320,256]{2,1,0:T(8,128)(2,1)S(1)} %convert_add_fusion.2.refs_0_), channel_id=1, source_target_pairs={{0,64},{32,96},{64,0},{96,32},{128,192},{160,224},{192,128},{224,1... | collective-permute-start | bytes 983048 | tf_op jit(solution)/shard_map/ppermute | solution.py:230
  211.4 16.6 %collective-permute-start.25 = (bf16[2,320,256]{2,1,0:T(8,128)(2,1)S(1)}, bf16[2,320,256]{2,1,0:T(8,128)(2,1)}, u32[]{:S(2)}, u32[]{:S(2)}) collective-permute-start(bf16[2,320,256]{2,1,0:T(8,128)(2,1)S(1)} %convert_add_fusion.2.refs_0_), channel_id=1, source_target_pairs={{0,96},{32,0},{64,32},{96,64},{128,224},{160,128},{192,160},{224,1... | collective-permute-start | bytes 983048 | tf_op jit(solution)/shard_map/ppermute | solution.py:230
  (28 other events, 238.1 us)
Sparse Core Ops, SparseCore 0:
  131.9 80.0 all-gather.1

commit v8 on v7

--- a/solution.py
+++ b/solution.py
@@ -194,7 +194,7 @@
     shape = (NX * NZ, n * ZH * NY // MP, old)
     return call(
         row_body, place, (inner, *grads), [struct(shape, F32), struct(shape, BF)],
-        2 * inner.size * n * ZH * NY, limit=56,
+        2 * inner.size * n * ZH * NY,
     )
 
 
@@ -254,8 +254,8 @@
 
 def panel_rows(slots, slot_of, z_hi, y):
     sub, width = slots.shape[1:]
-    panels = jnp.take(slots, slot_of, axis=0).reshape(ZH, NY, -1, sub, width)
-    panels = pick(panels, z_hi)
+    mine = lax.dynamic_slice_in_dim(slot_of, z_hi * (MP // ZH), MP // ZH)
+    panels = jnp.take(slots, mine, axis=0).reshape(NY, -1, sub, width)
     got = exchange_y(lambda k: pick(panels, (y + k) % NY))
     got[0] = pick(panels, y)
     chunk = jnp.stack([choose((y - j) % NY, got) for j in range(NY)])
@@ -288,19 +288,19 @@
 
     slots = panel_slots(saved_panels, y)
     part = sum_y(grad_terms(place, tokens, cotangent.T))
-    slots, part = together(slots, part)
+    strip = own_strip(row_growth, z_hi, mp_index)
+    slots, part, strip = together(slots, part, strip)
 
     grads = sum_z(part)
     rows = panel_rows(slots, slot_of, z_hi, y)
-    rows, grads = together(rows, grads)
-
-    strip = own_strip(row_growth, z_hi, mp_index)
+    rows, grads, strip = together(rows, grads, strip)
+
+    strips = jnp.concatenate(gather_y(strip))
     rows = gather(rows, Z_GROUPS)
-    rows, grads, strip = together(rows, grads, strip)
+    rows, grads, strips = together(rows, grads, strips)
 
     grad = pick(grads, z_hi).T
     grads = gather_y(grads.astype(BF))
-    strips = jnp.concatenate(gather_y(strip))
     mixed = dot(strips, tokens, NT).astype(BF)
     half = gather(rows, X_GROUPS)
     half, grads, mixed = together(half, grads, mixed)

time: 243 us -> 235 us (0.967)
  starting transfers between devices: 78.7 us -> 74.5 us
  local copies, waits for them, and re-layouts: 14.6 us -> 11.7 us
    ppermute x1, waiting for transfers between devices: 10.7 us -> 0.01 us  [own_strip(): other = lax.ppermute(mine, 'dp', SWAP_ZH)]
    ppermute x2, waiting for transfers between devices: 13.8 us -> 20.5 us  [sum_z(): return part + lax.ppermute(part.astype(BF), 'dp', SWAP_ZH).astype(F32)]
    ppermute x21, starting transfers between devices: 25.7 us -> 29 us  [exchange_y(): got = {k: lax.ppermute(block_for(k), 'dp', shift_y(k)) for k in (2, 1, 3)}]
    ppermute x1, starting transfers between devices: 4.7 us -> 1.56 us  [shards(): other = lax.ppermute(back, 'dp', SWAP_ZH)]
    all_to_all x1, starting transfers between devices: 9.09 us -> 6.34 us  [panel_slots(): return lax.all_to_all(mine, 'mp', 0, 0)]
    ppermute x2, starting transfers between devices: 10.8 us -> 8.31 us  [sum_z(): return part + lax.ppermute(part.astype(BF), 'dp', SWAP_ZH).astype(F32)]
    unnamed x44 -> x42, local copies, waits for them, and re-layouts: 8.17 us -> 7.48 us
  transfers between devices with their start and end apart: 32 -> 32, of which waited for: 18 -> 18; matrix products, arithmetic and copies ran while one was open for 10% -> 9% of each run, Pallas kernels for 8% -> 8%
where the time goes in v8:
time: 235 us; the launch traced here: 231 us
  waiting for transfers between devices  83.6 us (36%)
  starting transfers between devices  74.5 us (32%)
  Pallas kernels  29.9 us (13%)
  between operations  14.4 us (6%)
  other arithmetic  12.4 us (5%)
  local copies, waits for them, and re-layouts  11.7 us (5%)
  matrix products  4.84 us (2%)
    ppermute x21, waiting for transfers between devices, exchange_y(): got = {k: lax.ppermute(block_for(k), 'dp', shift_y(k)) for k in (2, 1, 3)}  31.3 us
    pallas_call x6, Pallas kernels, call(): pl.pallas_call(body, out_shape=outs, grid=specs.get('grid', ()), in_specs...  29.9 us
    ppermute x21, starting transfers between devices, exchange_y(): got = {k: lax.ppermute(block_for(k), 'dp', shift_y(k)) for k in (2, 1, 3)}  29 us
    ppermute x2, waiting for transfers between devices, sum_z(): return part + lax.ppermute(part.astype(BF), 'dp', SWAP_ZH).astype(F32)  20.5 us
    all_to_all x2, starting transfers between devices, gather(): lax.all_to_all(blocks, 'mp', 0, 0, axis_index_groups=groups)  15 us
    ppermute x1, waiting for transfers between devices, shards(): other = lax.ppermute(back, 'dp', SWAP_ZH)  14.6 us
    ppermute x2, starting transfers between devices, sum_z(): return part + lax.ppermute(part.astype(BF), 'dp', SWAP_ZH).astype(F32)  8.31 us
    unnamed x42, local copies, waits for them, and re-layouts  7.48 us
  transfers between devices with their start and end apart: 32, of which 18 were waited for; matrix products, arithmetic and copies ran while one was open for 9% of the time, Pallas kernels for 8%

profile of v8, /device:TPU:30, one launch (start us, length us, event | category | flops | bytes accessed | tf_op | source)
XLA Modules:
  0.0 231.4 jit_solution(13387469033721118686)
XLA Ops:
  7.9 7.2 %shard_map.93 = (f32[2,320,320]{2,1,0:T(8,128)}, bf16[2,320,320]{2,1,0:T(8,128)(2,1)}, bf16[2,320,320]{2,1,0:T(8,128)(2,1)}, bf16[2,320,320]{2,1,0:T(8,128)(2,1)}) custom-call(s32[4]{0:T(128)} %pad_add_fusion.place, bf16[1024,2560]{1,0:T(8,128)(2,1)} %tokens.1, bf16[320,1024]{1,0:T(8,128)(2,1)} %bitcast.100), custom_call_target="tpu_custom_call" | custom-call | flops 1677721600 | bytes 7946240 | tf_op jit(solution)/shard_map/pallas_call | solution.py:43
  15.3 2.6 %collective-permute-start.1 = (bf16[2,320,320]{2,1,0:T(8,128)(2,1)}, bf16[2,320,320]{2,1,0:T(8,128)(2,1)}, u32[]{:S(2)}, u32[]{:S(2)}) collective-permute-start(bf16[2,320,320]{2,1,0:T(8,128)(2,1)} %get-tuple-element.40), channel_id=1, source_target_pairs={{0,64},{32,96},{64,0},{96,32},{128,192},{160,224},{192,128},{224,1... | collective-permute-start | bytes 1228808 | tf_op jit(solution)/shard_map/ppermute | solution.py:230
  20.4 7.2 %collective-permute-start.3 = (bf16[16,2560]{1,0:T(8,128)(2,1)S(1)}, bf16[16,2560]{1,0:T(8,128)(2,1)S(1)}, u32[]{:S(2)}, u32[]{:S(2)}) collective-permute-start(bf16[16,2560]{1,0:T(8,128)(2,1)S(1)} %dynamic-slice_bitcast_fusion.2), channel_id=1, source_target_pairs={{0,128},{32,160},{64,192},{96,224},{128,0},{160,32},{192,64},{224,... | collective-permute-start | bytes 245768 | tf_op jit(solution)/shard_map/ppermute | solution.py:278
  28.4 6.3 %all-to-all-start = ((bf16[32,16,256]{2,1,0:T(8,128)(2,1)}), bf16[32,16,256]{2,1,0:T(8,128)(2,1)S(1)}, u32[]{:S(2)}, u32[]{:S(2)}) async-start(bf16[32,16,256]{2,1,0:T(8,128)(2,1)} %bitcast.8), calls=%async_computation | async-start | bytes 524288 | tf_op jit(solution)/shard_map/all_to_all | solution.py:252
  35.9 4.5 %collective-permute-done.2 = bf16[2,320,320]{2,1,0:T(8,128)(2,1)} collective-permute-done((bf16[2,320,320]{2,1,0:T(8,128)(2,1)}, bf16[2,320,320]{2,1,0:T(8,128)(2,1)}, u32[]{:S(2)}, u32[]{:S(2)}) %collective-permute-start.2) | collective-permute-done | bytes 409632 | tf_op jit(solution)/shard_map/ppermute | solution.py:230
  44.4 5.6 %collective-permute-start.7 = (bf16[2,320,320]{2,1,0:T(8,128)(2,1)}, bf16[2,320,320]{2,1,0:T(8,128)(2,1)S(1)}, u32[]{:S(2)}, u32[]{:S(2)}) collective-permute-start(bf16[2,320,320]{2,1,0:T(8,128)(2,1)} %convert_element_type.51), channel_id=1, source_target_pairs={{0,128},{32,160},{64,192},{96,224},{128,0},{160,32},{192,64},{224,... | collective-permute-start | bytes 1228808 | tf_op jit(solution)/shard_map/ppermute | solution.py:240
  56.4 3.1 %collective-permute-done.6 = bf16[4,16,256]{2,1,0:T(8,128)(2,1)S(1)} collective-permute-done((bf16[4,16,256]{2,1,0:T(8,128)(2,1)S(1)}, bf16[4,16,256]{2,1,0:T(8,128)(2,1)S(1)}, u32[]{:S(2)}, u32[]{:S(2)}) %collective-permute-start.6) | collective-permute-done | bytes 32800 | tf_op jit(solution)/shard_map/ppermute | solution.py:230
  59.7 8.2 %collective-permute-done.7 = bf16[2,320,320]{2,1,0:T(8,128)(2,1)S(1)} collective-permute-done((bf16[2,320,320]{2,1,0:T(8,128)(2,1)}, bf16[2,320,320]{2,1,0:T(8,128)(2,1)S(1)}, u32[]{:S(2)}, u32[]{:S(2)}) %collective-permute-start.7) | collective-permute-done | bytes 409632 | tf_op jit(solution)/shard_map/ppermute | solution.py:240
  69.8 7.3 %all-to-all-start.1 = ((bf16[4,64,1024]{2,1,0:T(8,128)(2,1)}), bf16[4,64,1024]{2,1,0:T(8,128)(2,1)S(1)}, u32[]{:S(2)}, u32[]{:S(2)}) async-start(bf16[4,64,1024]{2,1,0:T(8,128)(2,1)} %broadcast_in_dim.30), calls=%async_computation.1 | async-start | bytes 1048576 | tf_op jit(solution)/shard_map/all_to_all | solution.py:267
  84.4 3.4 %collective-permute-done.9 = bf16[16,2560]{1,0:T(8,128)(2,1)S(1)} collective-permute-done((bf16[16,2560]{1,0:T(8,128)(2,1)S(1)}, bf16[16,2560]{1,0:T(8,128)(2,1)S(1)}, u32[]{:S(2)}, u32[]{:S(2)}) %collective-permute-start.9) | collective-permute-done | bytes 81952 | tf_op jit(solution)/shard_map/ppermute | solution.py:230
  92.5 7.8 %all-to-all-start.2 = ((bf16[4,256,1024]{2,1,0:T(8,128)(2,1)}), bf16[4,256,1024]{2,1,0:T(8,128)(2,1)S(1)}, u32[]{:S(2)}, u32[]{:S(2)}) async-start(bf16[4,256,1024]{2,1,0:T(8,128)(2,1)} %broadcast_in_dim.31), calls=%async_computation.2 | async-start | bytes 4194304 | tf_op jit(solution)/shard_map/all_to_all | solution.py:267
  106.9 4.8 %convolution_convert_fusion = bf16[64,1024]{1,0:T(8,128)(2,1)} fusion(bf16[64,2560]{1,0:T(8,128)(2,1)S(1)} %pad_maximum_fusion, bf16[1024,2560]{1,0:T(8,128)(2,1)} %tokens.1), kind=kOutput, calls=%fused_computation.3 | convolution fusion | flops 335609856 | bytes 5701632 | tf_op jit(solution)/shard_map/dot_general | solution.py:26
  111.7 13.5 %collective-permute-done.11.refs_1_ = bf16[2,320,320]{2,1,0:T(8,128)(2,1)} collective-permute-done((bf16[2,320,320]{2,1,0:T(8,128)(2,1)}, bf16[2,320,320]{2,1,0:T(8,128)(2,1)}, u32[]{:S(2)}, u32[]{:S(2)}) %collective-permute-start.11) | collective-permute-done | bytes 409632 | tf_op jit(solution)/shard_map/ppermute | solution.py:230
  125.2 3.7 %collective-permute-done.13.refs_3_ = bf16[2,320,320]{2,1,0:T(8,128)(2,1)} collective-permute-done((bf16[2,320,320]{2,1,0:T(8,128)(2,1)}, bf16[2,320,320]{2,1,0:T(8,128)(2,1)}, u32[]{:S(2)}, u32[]{:S(2)}) %collective-permute-start.13) | collective-permute-done | bytes 409632 | tf_op jit(solution)/shard_map/ppermute | solution.py:230
  129.0 4.1 %collective-permute-done.14.other = bf16[1024,1024]{1,0:T(8,128)(2,1)S(1)} collective-permute-done((bf16[1024,1024]{1,0:T(8,128)(2,1)S(1)}, bf16[1024,1024]{1,0:T(8,128)(2,1)S(1)}, u32[]{:S(2)}, u32[]{:S(2)}) %collective-permute-start.14) | collective-permute-done | bytes 2097184 | tf_op jit(solution)/shard_map/ppermute | solution.py:271
  134.3 5.7 %shard_map.94 = (f32[2,320,256]{2,1,0:T(8,128)S(1)}, bf16[2,320,256]{2,1,0:T(8,128)(2,1)}, bf16[2,320,256]{2,1,0:T(8,128)(2,1)}, bf16[2,320,256]{2,1,0:T(8,128)(2,1)S(1)}) custom-call(s32[4]{0:T(128)S(1)} %copy-done.5, bf16[320,1024]{1,0:T(8,128)(2,1)S(1)} %copy-done.7, bf16[1024,1024]{1,0:T(8,128)(2,1)S(1)} %bitcast.88, ...), custom_call_target="tpu_custom_call" | custom-call | flops 1342177280 | bytes 6488064 | tf_op jit(solution)/shard_map/pallas_call | solution.py:43
  143.2 3.4 %shard_map.95 = bf16[320,256]{1,0:T(8,128)(2,1)} custom-call(s32[4]{0:T(128)} %pad_add_fusion.place, bf16[2560,256]{1,0:T(8,128)(2,1)} %grown.1, bf16[2,320,320]{2,1,0:T(8,128)(2,1)} %convert_element_type.53.refs_0_, bf16[2,320,320]{2,1,0:T(8,128)(2,1)} %collective-permute-done.11.refs_1_, bf16[2,320,320]{2,1,0:T(8,128)(2,1)} %collective-permute-done.12.refs_2_, ...), custom_call_target="tpu_custom_call" | custom-call | flops 419430400 | bytes 3112960 | tf_op jit(solution)/shard_map/pallas_call | solution.py:43
  148.2 14.6 %collective-permute-done.18 = bf16[320,256]{1,0:T(8,128)(2,1)S(1)} collective-permute-done((bf16[320,256]{1,0:T(8,128)(2,1)}, bf16[320,256]{1,0:T(8,128)(2,1)S(1)}, u32[]{:S(2)}, u32[]{:S(2)}) %collective-permute-start.18) | collective-permute-done | bytes 163872 | tf_op jit(solution)/shard_map/ppermute | solution.py:313
  167.5 2.7 %collective-permute-start.19 = (bf16[2,320,256]{2,1,0:T(8,128)(2,1)S(1)}, bf16[2,320,256]{2,1,0:T(8,128)(2,1)S(1)}, u32[]{:S(2)}, u32[]{:S(2)}) collective-permute-start(bf16[2,320,256]{2,1,0:T(8,128)(2,1)S(1)} %convert_element_type.58), channel_id=1, source_target_pairs={{0,128},{32,160},{64,192},{96,224},{128,0},{160,32},{192,64},{224,... | collective-permute-start | bytes 983048 | tf_op jit(solution)/shard_map/ppermute | solution.py:240
  175.4 12.3 %collective-permute-done.19 = bf16[2,320,256]{2,1,0:T(8,128)(2,1)S(1)} collective-permute-done((bf16[2,320,256]{2,1,0:T(8,128)(2,1)S(1)}, bf16[2,320,256]{2,1,0:T(8,128)(2,1)S(1)}, u32[]{:S(2)}, u32[]{:S(2)}) %collective-permute-start.19) | collective-permute-done | bytes 327712 | tf_op jit(solution)/shard_map/ppermute | solution.py:240
  193.6 6.9 %all-to-all-start.3 = ((bf16[16,80,256]{2,1,0:T(8,128)(2,1)}), bf16[16,80,256]{2,1,0:T(8,128)(2,1)S(1)}, u32[]{:S(2)}, u32[]{:S(2)}) async-start(bf16[16,80,256]{2,1,0:T(8,128)(2,1)} %add_convert_fusion), calls=%async_computation.3 | async-start | bytes 1310720 | tf_op jit(solution)/shard_map/all_to_all | solution.py:324
  204.8 5.7 %shard_map.96 = f32[320,1024]{1,0:T(8,128)} custom-call(s32[4]{0:T(128)} %pad_add_fusion.place, bf16[1024,1024]{1,0:T(8,128)(2,1)} %bitcast.89, bf16[1024,1024]{1,0:T(8,128)(2,1)} %copy-done.2, bf16[2,320,256]{2,1,0:T(8,128)(2,1)} %copy-done.11, bf16[2,320,256]{2,1,0:T(8,128)(2,1)} %copy-done.16, bf16[2,320,256]{2,1,0:T(8,128)(2,1)} %collective-permute-done.21.refs_2_, ...), custom_call_target="tpu_custom_call" | custom-call | flops 1342177280 | bytes 6815744 | tf_op jit(solution)/shard_map/pallas_call | solution.py:43
  210.5 7.2 %all-to-all-done.3 = bf16[16,80,256]{2,1,0:T(8,128)(2,1)S(1)} async-done(((bf16[16,80,256]{2,1,0:T(8,128)(2,1)}), bf16[16,80,256]{2,1,0:T(8,128)(2,1)S(1)}, u32[]{:S(2)}, u32[]{:S(2)}) %all-to-all-start.3) | async-done | bytes 655392 | tf_op jit(solution)/shard_map/all_to_all | solution.py:324
  219.3 5.3 %shard_map.97 = bf16[320,1024]{1,0:T(8,128)(2,1)} custom-call(s32[4]{0:T(128)} %pad_add_fusion.place, bf16[16,2,4,16,1024]{4,3,2,1,0:T(8,128)(2,1)} %bitcast.90, bf16[2,320,256]{2,1,0:T(8,128)(2,1)} %copy-done.10, bf16[2,320,256]{2,1,0:T(8,128)(2,1)} %collective-permute-done.23.refs_1_, bf16[2,320,256]{2,1,0:T(8,128)(2,1)} %collective-permute-done.24.refs_2_, ...), custom_call_target="tpu_custom_call" | custom-call | flops 1342177280 | bytes 6160384 | tf_op jit(solution)/shard_map/pallas_call | solution.py:43
  (119 shorter events, 63.8 us)
Async XLA Ops:
  15.1 20.8 %collective-permute-start = (bf16[2,320,320]{2,1,0:T(8,128)(2,1)}, bf16[2,320,320]{2,1,0:T(8,128)(2,1)}, u32[]{:S(2)}, u32[]{:S(2)}) collective-permute-start(bf16[2,320,320]{2,1,0:T(8,128)(2,1)} %get-tuple-element.39), channel_id=1, source_target_pairs={{0,32},{32,64},{64,96},{96,0},{128,160},{160,192},{192,224},{224,1... | collective-permute-start | bytes 1228808 | tf_op jit(solution)/shard_map/ppermute | solution.py:230
  15.3 20.6 %collective-permute-start.1 = (bf16[2,320,320]{2,1,0:T(8,128)(2,1)}, bf16[2,320,320]{2,1,0:T(8,128)(2,1)}, u32[]{:S(2)}, u32[]{:S(2)}) collective-permute-start(bf16[2,320,320]{2,1,0:T(8,128)(2,1)} %get-tuple-element.40), channel_id=1, source_target_pairs={{0,64},{32,96},{64,0},{96,32},{128,192},{160,224},{192,128},{224,1... | collective-permute-start | bytes 1228808 | tf_op jit(solution)/shard_map/ppermute | solution.py:230
  17.9 22.6 %collective-permute-start.2 = (bf16[2,320,320]{2,1,0:T(8,128)(2,1)}, bf16[2,320,320]{2,1,0:T(8,128)(2,1)}, u32[]{:S(2)}, u32[]{:S(2)}) collective-permute-start(bf16[2,320,320]{2,1,0:T(8,128)(2,1)} %get-tuple-element.41), channel_id=1, source_target_pairs={{0,96},{32,0},{64,32},{96,64},{128,224},{160,128},{192,160},{224,1... | collective-permute-start | bytes 1228808 | tf_op jit(solution)/shard_map/ppermute | solution.py:230
  20.4 14.6 %collective-permute-start.3 = (bf16[16,2560]{1,0:T(8,128)(2,1)S(1)}, bf16[16,2560]{1,0:T(8,128)(2,1)S(1)}, u32[]{:S(2)}, u32[]{:S(2)}) collective-permute-start(bf16[16,2560]{1,0:T(8,128)(2,1)S(1)} %dynamic-slice_bitcast_fusion.2), channel_id=1, source_target_pairs={{0,128},{32,160},{64,192},{96,224},{128,0},{160,32},{192,64},{224,... | collective-permute-start | bytes 245768 | tf_op jit(solution)/shard_map/ppermute | solution.py:278
  28.4 15.2 %all-to-all-start = ((bf16[32,16,256]{2,1,0:T(8,128)(2,1)}), bf16[32,16,256]{2,1,0:T(8,128)(2,1)S(1)}, u32[]{:S(2)}, u32[]{:S(2)}) async-start(bf16[32,16,256]{2,1,0:T(8,128)(2,1)} %bitcast.8), calls=%async_computation | async-start | bytes 524288 | tf_op jit(solution)/shard_map/all_to_all | solution.py:252
  44.4 23.5 %collective-permute-start.7 = (bf16[2,320,320]{2,1,0:T(8,128)(2,1)}, bf16[2,320,320]{2,1,0:T(8,128)(2,1)S(1)}, u32[]{:S(2)}, u32[]{:S(2)}) collective-permute-start(bf16[2,320,320]{2,1,0:T(8,128)(2,1)} %convert_element_type.51), channel_id=1, source_target_pairs={{0,128},{32,160},{64,192},{96,224},{128,0},{160,32},{192,64},{224,... | collective-permute-start | bytes 1228808 | tf_op jit(solution)/shard_map/ppermute | solution.py:240
  69.8 21.0 %all-to-all-start.1 = ((bf16[4,64,1024]{2,1,0:T(8,128)(2,1)}), bf16[4,64,1024]{2,1,0:T(8,128)(2,1)S(1)}, u32[]{:S(2)}, u32[]{:S(2)}) async-start(bf16[4,64,1024]{2,1,0:T(8,128)(2,1)} %broadcast_in_dim.30), calls=%async_computation.1 | async-start | bytes 1048576 | tf_op jit(solution)/shard_map/all_to_all | solution.py:267
  92.5 36.4 %all-to-all-start.2 = ((bf16[4,256,1024]{2,1,0:T(8,128)(2,1)}), bf16[4,256,1024]{2,1,0:T(8,128)(2,1)S(1)}, u32[]{:S(2)}, u32[]{:S(2)}) async-start(bf16[4,256,1024]{2,1,0:T(8,128)(2,1)} %broadcast_in_dim.31), calls=%async_computation.2 | async-start | bytes 4194304 | tf_op jit(solution)/shard_map/all_to_all | solution.py:267
  100.2 118.3 %all-gather.2.cloned.1.call-start = ((), (), s32[]{:S(2)}) async-start(), calls=%async_computation.4 | async-start | bytes 4325376 | tf_op jit(solution)/shard_map/all_gather | solution.py:308
  102.3 22.9 %collective-permute-start.11 = (bf16[2,320,320]{2,1,0:T(8,128)(2,1)}, bf16[2,320,320]{2,1,0:T(8,128)(2,1)}, u32[]{:S(2)}, u32[]{:S(2)}) collective-permute-start(bf16[2,320,320]{2,1,0:T(8,128)(2,1)} %convert_element_type.53.refs_0_), channel_id=1, source_target_pairs={{0,32},{32,64},{64,96},{96,0},{128,160},{160,192},{192,224},{224,1... | collective-permute-start | bytes 1228808 | tf_op jit(solution)/shard_map/ppermute | solution.py:230
  104.8 20.4 %collective-permute-start.12 = (bf16[2,320,320]{2,1,0:T(8,128)(2,1)}, bf16[2,320,320]{2,1,0:T(8,128)(2,1)}, u32[]{:S(2)}, u32[]{:S(2)}) collective-permute-start(bf16[2,320,320]{2,1,0:T(8,128)(2,1)} %convert_element_type.53.refs_0_), channel_id=1, source_target_pairs={{0,64},{32,96},{64,0},{96,32},{128,192},{160,224},{192,128},{224,1... | collective-permute-start | bytes 1228808 | tf_op jit(solution)/shard_map/ppermute | solution.py:230
  105.5 23.4 %collective-permute-start.13 = (bf16[2,320,320]{2,1,0:T(8,128)(2,1)}, bf16[2,320,320]{2,1,0:T(8,128)(2,1)}, u32[]{:S(2)}, u32[]{:S(2)}) collective-permute-start(bf16[2,320,320]{2,1,0:T(8,128)(2,1)} %convert_element_type.53.refs_0_), channel_id=1, source_target_pairs={{0,96},{32,0},{64,32},{96,64},{128,224},{160,128},{192,160},{224,1... | collective-permute-start | bytes 1228808 | tf_op jit(solution)/shard_map/ppermute | solution.py:230
  140.8 23.8 %collective-permute-start.15 = (bf16[2,320,256]{2,1,0:T(8,128)(2,1)}, bf16[2,320,256]{2,1,0:T(8,128)(2,1)S(1)}, u32[]{:S(2)}, u32[]{:S(2)}) collective-permute-start(bf16[2,320,256]{2,1,0:T(8,128)(2,1)} %get-tuple-element.54), channel_id=1, source_target_pairs={{0,32},{32,64},{64,96},{96,0},{128,160},{160,192},{192,224},{224,1... | collective-permute-start | bytes 983048 | tf_op jit(solution)/shard_map/ppermute | solution.py:230
  141.4 23.2 %collective-permute-start.16 = (bf16[2,320,256]{2,1,0:T(8,128)(2,1)}, bf16[2,320,256]{2,1,0:T(8,128)(2,1)S(1)}, u32[]{:S(2)}, u32[]{:S(2)}) collective-permute-start(bf16[2,320,256]{2,1,0:T(8,128)(2,1)} %get-tuple-element.55), channel_id=1, source_target_pairs={{0,64},{32,96},{64,0},{96,32},{128,192},{160,224},{192,128},{224,1... | collective-permute-start | bytes 983048 | tf_op jit(solution)/shard_map/ppermute | solution.py:230
  142.4 22.3 %collective-permute-start.17 = (bf16[2,320,256]{2,1,0:T(8,128)(2,1)S(1)}, bf16[2,320,256]{2,1,0:T(8,128)(2,1)S(1)}, u32[]{:S(2)}, u32[]{:S(2)}) collective-permute-start(bf16[2,320,256]{2,1,0:T(8,128)(2,1)S(1)} %get-tuple-element.56), channel_id=1, source_target_pairs={{0,96},{32,0},{64,32},{96,64},{128,224},{160,128},{192,160},{224,1... | collective-permute-start | bytes 983048 | tf_op jit(solution)/shard_map/ppermute | solution.py:230
  146.6 16.2 %collective-permute-start.18 = (bf16[320,256]{1,0:T(8,128)(2,1)}, bf16[320,256]{1,0:T(8,128)(2,1)S(1)}, u32[]{:S(2)}, u32[]{:S(2)}) collective-permute-start(bf16[320,256]{1,0:T(8,128)(2,1)} %shard_map.95), channel_id=1, source_target_pairs={{0,128},{32,160},{64,192},{96,224},{128,0},{160,32},{192,64},{224,... | collective-permute-start | bytes 491528 | tf_op jit(solution)/shard_map/ppermute | solution.py:313
  167.5 20.2 %collective-permute-start.19 = (bf16[2,320,256]{2,1,0:T(8,128)(2,1)S(1)}, bf16[2,320,256]{2,1,0:T(8,128)(2,1)S(1)}, u32[]{:S(2)}, u32[]{:S(2)}) collective-permute-start(bf16[2,320,256]{2,1,0:T(8,128)(2,1)S(1)} %convert_element_type.58), channel_id=1, source_target_pairs={{0,128},{32,160},{64,192},{96,224},{128,0},{160,32},{192,64},{224,... | collective-permute-start | bytes 983048 | tf_op jit(solution)/shard_map/ppermute | solution.py:240
  170.2 17.5 %collective-permute-start.20 = (bf16[2,320,256]{2,1,0:T(8,128)(2,1)S(1)}, bf16[2,320,256]{2,1,0:T(8,128)(2,1)S(1)}, u32[]{:S(2)}, u32[]{:S(2)}) collective-permute-start(bf16[2,320,256]{2,1,0:T(8,128)(2,1)S(1)} %maximum_select_fusion.refs_0_), channel_id=1, source_target_pairs={{0,32},{32,64},{64,96},{96,0},{128,160},{160,192},{192,224},{224,1... | collective-permute-start | bytes 983048 | tf_op jit(solution)/shard_map/ppermute | solution.py:230
  172.6 15.1 %collective-permute-start.21 = (bf16[2,320,256]{2,1,0:T(8,128)(2,1)S(1)}, bf16[2,320,256]{2,1,0:T(8,128)(2,1)}, u32[]{:S(2)}, u32[]{:S(2)}) collective-permute-start(bf16[2,320,256]{2,1,0:T(8,128)(2,1)S(1)} %maximum_select_fusion.refs_0_), channel_id=1, source_target_pairs={{0,64},{32,96},{64,0},{96,32},{128,192},{160,224},{192,128},{224,1... | collective-permute-start | bytes 983048 | tf_op jit(solution)/shard_map/ppermute | solution.py:230
  174.0 13.8 %collective-permute-start.22 = (bf16[2,320,256]{2,1,0:T(8,128)(2,1)S(1)}, bf16[2,320,256]{2,1,0:T(8,128)(2,1)}, u32[]{:S(2)}, u32[]{:S(2)}) collective-permute-start(bf16[2,320,256]{2,1,0:T(8,128)(2,1)S(1)} %maximum_select_fusion.refs_0_), channel_id=1, source_target_pairs={{0,96},{32,0},{64,32},{96,64},{128,224},{160,128},{192,160},{224,1... | collective-permute-start | bytes 983048 | tf_op jit(solution)/shard_map/ppermute | solution.py:230
  193.6 24.2 %all-to-all-start.3 = ((bf16[16,80,256]{2,1,0:T(8,128)(2,1)}), bf16[16,80,256]{2,1,0:T(8,128)(2,1)S(1)}, u32[]{:S(2)}, u32[]{:S(2)}) async-start(bf16[16,80,256]{2,1,0:T(8,128)(2,1)} %add_convert_fusion), calls=%async_computation.3 | async-start | bytes 1310720 | tf_op jit(solution)/shard_map/all_to_all | solution.py:324
  200.4 18.1 %collective-permute-start.23 = (bf16[2,320,256]{2,1,0:T(8,128)(2,1)S(1)}, bf16[2,320,256]{2,1,0:T(8,128)(2,1)}, u32[]{:S(2)}, u32[]{:S(2)}) collective-permute-start(bf16[2,320,256]{2,1,0:T(8,128)(2,1)S(1)} %convert_add_fusion.2.refs_0_), channel_id=1, source_target_pairs={{0,32},{32,64},{64,96},{96,0},{128,160},{160,192},{192,224},{224,1... | collective-permute-start | bytes 983048 | tf_op jit(solution)/shard_map/ppermute | solution.py:230
  201.5 17.0 %collective-permute-start.24 = (bf16[2,320,256]{2,1,0:T(8,128)(2,1)S(1)}, bf16[2,320,256]{2,1,0:T(8,128)(2,1)}, u32[]{:S(2)}, u32[]{:S(2)}) collective-permute-start(bf16[2,320,256]{2,1,0:T(8,128)(2,1)S(1)} %convert_add_fusion.2.refs_0_), channel_id=1, source_target_pairs={{0,64},{32,96},{64,0},{96,32},{128,192},{160,224},{192,128},{224,1... | collective-permute-start | bytes 983048 | tf_op jit(solution)/shard_map/ppermute | solution.py:230
  203.3 15.9 %collective-permute-start.25 = (bf16[2,320,256]{2,1,0:T(8,128)(2,1)S(1)}, bf16[2,320,256]{2,1,0:T(8,128)(2,1)}, u32[]{:S(2)}, u32[]{:S(2)}) collective-permute-start(bf16[2,320,256]{2,1,0:T(8,128)(2,1)S(1)} %convert_add_fusion.2.refs_0_), channel_id=1, source_target_pairs={{0,96},{32,0},{64,32},{96,64},{128,224},{160,128},{192,160},{224,1... | collective-permute-start | bytes 983048 | tf_op jit(solution)/shard_map/ppermute | solution.py:230
  (27 other events, 288.9 us)
Sparse Core Ops, SparseCore 0:
  129.1 78.3 all-gather.1

commit v9 on v8

--- a/solution.py
+++ b/solution.py
@@ -297,10 +297,10 @@
 
     strips = jnp.concatenate(gather_y(strip))
     rows = gather(rows, Z_GROUPS)
-    rows, grads, strips = together(rows, grads, strips)
-
     grad = pick(grads, z_hi).T
-    grads = gather_y(grads.astype(BF))
+    rows, grads, strips = together(rows, grads.astype(BF), strips)
+
+    grads = gather_y(grads)
     mixed = dot(strips, tokens, NT).astype(BF)
     half = gather(rows, X_GROUPS)
     half, grads, mixed = together(half, grads, mixed)

time: 235 us -> 231 us (0.983)
  other arithmetic: 12.4 us -> 9.46 us
    unnamed x42 -> x46, local copies, waits for them, and re-layouts: 7.48 us -> 6.2 us
  transfers between devices with their start and end apart: 32 -> 32, of which waited for: 18 -> 17; matrix products, arithmetic and copies ran while one was open for 9% -> 8% of each run, Pallas kernels for 8% -> 7%
where the time goes in v9:
time: 231 us; the launch traced here: 228 us
  waiting for transfers between devices  84.7 us (37%)
  starting transfers between devices  74.2 us (32%)
  Pallas kernels  29.6 us (13%)
  between operations  14.5 us (6%)
  local copies, waits for them, and re-layouts  10.5 us (5%)
  other arithmetic  9.46 us (4%)
  matrix products  4.84 us (2%)
    ppermute x21, waiting for transfers between devices, exchange_y(): got = {k: lax.ppermute(block_for(k), 'dp', shift_y(k)) for k in (2, 1, 3)}  31.2 us
    pallas_call x6, Pallas kernels, call(): pl.pallas_call(body, out_shape=outs, grid=specs.get('grid', ()), in_specs...  29.6 us
    ppermute x21, starting transfers between devices, exchange_y(): got = {k: lax.ppermute(block_for(k), 'dp', shift_y(k)) for k in (2, 1, 3)}  28.6 us
    ppermute x2, waiting for transfers between devices, sum_z(): return part + lax.ppermute(part.astype(BF), 'dp', SWAP_ZH).astype(F32)  20.1 us
    all_to_all x2, starting transfers between devices, gather(): lax.all_to_all(blocks, 'mp', 0, 0, axis_index_groups=groups)  15 us
    ppermute x1, waiting for transfers between devices, shards(): other = lax.ppermute(back, 'dp', SWAP_ZH)  14.7 us
    ppermute x2, starting transfers between devices, sum_z(): return part + lax.ppermute(part.astype(BF), 'dp', SWAP_ZH).astype(F32)  8.32 us
    all_to_all x1, waiting for transfers between devices, shards(): lax.all_to_all(keep.astype(BF), 'mp', 0, 0, axis_index_groups=PLANE_GROUPS)  7.85 us
  transfers between devices with their start and end apart: 32, of which 17 were waited for; matrix products, arithmetic and copies ran while one was open for 8% of the time, Pallas kernels for 7%

profile of v9, /device:TPU:30, one launch (start us, length us, event | category | flops | bytes accessed | tf_op | source)
XLA Modules:
  0.0 227.7 jit_solution(2484484817449489111)
XLA Ops:
  7.8 7.2 %shard_map.93 = (f32[2,320,320]{2,1,0:T(8,128)}, bf16[2,320,320]{2,1,0:T(8,128)(2,1)}, bf16[2,320,320]{2,1,0:T(8,128)(2,1)}, bf16[2,320,320]{2,1,0:T(8,128)(2,1)}) custom-call(s32[4]{0:T(128)} %pad_add_fusion.place, bf16[1024,2560]{1,0:T(8,128)(2,1)} %tokens.1, bf16[320,1024]{1,0:T(8,128)(2,1)} %bitcast.100), custom_call_target="tpu_custom_call" | custom-call | flops 1677721600 | bytes 7946240 | tf_op jit(solution)/shard_map/pallas_call | solution.py:43
  20.4 7.2 %collective-permute-start.3 = (bf16[16,2560]{1,0:T(8,128)(2,1)S(1)}, bf16[16,2560]{1,0:T(8,128)(2,1)S(1)}, u32[]{:S(2)}, u32[]{:S(2)}) collective-permute-start(bf16[16,2560]{1,0:T(8,128)(2,1)S(1)} %dynamic-slice_bitcast_fusion.2), channel_id=1, source_target_pairs={{0,128},{32,160},{64,192},{96,224},{128,0},{160,32},{192,64},{224,... | collective-permute-start | bytes 245768 | tf_op jit(solution)/shard_map/ppermute | solution.py:278
  28.3 6.3 %all-to-all-start = ((bf16[32,16,256]{2,1,0:T(8,128)(2,1)}), bf16[32,16,256]{2,1,0:T(8,128)(2,1)S(1)}, u32[]{:S(2)}, u32[]{:S(2)}) async-start(bf16[32,16,256]{2,1,0:T(8,128)(2,1)} %bitcast.8), calls=%async_computation | async-start | bytes 524288 | tf_op jit(solution)/shard_map/all_to_all | solution.py:252
  35.9 4.5 %collective-permute-done.2 = bf16[2,320,320]{2,1,0:T(8,128)(2,1)} collective-permute-done((bf16[2,320,320]{2,1,0:T(8,128)(2,1)}, bf16[2,320,320]{2,1,0:T(8,128)(2,1)}, u32[]{:S(2)}, u32[]{:S(2)}) %collective-permute-start.2) | collective-permute-done | bytes 409632 | tf_op jit(solution)/shard_map/ppermute | solution.py:230
  43.6 5.7 %collective-permute-start.7 = (bf16[2,320,320]{2,1,0:T(8,128)(2,1)S(1)}, bf16[2,320,320]{2,1,0:T(8,128)(2,1)}, u32[]{:S(2)}, u32[]{:S(2)}) collective-permute-start(bf16[2,320,320]{2,1,0:T(8,128)(2,1)S(1)} %convert_element_type.51), channel_id=1, source_target_pairs={{0,128},{32,160},{64,192},{96,224},{128,0},{160,32},{192,64},{224,... | collective-permute-start | bytes 1228808 | tf_op jit(solution)/shard_map/ppermute | solution.py:240
  55.7 3.1 %collective-permute-done.6 = bf16[4,16,256]{2,1,0:T(8,128)(2,1)S(1)} collective-permute-done((bf16[4,16,256]{2,1,0:T(8,128)(2,1)S(1)}, bf16[4,16,256]{2,1,0:T(8,128)(2,1)S(1)}, u32[]{:S(2)}, u32[]{:S(2)}) %collective-permute-start.6) | collective-permute-done | bytes 32800 | tf_op jit(solution)/shard_map/ppermute | solution.py:230
  59.0 8.1 %collective-permute-done.7 = bf16[2,320,320]{2,1,0:T(8,128)(2,1)} collective-permute-done((bf16[2,320,320]{2,1,0:T(8,128)(2,1)S(1)}, bf16[2,320,320]{2,1,0:T(8,128)(2,1)}, u32[]{:S(2)}, u32[]{:S(2)}) %collective-permute-start.7) | collective-permute-done | bytes 409632 | tf_op jit(solution)/shard_map/ppermute | solution.py:240
  69.2 7.2 %all-to-all-start.1 = ((bf16[4,64,1024]{2,1,0:T(8,128)(2,1)}), bf16[4,64,1024]{2,1,0:T(8,128)(2,1)S(1)}, u32[]{:S(2)}, u32[]{:S(2)}) async-start(bf16[4,64,1024]{2,1,0:T(8,128)(2,1)} %broadcast_in_dim.30), calls=%async_computation.1 | async-start | bytes 1048576 | tf_op jit(solution)/shard_map/all_to_all | solution.py:267
  84.2 2.9 %collective-permute-done.9 = bf16[16,2560]{1,0:T(8,128)(2,1)S(1)} collective-permute-done((bf16[16,2560]{1,0:T(8,128)(2,1)S(1)}, bf16[16,2560]{1,0:T(8,128)(2,1)S(1)}, u32[]{:S(2)}, u32[]{:S(2)}) %collective-permute-start.9) | collective-permute-done | bytes 81952 | tf_op jit(solution)/shard_map/ppermute | solution.py:230
  87.1 3.1 %all-to-all-done.1 = bf16[4,64,1024]{2,1,0:T(8,128)(2,1)S(1)} async-done(((bf16[4,64,1024]{2,1,0:T(8,128)(2,1)}), bf16[4,64,1024]{2,1,0:T(8,128)(2,1)S(1)}, u32[]{:S(2)}, u32[]{:S(2)}) %all-to-all-start.1) | async-done | bytes 524320 | tf_op jit(solution)/shard_map/all_to_all | solution.py:267
  91.8 7.8 %all-to-all-start.2 = ((bf16[4,256,1024]{2,1,0:T(8,128)(2,1)}), bf16[4,256,1024]{2,1,0:T(8,128)(2,1)S(1)}, u32[]{:S(2)}, u32[]{:S(2)}) async-start(bf16[4,256,1024]{2,1,0:T(8,128)(2,1)} %broadcast_in_dim.31), calls=%async_computation.2 | async-start | bytes 4194304 | tf_op jit(solution)/shard_map/all_to_all | solution.py:267
  104.2 4.8 %convolution_convert_fusion = bf16[64,1024]{1,0:T(8,128)(2,1)} fusion(bf16[64,2560]{1,0:T(8,128)(2,1)S(1)} %pad_maximum_fusion, bf16[1024,2560]{1,0:T(8,128)(2,1)} %tokens.1), kind=kOutput, calls=%fused_computation.3 | convolution fusion | flops 335609856 | bytes 5701632 | tf_op jit(solution)/shard_map/dot_general | solution.py:26
  109.0 13.5 %collective-permute-done.11.refs_1_ = bf16[2,320,320]{2,1,0:T(8,128)(2,1)} collective-permute-done((bf16[2,320,320]{2,1,0:T(8,128)(2,1)}, bf16[2,320,320]{2,1,0:T(8,128)(2,1)}, u32[]{:S(2)}, u32[]{:S(2)}) %collective-permute-start.11) | collective-permute-done | bytes 409632 | tf_op jit(solution)/shard_map/ppermute | solution.py:230
  122.5 3.7 %collective-permute-done.13.refs_3_ = bf16[2,320,320]{2,1,0:T(8,128)(2,1)} collective-permute-done((bf16[2,320,320]{2,1,0:T(8,128)(2,1)}, bf16[2,320,320]{2,1,0:T(8,128)(2,1)}, u32[]{:S(2)}, u32[]{:S(2)}) %collective-permute-start.13) | collective-permute-done | bytes 409632 | tf_op jit(solution)/shard_map/ppermute | solution.py:230
  126.3 4.1 %collective-permute-done.14.other = bf16[1024,1024]{1,0:T(8,128)(2,1)S(1)} collective-permute-done((bf16[1024,1024]{1,0:T(8,128)(2,1)S(1)}, bf16[1024,1024]{1,0:T(8,128)(2,1)S(1)}, u32[]{:S(2)}, u32[]{:S(2)}) %collective-permute-start.14) | collective-permute-done | bytes 2097184 | tf_op jit(solution)/shard_map/ppermute | solution.py:271
  131.6 5.7 %shard_map.94 = (f32[2,320,256]{2,1,0:T(8,128)S(1)}, bf16[2,320,256]{2,1,0:T(8,128)(2,1)}, bf16[2,320,256]{2,1,0:T(8,128)(2,1)}, bf16[2,320,256]{2,1,0:T(8,128)(2,1)S(1)}) custom-call(s32[4]{0:T(128)S(1)} %copy-done.6, bf16[320,1024]{1,0:T(8,128)(2,1)S(1)} %copy-done.8, bf16[1024,1024]{1,0:T(8,128)(2,1)S(1)} %bitcast.88, ...), custom_call_target="tpu_custom_call" | custom-call | flops 1342177280 | bytes 6488064 | tf_op jit(solution)/shard_map/pallas_call | solution.py:43
  140.7 3.4 %shard_map.95 = bf16[320,256]{1,0:T(8,128)(2,1)} custom-call(s32[4]{0:T(128)} %pad_add_fusion.place, bf16[2560,256]{1,0:T(8,128)(2,1)} %grown.1, bf16[2,320,320]{2,1,0:T(8,128)(2,1)} %convert_element_type.53.refs_0_, bf16[2,320,320]{2,1,0:T(8,128)(2,1)} %collective-permute-done.11.refs_1_, bf16[2,320,320]{2,1,0:T(8,128)(2,1)} %collective-permute-done.12.refs_2_, ...), custom_call_target="tpu_custom_call" | custom-call | flops 419430400 | bytes 3112960 | tf_op jit(solution)/shard_map/pallas_call | solution.py:43
  145.4 14.7 %collective-permute-done.18 = bf16[320,256]{1,0:T(8,128)(2,1)S(1)} collective-permute-done((bf16[320,256]{1,0:T(8,128)(2,1)}, bf16[320,256]{1,0:T(8,128)(2,1)S(1)}, u32[]{:S(2)}, u32[]{:S(2)}) %collective-permute-start.18) | collective-permute-done | bytes 163872 | tf_op jit(solution)/shard_map/ppermute | solution.py:313
  163.5 2.7 %collective-permute-start.19 = (bf16[2,320,256]{2,1,0:T(8,128)(2,1)S(1)}, bf16[2,320,256]{2,1,0:T(8,128)(2,1)S(1)}, u32[]{:S(2)}, u32[]{:S(2)}) collective-permute-start(bf16[2,320,256]{2,1,0:T(8,128)(2,1)S(1)} %convert_element_type.58), channel_id=1, source_target_pairs={{0,128},{32,160},{64,192},{96,224},{128,0},{160,32},{192,64},{224,... | collective-permute-start | bytes 983048 | tf_op jit(solution)/shard_map/ppermute | solution.py:240
  171.3 11.9 %collective-permute-done.19 = bf16[2,320,256]{2,1,0:T(8,128)(2,1)S(1)} collective-permute-done((bf16[2,320,256]{2,1,0:T(8,128)(2,1)S(1)}, bf16[2,320,256]{2,1,0:T(8,128)(2,1)S(1)}, u32[]{:S(2)}, u32[]{:S(2)}) %collective-permute-start.19) | collective-permute-done | bytes 327712 | tf_op jit(solution)/shard_map/ppermute | solution.py:240
  189.6 7.3 %all-to-all-start.3 = ((bf16[16,80,256]{2,1,0:T(8,128)(2,1)}), bf16[16,80,256]{2,1,0:T(8,128)(2,1)S(1)}, u32[]{:S(2)}, u32[]{:S(2)}) async-start(bf16[16,80,256]{2,1,0:T(8,128)(2,1)} %add_convert_fusion), calls=%async_computation.3 | async-start | bytes 1310720 | tf_op jit(solution)/shard_map/all_to_all | solution.py:324
  200.6 5.7 %shard_map.96 = f32[320,1024]{1,0:T(8,128)} custom-call(s32[4]{0:T(128)} %pad_add_fusion.place, bf16[1024,1024]{1,0:T(8,128)(2,1)} %bitcast.89, bf16[1024,1024]{1,0:T(8,128)(2,1)} %copy-done.3, bf16[2,320,256]{2,1,0:T(8,128)(2,1)} %copy-done.13, bf16[2,320,256]{2,1,0:T(8,128)(2,1)} %copy-done.19, bf16[2,320,256]{2,1,0:T(8,128)(2,1)} %collective-permute-done.21.refs_2_, ...), custom_call_target="tpu_custom_call" | custom-call | flops 1342177280 | bytes 6815744 | tf_op jit(solution)/shard_map/pallas_call | solution.py:43
  206.3 7.8 %all-to-all-done.3 = bf16[16,80,256]{2,1,0:T(8,128)(2,1)S(1)} async-done(((bf16[16,80,256]{2,1,0:T(8,128)(2,1)}), bf16[16,80,256]{2,1,0:T(8,128)(2,1)S(1)}, u32[]{:S(2)}, u32[]{:S(2)}) %all-to-all-start.3) | async-done | bytes 655392 | tf_op jit(solution)/shard_map/all_to_all | solution.py:324
  215.6 5.3 %shard_map.97 = bf16[320,1024]{1,0:T(8,128)(2,1)} custom-call(s32[4]{0:T(128)} %pad_add_fusion.place, bf16[16,2,4,16,1024]{4,3,2,1,0:T(8,128)(2,1)} %bitcast.90, bf16[2,320,256]{2,1,0:T(8,128)(2,1)} %copy-done.12, bf16[2,320,256]{2,1,0:T(8,128)(2,1)} %collective-permute-done.23.refs_1_, bf16[2,320,256]{2,1,0:T(8,128)(2,1)} %collective-permute-done.24.refs_2_, ...), custom_call_target="tpu_custom_call" | custom-call | flops 1342177280 | bytes 6160384 | tf_op jit(solution)/shard_map/pallas_call | solution.py:43
  (123 shorter events, 59.4 us)
Async XLA Ops:
  15.1 20.8 %collective-permute-start = (bf16[2,320,320]{2,1,0:T(8,128)(2,1)}, bf16[2,320,320]{2,1,0:T(8,128)(2,1)}, u32[]{:S(2)}, u32[]{:S(2)}) collective-permute-start(bf16[2,320,320]{2,1,0:T(8,128)(2,1)} %get-tuple-element.39), channel_id=1, source_target_pairs={{0,32},{32,64},{64,96},{96,0},{128,160},{160,192},{192,224},{224,1... | collective-permute-start | bytes 1228808 | tf_op jit(solution)/shard_map/ppermute | solution.py:230
  15.2 20.7 %collective-permute-start.1 = (bf16[2,320,320]{2,1,0:T(8,128)(2,1)}, bf16[2,320,320]{2,1,0:T(8,128)(2,1)}, u32[]{:S(2)}, u32[]{:S(2)}) collective-permute-start(bf16[2,320,320]{2,1,0:T(8,128)(2,1)} %get-tuple-element.40), channel_id=1, source_target_pairs={{0,64},{32,96},{64,0},{96,32},{128,192},{160,224},{192,128},{224,1... | collective-permute-start | bytes 1228808 | tf_op jit(solution)/shard_map/ppermute | solution.py:230
  17.8 22.6 %collective-permute-start.2 = (bf16[2,320,320]{2,1,0:T(8,128)(2,1)}, bf16[2,320,320]{2,1,0:T(8,128)(2,1)}, u32[]{:S(2)}, u32[]{:S(2)}) collective-permute-start(bf16[2,320,320]{2,1,0:T(8,128)(2,1)} %get-tuple-element.41), channel_id=1, source_target_pairs={{0,96},{32,0},{64,32},{96,64},{128,224},{160,128},{192,160},{224,1... | collective-permute-start | bytes 1228808 | tf_op jit(solution)/shard_map/ppermute | solution.py:230
  20.4 14.6 %collective-permute-start.3 = (bf16[16,2560]{1,0:T(8,128)(2,1)S(1)}, bf16[16,2560]{1,0:T(8,128)(2,1)S(1)}, u32[]{:S(2)}, u32[]{:S(2)}) collective-permute-start(bf16[16,2560]{1,0:T(8,128)(2,1)S(1)} %dynamic-slice_bitcast_fusion.2), channel_id=1, source_target_pairs={{0,128},{32,160},{64,192},{96,224},{128,0},{160,32},{192,64},{224,... | collective-permute-start | bytes 245768 | tf_op jit(solution)/shard_map/ppermute | solution.py:278
  28.3 15.2 %all-to-all-start = ((bf16[32,16,256]{2,1,0:T(8,128)(2,1)}), bf16[32,16,256]{2,1,0:T(8,128)(2,1)S(1)}, u32[]{:S(2)}, u32[]{:S(2)}) async-start(bf16[32,16,256]{2,1,0:T(8,128)(2,1)} %bitcast.8), calls=%async_computation | async-start | bytes 524288 | tf_op jit(solution)/shard_map/all_to_all | solution.py:252
  43.6 23.5 %collective-permute-start.7 = (bf16[2,320,320]{2,1,0:T(8,128)(2,1)S(1)}, bf16[2,320,320]{2,1,0:T(8,128)(2,1)}, u32[]{:S(2)}, u32[]{:S(2)}) collective-permute-start(bf16[2,320,320]{2,1,0:T(8,128)(2,1)S(1)} %convert_element_type.51), channel_id=1, source_target_pairs={{0,128},{32,160},{64,192},{96,224},{128,0},{160,32},{192,64},{224,... | collective-permute-start | bytes 1228808 | tf_op jit(solution)/shard_map/ppermute | solution.py:240
  69.2 21.0 %all-to-all-start.1 = ((bf16[4,64,1024]{2,1,0:T(8,128)(2,1)}), bf16[4,64,1024]{2,1,0:T(8,128)(2,1)S(1)}, u32[]{:S(2)}, u32[]{:S(2)}) async-start(bf16[4,64,1024]{2,1,0:T(8,128)(2,1)} %broadcast_in_dim.30), calls=%async_computation.1 | async-start | bytes 1048576 | tf_op jit(solution)/shard_map/all_to_all | solution.py:267
  91.8 34.4 %all-to-all-start.2 = ((bf16[4,256,1024]{2,1,0:T(8,128)(2,1)}), bf16[4,256,1024]{2,1,0:T(8,128)(2,1)S(1)}, u32[]{:S(2)}, u32[]{:S(2)}) async-start(bf16[4,256,1024]{2,1,0:T(8,128)(2,1)} %broadcast_in_dim.31), calls=%async_computation.2 | async-start | bytes 4194304 | tf_op jit(solution)/shard_map/all_to_all | solution.py:267
  99.6 115.3 %all-gather.2.cloned.1.call-start = ((), (), s32[]{:S(2)}) async-start(), calls=%async_computation.4 | async-start | bytes 4325376 | tf_op jit(solution)/shard_map/all_gather | solution.py:308
  99.6 22.9 %collective-permute-start.11 = (bf16[2,320,320]{2,1,0:T(8,128)(2,1)}, bf16[2,320,320]{2,1,0:T(8,128)(2,1)}, u32[]{:S(2)}, u32[]{:S(2)}) collective-permute-start(bf16[2,320,320]{2,1,0:T(8,128)(2,1)} %convert_element_type.53.refs_0_), channel_id=1, source_target_pairs={{0,32},{32,64},{64,96},{96,0},{128,160},{160,192},{192,224},{224,1... | collective-permute-start | bytes 1228808 | tf_op jit(solution)/shard_map/ppermute | solution.py:230
  102.1 20.4 %collective-permute-start.12 = (bf16[2,320,320]{2,1,0:T(8,128)(2,1)}, bf16[2,320,320]{2,1,0:T(8,128)(2,1)}, u32[]{:S(2)}, u32[]{:S(2)}) collective-permute-start(bf16[2,320,320]{2,1,0:T(8,128)(2,1)} %convert_element_type.53.refs_0_), channel_id=1, source_target_pairs={{0,64},{32,96},{64,0},{96,32},{128,192},{160,224},{192,128},{224,1... | collective-permute-start | bytes 1228808 | tf_op jit(solution)/shard_map/ppermute | solution.py:230
  103.0 23.2 %collective-permute-start.13 = (bf16[2,320,320]{2,1,0:T(8,128)(2,1)}, bf16[2,320,320]{2,1,0:T(8,128)(2,1)}, u32[]{:S(2)}, u32[]{:S(2)}) collective-permute-start(bf16[2,320,320]{2,1,0:T(8,128)(2,1)} %convert_element_type.53.refs_0_), channel_id=1, source_target_pairs={{0,96},{32,0},{64,32},{96,64},{128,224},{160,128},{192,160},{224,1... | collective-permute-start | bytes 1228808 | tf_op jit(solution)/shard_map/ppermute | solution.py:230
  138.1 23.1 %collective-permute-start.15 = (bf16[2,320,256]{2,1,0:T(8,128)(2,1)}, bf16[2,320,256]{2,1,0:T(8,128)(2,1)S(1)}, u32[]{:S(2)}, u32[]{:S(2)}) collective-permute-start(bf16[2,320,256]{2,1,0:T(8,128)(2,1)} %get-tuple-element.54), channel_id=1, source_target_pairs={{0,32},{32,64},{64,96},{96,0},{128,160},{160,192},{192,224},{224,1... | collective-permute-start | bytes 983048 | tf_op jit(solution)/shard_map/ppermute | solution.py:230
  138.7 22.5 %collective-permute-start.16 = (bf16[2,320,256]{2,1,0:T(8,128)(2,1)}, bf16[2,320,256]{2,1,0:T(8,128)(2,1)S(1)}, u32[]{:S(2)}, u32[]{:S(2)}) collective-permute-start(bf16[2,320,256]{2,1,0:T(8,128)(2,1)} %get-tuple-element.55), channel_id=1, source_target_pairs={{0,64},{32,96},{64,0},{96,32},{128,192},{160,224},{192,128},{224,1... | collective-permute-start | bytes 983048 | tf_op jit(solution)/shard_map/ppermute | solution.py:230
  139.9 21.3 %collective-permute-start.17 = (bf16[2,320,256]{2,1,0:T(8,128)(2,1)S(1)}, bf16[2,320,256]{2,1,0:T(8,128)(2,1)}, u32[]{:S(2)}, u32[]{:S(2)}) collective-permute-start(bf16[2,320,256]{2,1,0:T(8,128)(2,1)S(1)} %get-tuple-element.56), channel_id=1, source_target_pairs={{0,96},{32,0},{64,32},{96,64},{128,224},{160,128},{192,160},{224,1... | collective-permute-start | bytes 983048 | tf_op jit(solution)/shard_map/ppermute | solution.py:230
  144.2 16.0 %collective-permute-start.18 = (bf16[320,256]{1,0:T(8,128)(2,1)}, bf16[320,256]{1,0:T(8,128)(2,1)S(1)}, u32[]{:S(2)}, u32[]{:S(2)}) collective-permute-start(bf16[320,256]{1,0:T(8,128)(2,1)} %shard_map.95), channel_id=1, source_target_pairs={{0,128},{32,160},{64,192},{96,224},{128,0},{160,32},{192,64},{224,... | collective-permute-start | bytes 491528 | tf_op jit(solution)/shard_map/ppermute | solution.py:313
  163.5 19.7 %collective-permute-start.19 = (bf16[2,320,256]{2,1,0:T(8,128)(2,1)S(1)}, bf16[2,320,256]{2,1,0:T(8,128)(2,1)S(1)}, u32[]{:S(2)}, u32[]{:S(2)}) collective-permute-start(bf16[2,320,256]{2,1,0:T(8,128)(2,1)S(1)} %convert_element_type.58), channel_id=1, source_target_pairs={{0,128},{32,160},{64,192},{96,224},{128,0},{160,32},{192,64},{224,... | collective-permute-start | bytes 983048 | tf_op jit(solution)/shard_map/ppermute | solution.py:240
  166.2 17.1 %collective-permute-start.20 = (bf16[2,320,256]{2,1,0:T(8,128)(2,1)S(1)}, bf16[2,320,256]{2,1,0:T(8,128)(2,1)S(1)}, u32[]{:S(2)}, u32[]{:S(2)}) collective-permute-start(bf16[2,320,256]{2,1,0:T(8,128)(2,1)S(1)} %maximum_select_fusion.refs_0_), channel_id=1, source_target_pairs={{0,32},{32,64},{64,96},{96,0},{128,160},{160,192},{192,224},{224,1... | collective-permute-start | bytes 983048 | tf_op jit(solution)/shard_map/ppermute | solution.py:230
  168.4 14.9 %collective-permute-start.21 = (bf16[2,320,256]{2,1,0:T(8,128)(2,1)S(1)}, bf16[2,320,256]{2,1,0:T(8,128)(2,1)}, u32[]{:S(2)}, u32[]{:S(2)}) collective-permute-start(bf16[2,320,256]{2,1,0:T(8,128)(2,1)S(1)} %maximum_select_fusion.refs_0_), channel_id=1, source_target_pairs={{0,64},{32,96},{64,0},{96,32},{128,192},{160,224},{192,128},{224,1... | collective-permute-start | bytes 983048 | tf_op jit(solution)/shard_map/ppermute | solution.py:230
  169.9 14.2 %collective-permute-start.22 = (bf16[2,320,256]{2,1,0:T(8,128)(2,1)S(1)}, bf16[2,320,256]{2,1,0:T(8,128)(2,1)}, u32[]{:S(2)}, u32[]{:S(2)}) collective-permute-start(bf16[2,320,256]{2,1,0:T(8,128)(2,1)S(1)} %maximum_select_fusion.refs_0_), channel_id=1, source_target_pairs={{0,96},{32,0},{64,32},{96,64},{128,224},{160,128},{192,160},{224,1... | collective-permute-start | bytes 983048 | tf_op jit(solution)/shard_map/ppermute | solution.py:230
  189.6 24.6 %all-to-all-start.3 = ((bf16[16,80,256]{2,1,0:T(8,128)(2,1)}), bf16[16,80,256]{2,1,0:T(8,128)(2,1)S(1)}, u32[]{:S(2)}, u32[]{:S(2)}) async-start(bf16[16,80,256]{2,1,0:T(8,128)(2,1)} %add_convert_fusion), calls=%async_computation.3 | async-start | bytes 1310720 | tf_op jit(solution)/shard_map/all_to_all | solution.py:324
  196.8 18.1 %collective-permute-start.23 = (bf16[2,320,256]{2,1,0:T(8,128)(2,1)S(1)}, bf16[2,320,256]{2,1,0:T(8,128)(2,1)}, u32[]{:S(2)}, u32[]{:S(2)}) collective-permute-start(bf16[2,320,256]{2,1,0:T(8,128)(2,1)S(1)} %convert_add_fusion.2.refs_0_), channel_id=1, source_target_pairs={{0,32},{32,64},{64,96},{96,0},{128,160},{160,192},{192,224},{224,1... | collective-permute-start | bytes 983048 | tf_op jit(solution)/shard_map/ppermute | solution.py:230
  197.8 17.1 %collective-permute-start.24 = (bf16[2,320,256]{2,1,0:T(8,128)(2,1)S(1)}, bf16[2,320,256]{2,1,0:T(8,128)(2,1)}, u32[]{:S(2)}, u32[]{:S(2)}) collective-permute-start(bf16[2,320,256]{2,1,0:T(8,128)(2,1)S(1)} %convert_add_fusion.2.refs_0_), channel_id=1, source_target_pairs={{0,64},{32,96},{64,0},{96,32},{128,192},{160,224},{192,128},{224,1... | collective-permute-start | bytes 983048 | tf_op jit(solution)/shard_map/ppermute | solution.py:230
  199.2 16.4 %collective-permute-start.25 = (bf16[2,320,256]{2,1,0:T(8,128)(2,1)S(1)}, bf16[2,320,256]{2,1,0:T(8,128)(2,1)}, u32[]{:S(2)}, u32[]{:S(2)}) collective-permute-start(bf16[2,320,256]{2,1,0:T(8,128)(2,1)S(1)} %convert_add_fusion.2.refs_0_), channel_id=1, source_target_pairs={{0,96},{32,0},{64,32},{96,64},{128,224},{160,128},{192,160},{224,1... | collective-permute-start | bytes 983048 | tf_op jit(solution)/shard_map/ppermute | solution.py:230
  (29 other events, 327.7 us)
Sparse Core Ops, SparseCore 0:
  126.4 78.9 all-gather.1
